TPU v7x, 128 devices: a whole 4x4x4 slice. The times are simulated.
128 devices in a mesh: chan: 32 (over x, z, y_lo), tm: 4 (over y_hi, core).
Axes of the slice: x: 4, y: 4 (y_hi: 2, y_lo: 2; y = y_hi * 2 + y_lo), z: 4, core: 2. Of those that a mesh axis runs over, the one named last changes fastest.
Arguments:
- samples: bfloat16 [4096, 98304], P('chan', 'tm'), may hold values from -6 to 6
- plan: int32 [3], replicated, may hold values from 0 to 31
- owner_table: int32 [32], replicated, may hold values from 0 to 31, each once
Outputs:
- correlations: float32 [128, 3, 101, 4096], P('tm', None, None, 'chan')
Inputs may be any that keep to these rules, and one draw needn't show every extreme that they name: `plan`: each entry names a cable block. `owner_table`: each stored block holds exactly one cable block.
All inputs are finite; a program needn't handle non-finite values.
Results may differ from a plain program's by a relative error of at most 0.0036.
Values may be sent and summed in bfloat16 or wider, within the bound.
No kernel may reach another device: no remote copies, remote signals or barrier semaphores. Data moves between devices by JAX's collectives and lax.ppermute only.
A program may use at most 128 MiB of HBM per device.

v0:
```python
import math

import jax
import jax.numpy as jnp
from jax import lax
from jax.sharding import PartitionSpec as P

WINLEN = 1024
BINS = 128
BIN0 = 16
SMOOTH = 4
LAGS = 101
STEPS = 3


magnitude_eps = 1e-06
water_level = 0.25


def from_behind(value, axis, steps):
    count = lax.axis_size(axis)
    initial, last = (max(0, -steps), min(count, count - steps))
    return lax.ppermute(value, axis, [(source, source + steps) for source in range(initial, last)])


def broadcast(x, axis, root):
    mine = lax.axis_index(axis) == root
    return lax.psum(jnp.where(mine, x, jnp.zeros_like(x)), axis)


def dft_table():
    positions = jnp.arange(WINLEN, dtype=jnp.int32)
    bin_index = BIN0 + jnp.arange(BINS, dtype=jnp.int32)
    phase_steps = positions[:, None] * bin_index[None, :] % WINLEN
    angles = 2.0 * math.pi / WINLEN * phase_steps.astype(jnp.float32)
    taper = 0.5 - 0.5 * jnp.cos(2.0 * math.pi / WINLEN * positions.astype(jnp.float32))
    return jnp.concatenate(
        [taper[:, None] * jnp.cos(angles), -taper[:, None] * jnp.sin(angles)], axis=1
    ).astype(jnp.bfloat16)


def band_table():
    bin_index = jnp.arange(BINS, dtype=jnp.int32)
    inside = (jnp.abs(bin_index[:, None] - bin_index[None, :]) <= SMOOTH).astype(jnp.float32)
    totals = jnp.sum(inside, axis=0)
    return inside / totals[None, :]


def lag_table(windows):
    lag_steps = jnp.arange(LAGS, dtype=jnp.int32) - LAGS // 2
    bin_index = BIN0 + jnp.arange(BINS, dtype=jnp.int32)
    phase_steps = jnp.mod(lag_steps[:, None] * bin_index[None, :], WINLEN)
    angles = 2.0 * math.pi / WINLEN * phase_steps.astype(jnp.float32)
    factor = 1.0 / math.sqrt(BINS * windows)
    return jnp.stack([jnp.cos(angles) * factor, -jnp.sin(angles) * factor], axis=1)


def whiten(spectra, band):
    real_part = spectra[..., :BINS]
    imag_part = spectra[..., BINS:]
    magnitude = jnp.sqrt(real_part * real_part + imag_part * imag_part + magnitude_eps)
    running = jnp.dot(magnitude.reshape(-1, BINS), band, precision=lax.Precision.HIGHEST).reshape(
        magnitude.shape
    )
    divisor = running + water_level * jnp.mean(magnitude, axis=-1, keepdims=True)
    return (spectra / jnp.concatenate([divisor, divisor], axis=-1)).astype(jnp.bfloat16)


def cross_spectra(own_rows, reference_rows):
    own_parts = own_rows.reshape(own_rows.shape[0], own_rows.shape[1], 2, BINS)
    ref_parts = reference_rows.reshape(reference_rows.shape[0], reference_rows.shape[1], 2, BINS)
    rotated = jnp.stack([-ref_parts[:, :, 1], ref_parts[:, :, 0]], axis=2)
    real_part = jnp.einsum(
        "awkf,bwkf->fba", own_parts, ref_parts, preferred_element_type=jnp.float32
    )
    imag_part = jnp.einsum("awkf,bwkf->fba", own_parts, rotated, preferred_element_type=jnp.float32)
    return jnp.stack([real_part, imag_part])


def lag_rows(lag_weights, spectra_pair):
    return jnp.einsum("tkf,kfba->bta", lag_weights, spectra_pair, precision=lax.Precision.HIGHEST)


def shards(samples, plan, owner_table):
    chan_dev = samples.shape[0]
    hop_len = WINLEN // 2
    win_dev = samples.shape[1] // hop_len
    windows = win_dev * lax.axis_size("tm")
    transform = dft_table()
    band = band_table()
    lag_weights = lag_table(windows)
    hop_rows = samples.reshape(chan_dev, win_dev, hop_len)
    edge_rows = from_behind(samples[:, :hop_len], "tm", -1)
    extended = jnp.concatenate([hop_rows, edge_rows[:, None, :]], axis=1)
    frames = jnp.concatenate([extended[:, :-1], extended[:, 1:]], axis=2)
    spectra = jnp.dot(frames.reshape(-1, WINLEN), transform, preferred_element_type=jnp.float32)
    spectra = spectra.reshape(chan_dev, win_dev, 2 * BINS)
    whitened = whiten(spectra, band)
    results = []
    for step_index in range(STEPS):
        root_index = owner_table[plan[step_index]]
        reference_rows = broadcast(whitened, "chan", root_index)
        spectra_pair = cross_spectra(whitened, reference_rows)
        results.append(
            lax.psum_scatter(
                lag_rows(lag_weights, spectra_pair), "tm", scatter_dimension=0, tiled=True
            )
        )
    return jnp.stack(results, axis=1)


def solution(mesh):
    placed = (P("chan", "tm"), P(), P())
    return jax.shard_map(
        shards, mesh=mesh, in_specs=placed, out_specs=P("tm", None, None, "chan"), check_vma=False
    )
```

profile of v0, /device:TPU:1, one launch (start us, length us, event | category | flops | bytes accessed | tf_op | source)
XLA Modules:
  0.0 802.6 jit_solution(3600450527404082001)
XLA Ops:
  16.0 8.6 %copy.18 = bf16[128,24576]{0,1:T(8,128)(2,1)} copy(bf16[128,24576]{1,0:T(8,128)(2,1)} %param.3) | data formatting | bytes 12582912 | tf_op args[0]
  24.8 8.6 %copy.20 = bf16[128,48,512]{2,0,1:T(8,128)(2,1)} copy(bf16[128,48,512]{0,2,1:T(8,128)(2,1)} %bitcast.78) | data formatting | bytes 12582912 | tf_op jit(solution)/shard_map/concatenate | solution.py:95
  40.3 7.1 fusion.7
  58.3 5.5 reshape.185
  63.9 6.6 copy.26
  70.5 5.5 reshape.186
  75.9 6.6 copy.30
  82.5 5.5 reshape.183
  88.1 6.6 copy.22
  98.3 5.5 copy.23
  103.8 417.8 %all-reduce.3.cloned.1.call-done = (bf16[128,48,2,128]{0,1,2,3:T(8,128)(2,1)}, bf16[128,48,2,128]{0,1,2,3:T(8,128)(2,1)}, bf16[128,48,2,128]{0,1,2,3:T(8,128)(2,1)}) async-done(((bf16[128,48,2,128]{0,1,2,3:T(8,128)(2,1)}, bf16[128,48,2,128]{0,1,2,3:T(8,128)(2,1)}, bf16[128,48,2,128]{0,1,2,3:T(8,128)(2,1)}), (bf16[128,48,2,128]{0,1,2,3:T(8,128)(2,1)}, bf16[128,48,2,128]{0,1,2,3:T(8,128)(2,1)}, ...) | async-done | bytes 9437200 | tf_op jit(solution)/shard_map/psum | solution.py:28
  529.1 4.6 convolution_bitcast_fusion.4
  533.7 6.9 pad_maximum_fusion
  540.6 37.1 %fusion.24 = f32[128,101,128]{2,1,0:T(8,128)} fusion(f32[2,128,128,128]{3,2,1,0:T(8,128)S(1)} %pad_maximum_fusion, f32[101,1,128]{2,0,1:T(8,128)S(1)} %get-tuple-element.19, f32[101,1,128]{2,0,1:T(8,128)S(1)} %get-tuple-element.18), kind=kOutput, calls=%fused_computation.40 | convolution fusion | flops 5083522048 | bytes 23499776 | tf_op jit(solution)/shard_map/tkf,kfba->bta/dot_general | solution.py:81
  580.0 4.6 convolution_bitcast_fusion.2
  584.6 5.6 convolution_bitcast_fusion.3
  590.2 8.5 %pad_maximum_fusion.1 = f32[2,128,128,128]{3,2,1,0:T(8,128)S(1)} fusion(f32[1,128,128,128]{3,2,1,0:T(8,128)} %convolution_bitcast_fusion.2, f32[1,128,128,128]{3,2,1,0:T(8,128)} %convolution_bitcast_fusion.3), kind=kLoop, calls=%fused_computation.1 | loop fusion | flops 4194304 | bytes 33554432 | tf_op jit(solution)/shard_map/stack | solution.py:77
  598.8 26.5 %fusion.27 = f32[128,101,128]{2,1,0:T(8,128)} fusion(f32[2,128,128,128]{3,2,1,0:T(8,128)S(1)} %pad_maximum_fusion.1, f32[101,1,128]{2,0,1:T(8,128)S(1)} %get-tuple-element.19, f32[101,1,128]{2,0,1:T(8,128)S(1)} %get-tuple-element.18), kind=kOutput, calls=%fused_computation.41 | convolution fusion | flops 5083522048 | bytes 23499776 | tf_op jit(solution)/shard_map/tkf,kfba->bta/dot_general | solution.py:81
  627.6 4.6 convolution_bitcast_fusion
  632.2 4.6 convolution_bitcast_fusion.1
  636.8 7.0 pad_maximum_fusion.2
  643.8 26.2 %fusion.30 = f32[128,101,128]{2,1,0:T(8,128)} fusion(f32[2,128,128,128]{3,2,1,0:T(8,128)S(1)} %pad_maximum_fusion.2, f32[101,1,128]{2,0,1:T(8,128)S(1)} %get-tuple-element.19, f32[101,1,128]{2,0,1:T(8,128)S(1)} %get-tuple-element.18), kind=kOutput, calls=%fused_computation.42 | convolution fusion | flops 5083522048 | bytes 23499776 | tf_op jit(solution)/shard_map/tkf,kfba->bta/dot_general | solution.py:81
  670.1 48.8 %reduce-scatter.6.cloned.1.call-done = f32[32,101,128]{2,1,0:T(8,128)} async-done(((f32[128,101,128]{2,1,0:T(8,128)}), f32[32,101,128]{2,1,0:T(8,128)}) %reduce-scatter.6.cloned.1.call-update) | async-done | bytes 1654800 | tf_op jit(solution)/shard_map/reduce_scatter | solution.py:105
  719.0 70.7 %reduce-scatter.8.cloned.1.call-done = f32[32,101,128]{2,1,0:T(8,128)} async-done(((f32[128,101,128]{2,1,0:T(8,128)}), f32[32,101,128]{2,1,0:T(8,128)}) %reduce-scatter.8.cloned.1.call-update) | async-done | bytes 1654800 | tf_op jit(solution)/shard_map/reduce_scatter | solution.py:105
  (40 shorter events, 41.2 us)
Async XLA Ops:
  6.5 515.1 %all-reduce.3.cloned.1.call-start = ((), (), s32[]{:S(2)}) async-start(), calls=%async_computation.6 | async-start | bytes 18874368 | tf_op jit(solution)/shard_map/psum | solution.py:28
  7.5 32.8 %collective-permute-start = (bf16[128,512]{1,0:T(8,128)(2,1)S(1)}, bf16[128,512]{1,0:T(8,128)(2,1)S(1)}, u32[]{:S(2)}, u32[]{:S(2)}) collective-permute-start(bf16[128,512]{1,0:T(8,128)(2,1)S(1)} %slice.40), channel_id=1, source_target_pairs={{1,0},{2,1},{3,2},{5,4},{6,5},{7,6},{9,8},{10,9},{11,10},{13,12},{... | collective-permute-start | bytes 393224 | tf_op jit(solution)/shard_map/ppermute | solution.py:23
  24.8 10.6 %copy-start.3 = (s32[32]{0:T(128)S(1)}, s32[32]{0:T(128)}, u32[]{:S(2)}) copy-start(s32[32]{0:T(128)} %param.5) | copy-start | bytes 388
  94.7 575.4 %reduce-scatter.4.cloned.1.call-start = ((), (), s32[]{:S(2)}) async-start(), calls=%async_computation.3 | async-start | bytes 8519680 | tf_op jit(solution)/shard_map/reduce_scatter | solution.py:105
  521.6 2.9 copy-start.2
  577.7 141.3 %reduce-scatter.6.cloned.1.call-start = ((), (), s32[]{:S(2)}) async-start(), calls=%async_computation.4 | async-start | bytes 8519680 | tf_op jit(solution)/shard_map/reduce_scatter | solution.py:105
  580.0 4.6 copy-start.1
  625.3 164.4 %reduce-scatter.8.cloned.1.call-start = ((), (), s32[]{:S(2)}) async-start(), calls=%async_computation.5 | async-start | bytes 8519680 | tf_op jit(solution)/shard_map/reduce_scatter | solution.py:105
  627.5 4.6 copy-start
Sparse Core Ops, SparseCore 0:
  94.8 426.7 all-reduce.2
  577.8 70.0 reduce-scatter.3
  650.7 68.1 reduce-scatter.5
  721.5 68.2 reduce-scatter.7
where the time goes:
time: 812 us; the launch traced here: 803 us
  waiting for transfers between devices  537 us (66%)
  matrix products  130 us (16%)
  local copies, waits for them, and re-layouts  68.7 us (8%)
  other arithmetic  41.8 us (5%)
  between operations  21.3 us (3%)
    psum x1, waiting for transfers between devices, broadcast(): return lax.psum(jnp.where(mine, x, jnp.zeros_like(x)), axis)  418 us
    reduce_scatter x3, waiting for transfers between devices, shards(): lax.psum_scatter(lag_rows(lag_weights, spectra_pair), 'tm', scatter_dimen...  120 us
    dot_general x3, matrix products, lag_rows(): jnp.einsum('tkf,kfba->bta', lag_weights, spectra_pair, precision=lax.Prec...  89.8 us
    reshape x6, local copies, waits for them, and re-layouts, cross_spectra(): reference_rows.reshape(reference_rows.shape[0], reference_rows.shape[1],...  36.3 us
    another operation x3, other arithmetic, cross_spectra(): return jnp.stack([real_part, imag_part])  22.4 us
  transfers between devices with their start and end apart: 5, of which 3 were waited for; matrix products, arithmetic and copies ran while one was open for 15% of the time, Pallas kernels for 0%

commit v1 on v0

v1 whole, which is shorter than its diff:
```python
import functools
import math

import jax
import jax.numpy as jnp
import ml_dtypes
import numpy as np
from jax import lax
from jax.experimental import pallas as pl
from jax.experimental.pallas import tpu as pltpu
from jax.sharding import PartitionSpec as P

WINLEN = 1024
HOP = 512
BINS = 128
BIN0 = 16
SMOOTH = 4
LAGS = 101
STEPS = 3
HALF_RANK = 24
RANK = 2 * HALF_RANK
ROW = 136
magnitude_eps = 1e-06
water_level = 0.25
VMEM_BYTES = 60 * 1024 * 1024


def dft_table():
    n = np.arange(WINLEN)
    k = BIN0 + np.arange(BINS)
    angles = 2.0 * math.pi / WINLEN * (k[:, None] * n[None, :] % WINLEN)
    taper = 0.5 - 0.5 * np.cos(2.0 * math.pi / WINLEN * n)
    table = np.concatenate([np.cos(angles) * taper, -np.sin(angles) * taper], axis=0)
    return table.astype(np.float32).astype(ml_dtypes.bfloat16)


def band_tables():
    f = np.arange(BINS)
    inside = (np.abs(f[:, None] - f[None, :]) <= SMOOTH).astype(np.float32)
    counts = inside.sum(axis=1)
    return np.tile(inside, (1, 3)).astype(ml_dtypes.bfloat16), (1.0 / counts)[:, None].astype(np.float32)


def dot(a, b):
    return math.fsum(p * q for p, q in zip(a, b))


def row_basis(rows, count):
    left = [list(r) for r in rows]
    basis = []
    for _ in range(count):
        norms = [dot(r, r) for r in left]
        best = max(range(len(left)), key=lambda i: norms[i])
        q = left[best]
        for _ in range(2):
            for b in basis:
                d = dot(q, b)
                q = [x - d * y for x, y in zip(q, b)]
            size = math.sqrt(dot(q, q))
            q = [x / size for x in q]
        basis.append(q)
        for i, r in enumerate(left):
            d = dot(r, q)
            left[i] = [x - d * y for x, y in zip(r, q)]
    return basis


@functools.cache
def lag_factors(windows):
    factor = 1.0 / math.sqrt(BINS * windows)
    mid = LAGS // 2
    bins = range(BIN0, BIN0 + BINS)

    def angle(tau, k):
        return 2.0 * math.pi / WINLEN * (tau * k % WINLEN)

    even = [[math.cos(angle(t, k)) for k in bins] for t in range(mid + 1)]
    odd = [[-math.sin(angle(t, k)) for k in bins] for t in range(1, mid + 1)]
    even_basis = row_basis(even, HALF_RANK)
    odd_basis = row_basis(odd, HALF_RANK)
    even_u = np.array([[dot(r, b) for b in even_basis] for r in even])
    odd_u = np.array([[dot(r, b) for b in odd_basis] for r in odd])
    u = np.zeros((LAGS, RANK))
    for t in range(LAGS):
        tau = t - mid
        u[t, :HALF_RANK] = even_u[abs(tau)]
        if tau:
            u[t, HALF_RANK:] = math.copysign(1.0, tau) * odd_u[abs(tau) - 1]
    return u * factor, np.array(even_basis), np.array(odd_basis)


def split_bf16(value):
    high = value.astype(np.float32).astype(ml_dtypes.bfloat16)
    low = (value - high.astype(np.float64)).astype(np.float32).astype(ml_dtypes.bfloat16)
    return high, low


def bin_order():
    order = []
    for j in range(32):
        x, z, y = j // 8, j // 2 % 4, j % 2
        order += [2 * j, 2 * j + 1]
        order += [64 + 2 * ((z * 4 + x) * 2 + y), 65 + 2 * ((z * 4 + x) * 2 + y)]
    return np.array(order)


def spectra_kernel(windows, chunk, x_ref, next_ref, edge_ref, table_ref, band_ref, inverse_ref, out_ref, rows):
    i = pl.program_id(0)
    last = pl.num_programs(0) - 1
    tail = jnp.where(i == last, edge_ref[...], next_ref[...])
    for pair in range(chunk // 2):
        frames = []
        for w in (2 * pair, 2 * pair + 1):
            if w == chunk - 1:
                frames.append(jnp.concatenate([x_ref[:, w * HOP :], tail], axis=1))
            else:
                frames.append(x_ref[:, w * HOP : w * HOP + WINLEN])
        spectra = lax.dot_general(
            table_ref[...],
            jnp.concatenate(frames, axis=0),
            (((1,), (1,)), ((), ())),
            preferred_element_type=jnp.float32,
        )
        re, im = spectra[:BINS], spectra[BINS:]
        magnitude = jnp.sqrt(re * re + im * im + magnitude_eps)
        high = magnitude.astype(jnp.bfloat16)
        rest = magnitude - high.astype(jnp.float32)
        mid = rest.astype(jnp.bfloat16)
        low = (rest - mid.astype(jnp.float32)).astype(jnp.bfloat16)
        running = jnp.dot(
            band_ref[...], jnp.concatenate([high, mid, low], axis=0), preferred_element_type=jnp.float32
        )
        mean = jnp.sum(magnitude, axis=0, keepdims=True) * (1.0 / BINS)
        scale = 1.0 / (running * inverse_ref[...] + water_level * mean)
        for part, value in enumerate((re, im)):
            white = value * scale
            for h in range(2):
                row = part * windows + i * chunk + 2 * pair + h
                rows[pl.ds(row, BINS, stride=2 * windows), :] = white[:, h * 128 : (h + 1) * 128]

    @pl.when(i == last)
    def _():
        def one(j, carry):
            x, z, y = j // 8, (j // 2) % 4, j % 2
            first = 2 * j
            second = 64 + 2 * ((z * 4 + x) * 2 + y)
            for slot, f in enumerate((first, first + 1, second, second + 1)):
                start = pl.multiple_of(f * 2 * windows, 2 * windows)
                out_ref[4 * j + slot] = rows[pl.ds(start, 2 * windows), :].astype(jnp.bfloat16)
            return carry

        lax.fori_loop(0, 32, one, 0)


def whitened_spectra(samples, edge):
    channels, length = samples.shape
    windows = length // HOP
    chunk = 8
    band, inverse = band_tables()
    steps = windows // chunk
    whole = lambda shape: pl.BlockSpec(shape, lambda i: (0,) * len(shape))
    return pl.pallas_call(
        functools.partial(spectra_kernel, windows, chunk),
        grid=(steps,),
        out_shape=jax.ShapeDtypeStruct((BINS, 2 * windows, channels), jnp.bfloat16),
        in_specs=[
            pl.BlockSpec((channels, chunk * HOP), lambda i: (0, i)),
            pl.BlockSpec((channels, HOP), lambda i: (0, jnp.minimum((i + 1) * chunk, windows - 1))),
            whole((channels, HOP)),
            whole((2 * BINS, WINLEN)),
            whole((BINS, 3 * BINS)),
            whole((BINS, 1)),
        ],
        out_specs=whole((BINS, 2 * windows, channels)),
        scratch_shapes=[pltpu.VMEM((BINS * 2 * windows, channels), jnp.float32)],
        compiler_params=pltpu.CompilerParams(vmem_limit_bytes=VMEM_BYTES),
        name="spectra",
    )(samples, samples, edge, jnp.asarray(dft_table()), jnp.asarray(band), jnp.asarray(inverse))


def cross_kernel(windows, sizes, slots_ref, v_ref, own_ref, *refs):
    pieces = refs[: len(sizes)]
    out_ref, real_rows, imag_rows = refs[len(sizes) :]
    base = 0
    for piece, size in zip(pieces, sizes):

        def one(n, carry, piece=piece, base=base):
            q = slots_ref[base + n]
            own = own_ref[q]
            turned = jnp.concatenate([own[windows:], -own[:windows]], axis=0)
            cross = lax.dot_general(
                piece[n],
                jnp.concatenate([own, turned], axis=1),
                (((0,), (0,)), ((), ())),
                preferred_element_type=jnp.float32,
            )
            real_rows[pl.ds(q, 128, stride=ROW), :] = cross[:, :128]
            imag_rows[pl.ds(q, 128, stride=ROW), :] = cross[:, 128:]
            return carry

        lax.fori_loop(0, size, one, 0, unroll=4)
        base += size

    def two(n, carry):
        halves = []
        for h in range(2):
            start = pl.multiple_of((2 * n + h) * ROW, 8)
            halves.append(
                jnp.concatenate(
                    [real_rows[pl.ds(start, 128), :], imag_rows[pl.ds(start, 128), :]], axis=0
                ).astype(jnp.bfloat16)
            )
        both = jnp.dot(v_ref[...], jnp.concatenate(halves, axis=1), preferred_element_type=jnp.float32)
        total = both[:RANK] + both[RANK:]
        for h in range(2):
            out_ref[2 * n + h] = total[:, h * 128 : (h + 1) * 128].astype(out_ref.dtype)
        return carry

    lax.fori_loop(0, 64, two, 0, unroll=2)


def lag_coefficients(own, pieces, slots, v):
    windows = own.shape[1] // 2
    sizes = tuple(p.shape[0] for p in pieces)
    vmem = pl.BlockSpec(memory_space=pltpu.VMEM)
    return pl.pallas_call(
        functools.partial(cross_kernel, windows, sizes),
        out_shape=jax.ShapeDtypeStruct((128, RANK, 128), jnp.bfloat16),
        in_specs=[pl.BlockSpec(memory_space=pltpu.SMEM)] + [vmem] * (2 + len(pieces)),
        out_specs=vmem,
        scratch_shapes=[pltpu.VMEM((128 * ROW, 128), jnp.float32)] * 2,
        compiler_params=pltpu.CompilerParams(vmem_limit_bytes=VMEM_BYTES),
        name="cross",
    )(slots, v, own, *pieces)


def expand_kernel(u_ref, *refs):
    coefs, out_ref = refs[:-1], refs[-1]
    for s, c_ref in enumerate(coefs):

        def two(n, carry, s=s, c_ref=c_ref):
            value = jnp.concatenate([c_ref[2 * n], c_ref[2 * n + 1]], axis=1)
            high = value.astype(jnp.bfloat16)
            low = (value - high.astype(jnp.float32)).astype(jnp.bfloat16)
            lags = jnp.dot(
                u_ref[...], jnp.concatenate([high, high, low], axis=0), preferred_element_type=jnp.float32
            )
            out_ref[2 * n, s] = lags[:LAGS, :128]
            out_ref[2 * n + 1, s] = lags[:LAGS, 128:]
            return carry

        lax.fori_loop(0, c_ref.shape[0] // 2, two, 0, unroll=2)


def expand(coefs, u):
    vmem = pl.BlockSpec(memory_space=pltpu.VMEM)
    return pl.pallas_call(
        expand_kernel,
        out_shape=jax.ShapeDtypeStruct((coefs[0].shape[0], len(coefs), LAGS, 128), jnp.float32),
        in_specs=[vmem] * (1 + len(coefs)),
        out_specs=vmem,
        compiler_params=pltpu.CompilerParams(vmem_limit_bytes=VMEM_BYTES),
        name="expand",
    )(u, *coefs)


def place(x, z, y):
    return (x % 4) * 8 + (z % 4) * 2 + y % 2


def shift(value, dx=0, dz=0, dy=0):
    pairs = [(place(x, z, y), place(x + dx, z + dz, y + dy)) for x in range(4) for z in range(4) for y in range(2)]
    return lax.ppermute(value, "chan", pairs)


def gather_references(parts):
    both = jnp.concatenate([parts, shift(parts, dy=1)], axis=1)
    first = jnp.concatenate([both[:, 0:2], both[:, 4:6]], axis=1)
    second = jnp.concatenate([both[:, 2:4], both[:, 6:8]], axis=1)
    a = [shift(first, dz=1), shift(first, dz=-1)]
    b = [shift(second, dx=1), shift(second, dx=-1)]
    a, b = lax.optimization_barrier((a, b))
    a += [shift(a[0][:, :2], dz=1), shift(a[1][:, 2:], dz=-1)]
    b += [shift(b[0][:, :2], dx=1), shift(b[1][:, 2:], dx=-1)]
    a, b = lax.optimization_barrier((a, b))
    plane_a = jnp.concatenate([first] + a, axis=1)
    plane_b = jnp.concatenate([second] + b, axis=1)
    steps = parts.shape[0]
    before = None
    for s in range(steps + 1):
        sends = []
        for plane, axis in ((plane_a, "dx"), (plane_b, "dz")):
            for side, sign in ((0, 1), (1, -1)):
                group = []
                if before is not None:
                    got = before[axis][side]
                    group.append(got[:8] if side == 0 else got[8:])
                if s < steps:
                    group.append(plane[s])
                value = jnp.concatenate(group, axis=0) if len(group) > 1 else group[0]
                sends.append(shift(value, **{axis: sign}))
        sends = lax.optimization_barrier(sends)
        ahead = {}
        far = {}
        for n, axis in enumerate(("dx", "dz")):
            pair = sends[2 * n : 2 * n + 2]
            if before is not None:
                far[axis] = [p[:8] for p in pair]
                pair = [p[8:] for p in pair]
            ahead[axis] = pair
        if before is not None:
            yield (
                [plane_a[s - 1]] + before["dx"] + far["dx"] + [plane_b[s - 1]] + before["dz"] + far["dz"]
            )
        before = ahead


def slot_table():
    me = lax.axis_index("chan")
    x, z, y = me // 8, me // 2 % 4, me % 2
    offsets = (0, -1, 1, 2)
    dl, ds, dy, e = np.meshgrid(np.array(offsets), np.array(offsets), np.arange(2), np.arange(2), indexing="ij")
    dl, ds, dy, e = (t.reshape(-1).astype(np.int32) for t in (dl, ds, dy, e))
    y_of = (y + dy) % 2
    first = (((x + dl + 4) % 4) * 8 + ((z + ds + 4) % 4) * 2 + y_of) * 4 + e
    second = (((x + ds + 4) % 4) * 8 + ((z + dl + 4) % 4) * 2 + y_of) * 4 + 2 + e
    return jnp.concatenate([first, second]).astype(jnp.int32)


def sum_over_spans(value):
    me = lax.axis_index("tm")
    half, core = me // 2, me % 2
    quarters = value.reshape(2, 2, 32, RANK, 128)
    sent = lax.dynamic_index_in_dim(quarters, 1 - core, 1, keepdims=False)
    kept = lax.dynamic_index_in_dim(quarters, core, 1, keepdims=False).astype(jnp.float32)
    got = lax.ppermute(sent, "tm", [(0, 1), (1, 0), (2, 3), (3, 2)])
    chip = kept + got.astype(jnp.float32)
    sent = lax.dynamic_index_in_dim(chip, 1 - half, 0, keepdims=False).astype(jnp.bfloat16)
    kept = lax.dynamic_index_in_dim(chip, half, 0, keepdims=False)
    got = lax.ppermute(sent, "tm", [(0, 2), (2, 0), (1, 3), (3, 1)])
    return kept + got.astype(jnp.float32)


def shards(samples, plan, owner_table):
    windows = samples.shape[1] // HOP * lax.axis_size("tm")
    edge = lax.ppermute(samples[:, :HOP], "tm", [(1, 0), (2, 1), (3, 2)])
    own = whitened_spectra(samples, edge)
    everyone = lax.all_to_all(own.reshape((32, 4) + own.shape[1:]), "chan", 0, 0)
    roots = owner_table[plan]
    parts = jnp.stack([lax.dynamic_index_in_dim(everyone, roots[s], 0, keepdims=False) for s in range(STEPS)])
    u, even_basis, odd_basis = lag_factors(windows)
    order = bin_order()
    v = np.zeros((RANK, 2 * BINS))
    v[:HALF_RANK, :BINS] = even_basis[:, order]
    v[HALF_RANK:, BINS:] = odd_basis[:, order]
    v = jnp.asarray(np.concatenate(split_bf16(v), axis=0))
    padded = np.zeros((104, RANK))
    padded[:LAGS] = u
    u_high, u_low = split_bf16(padded)
    u = jnp.asarray(np.concatenate([u_high, u_low, u_high], axis=1))
    slots = slot_table()
    totals = []
    for pieces in gather_references(parts):
        totals.append(sum_over_spans(lag_coefficients(own, pieces, slots, v)))
    return expand(totals, u)


def solution(mesh):
    placed = (P("chan", "tm"), P(), P())
    return jax.shard_map(
        shards, mesh=mesh, in_specs=placed, out_specs=P("tm", None, None, "chan"), check_vma=False
    )
```

time: 812 us -> 280 us (0.34); the launches traced: 803 us -> 280 us
  waiting for transfers between devices: 537 us -> 87.9 us
  matrix products: 130 us -> 0 us
  Pallas kernels: 0 us -> 87.3 us
  starting transfers between devices: 3.71 us -> 57.5 us
  local copies, waits for them, and re-layouts: 68.7 us -> 30.6 us
  other arithmetic: 41.8 us -> 9.98 us
  between operations: 21.3 us -> 6.34 us
    psum x1 -> x0, waiting for transfers between devices: 418 us -> none  [broadcast(): return lax.psum(jnp.where(mine, x, jnp.zeros_like(x)), axis)]
    dot_general x11 -> x0, matrix products: 130 us -> none  [the longest x3 89.8 us: lag_rows(): jnp.einsum('tkf,kfba->bta', lag_weights, spectra_pair, precision=lax.Prec...]
    reduce_scatter x3 -> x0, waiting for transfers between devices: 120 us -> none  [shards(): lax.psum_scatter(lag_rows(lag_weights, spectra_pair), 'tm', scatter_dimen...]
    pallas_call x0 -> x5, Pallas kernels: none -> 87.3 us  [the longest x3 59.8 us: lag_coefficients(): pl.pallas_call(functools.partial(cross_kernel, windows, sizes), out_shape...]
    ppermute x1 -> x32, waiting for transfers between devices: 0.01 us -> 55.8 us  [the longest x25 29.3 us: shift(): return lax.ppermute(value, 'chan', pairs)]
    ppermute x1 -> x32, starting transfers between devices: 3.33 us -> 48.7 us  [the longest x25 33.3 us: shift(): return lax.ppermute(value, 'chan', pairs)]
    reshape x8 -> x0, local copies, waits for them, and re-layouts: 44.8 us -> none  [the longest x6 36.3 us: cross_spectra(): reference_rows.reshape(reference_rows.shape[0], reference_rows.shape[1],...]
    all_to_all x0 -> x1, waiting for transfers between devices: none -> 32.1 us  [shards(): lax.all_to_all(own.reshape((32, 4) + own.shape[1:]), 'chan', 0, 0)]
  transfers between devices with their start and end apart: 5 -> 33, of which waited for: 3 -> 14; matrix products, arithmetic and copies ran while one was open for 15% -> 9% of each run, Pallas kernels for 0% -> 21%
where the time goes in v1:
time: 280 us
  waiting for transfers between devices  87.9 us (31%)
  Pallas kernels  87.3 us (31%)
  starting transfers between devices  57.5 us (21%)
  local copies, waits for them, and re-layouts  30.6 us (11%)
  other arithmetic  9.98 us (4%)
  between operations  6.34 us (2%)
    pallas_call x3, Pallas kernels, lag_coefficients(): pl.pallas_call(functools.partial(cross_kernel, windows, sizes), out_shape...  59.8 us
    ppermute x25, starting transfers between devices, shift(): return lax.ppermute(value, 'chan', pairs)  33.3 us
    all_to_all x1, waiting for transfers between devices, shards(): lax.all_to_all(own.reshape((32, 4) + own.shape[1:]), 'chan', 0, 0)  32.1 us
    ppermute x25, waiting for transfers between devices, shift(): return lax.ppermute(value, 'chan', pairs)  29.3 us
    ppermute x3, waiting for transfers between devices, sum_over_spans(): got = lax.ppermute(sent, 'tm', [(0, 2), (2, 0), (1, 3), (3, 1)])  21 us
    pallas_call x1, Pallas kernels, whitened_spectra(): pl.pallas_call(functools.partial(spectra_kernel, windows, chunk), grid=(s...  19.5 us
    ppermute x3, starting transfers between devices, sum_over_spans(): got = lax.ppermute(sent, 'tm', [(0, 1), (1, 0), (2, 3), (3, 2)])  8.91 us
    all_to_all x1, starting transfers between devices, shards(): lax.all_to_all(own.reshape((32, 4) + own.shape[1:]), 'chan', 0, 0)  8.79 us
  transfers between devices with their start and end apart: 33, of which 14 were waited for; matrix products, arithmetic and copies ran while one was open for 9% of the time, Pallas kernels for 21%

profile of v1, /device:TPU:1, one launch (start us, length us, event | category | flops | bytes accessed | tf_op | source)
XLA Modules:
  0.0 279.7 jit_solution(3220139682684157448)
XLA Ops:
  0.9 3.3 %collective-permute-start = (bf16[128,512]{1,0:T(8,128)(2,1)S(1)}, bf16[128,512]{1,0:T(8,128)(2,1)S(1)}, u32[]{:S(2)}, u32[]{:S(2)}) collective-permute-start(bf16[128,512]{1,0:T(8,128)(2,1)S(1)} %slice.158), channel_id=1, source_target_pairs={{1,0},{2,1},{3,2},{5,4},{6,5},{7,6},{9,8},{10,9},{11,10},{13,12},{... | collective-permute-start | bytes 393224 | tf_op jit(solution)/shard_map/ppermute | solution.py:346
  4.3 5.5 %collective-permute-done.edge_ref = bf16[128,512]{1,0:T(8,128)(2,1)S(1)} collective-permute-done((bf16[128,512]{1,0:T(8,128)(2,1)S(1)}, bf16[128,512]{1,0:T(8,128)(2,1)S(1)}, u32[]{:S(2)}, u32[]{:S(2)}) %collective-permute-start) | collective-permute-done | bytes 131104 | tf_op jit(solution)/shard_map/ppermute | solution.py:346
  10.4 19.5 %spectra.1.own_ref = bf16[128,96,128]{2,1,0:T(8,128)(2,1)} custom-call(bf16[128,24576]{1,0:T(8,128)(2,1)} %next_ref.1, bf16[128,24576]{1,0:T(8,128)(2,1)} %next_ref.1, bf16[128,512]{1,0:T(8,128)(2,1)} %copy-done.19, bf16[256,1024]{1,0:T(8,128)(2,1)} %constant.164.clone.table_ref, bf16[128,384]{1,0:T(8,128)(2,1)} %constant.165.clone.band_ref, ...), custom_call_target="tpu_custom_call" | custom-call | tf_op jit(solution)/shard_map/spectra/pallas_call | solution.py:162
  29.9 8.8 %all-to-all-start = ((bf16[32,4,96,128]{3,2,1,0:T(8,128)(2,1)}), bf16[32,4,96,128]{3,2,1,0:T(8,128)(2,1)S(1)}, u32[]{:S(2)}, u32[]{:S(2)}) async-start(bf16[32,4,96,128]{3,2,1,0:T(8,128)(2,1)} %bitcast.52), calls=%async_computation | async-start | bytes 6291456 | tf_op jit(solution)/shard_map/all_to_all | solution.py:348
  45.9 32.1 %all-to-all-done = bf16[32,4,96,128]{3,2,1,0:T(8,128)(2,1)S(1)} async-done(((bf16[32,4,96,128]{3,2,1,0:T(8,128)(2,1)}), bf16[32,4,96,128]{3,2,1,0:T(8,128)(2,1)S(1)}, u32[]{:S(2)}, u32[]{:S(2)}) %all-to-all-start) | async-done | bytes 3145760 | tf_op jit(solution)/shard_map/all_to_all | solution.py:348
  78.3 6.7 %collective-permute-done.1 = bf16[3,4,96,128]{3,2,1,0:T(8,128)(2,1)S(1)} collective-permute-done((bf16[3,4,96,128]{3,2,1,0:T(8,128)(2,1)S(1)}, bf16[3,4,96,128]{3,2,1,0:T(8,128)(2,1)S(1)}, u32[]{:S(2)}, u32[]{:S(2)}) %collective-permute-start.1) | collective-permute-done | bytes 294944 | tf_op jit(solution)/shard_map/ppermute | solution.py:273
  90.6 3.9 %collective-permute-done.2 = bf16[3,4,96,128]{3,2,1,0:T(8,128)(2,1)S(1)} collective-permute-done((bf16[3,4,96,128]{3,2,1,0:T(8,128)(2,1)S(1)}, bf16[3,4,96,128]{3,2,1,0:T(8,128)(2,1)S(1)}, u32[]{:S(2)}, u32[]{:S(2)}) %collective-permute-start.2) | collective-permute-done | bytes 294944 | tf_op jit(solution)/shard_map/ppermute | solution.py:273
  97.4 2.7 collective-permute-start.7
  114.1 2.9 %collective-permute-done.12.refs_6_ = bf16[16,96,128]{2,1,0:T(8,128)(2,1)S(1)} collective-permute-done((bf16[16,96,128]{2,1,0:T(8,128)(2,1)S(1)}, bf16[16,96,128]{2,1,0:T(8,128)(2,1)S(1)}, u32[]{:S(2)}, u32[]{:S(2)}) %collective-permute-start.12) | collective-permute-done | bytes 393248 | tf_op jit(solution)/shard_map/ppermute | solution.py:273
  118.4 2.7 collective-permute-start.15
  122.3 2.7 collective-permute-start.17
  125.0 4.7 %collective-permute-done.14 = bf16[24,96,128]{2,1,0:T(8,128)(2,1)S(1)} collective-permute-done((bf16[24,96,128]{2,1,0:T(8,128)(2,1)}, bf16[24,96,128]{2,1,0:T(8,128)(2,1)S(1)}, u32[]{:S(2)}, u32[]{:S(2)}) %collective-permute-start.14) | collective-permute-done | bytes 589856 | tf_op jit(solution)/shard_map/ppermute | solution.py:273
  129.7 3.3 %collective-permute-done.16 = bf16[24,96,128]{2,1,0:T(8,128)(2,1)S(1)} collective-permute-done((bf16[24,96,128]{2,1,0:T(8,128)(2,1)}, bf16[24,96,128]{2,1,0:T(8,128)(2,1)S(1)}, u32[]{:S(2)}, u32[]{:S(2)}) %collective-permute-start.16) | collective-permute-done | bytes 589856 | tf_op jit(solution)/shard_map/ppermute | solution.py:273
  147.4 19.9 %cross.3 = bf16[128,48,128]{2,1,0:T(8,128)(2,1)} custom-call(s32[128]{0:T(128)} %pad_add_fusion.slots_ref, bf16[96,256]{1,0:T(8,128)(2,1)} %constant.167.clone.v_ref, bf16[128,96,128]{2,1,0:T(8,128)(2,1)} %spectra.1.own_ref, bf16[16,96,128]{2,1,0:T(8,128)(2,1)} %copy-done.9, bf16[16,96,128]{2,1,0:T(8,128)(2,1)} %copy-done.15, ...), custom_call_target="tpu_custom_call" | custom-call | tf_op jit(solution)/shard_map/cross/pallas_call | solution.py:226
  168.4 7.7 %collective-permute-start.18 = (bf16[2,32,48,128]{3,2,1,0:T(8,128)(2,1)S(1)}, bf16[2,32,48,128]{3,2,1,0:T(8,128)(2,1)S(1)}, u32[]{:S(2)}, u32[]{:S(2)}) collective-permute-start(bf16[2,32,48,128]{3,2,1,0:T(8,128)(2,1)S(1)} %dynamic-slice_bitcast_fusion.2), channel_id=1, source_target_pairs={{0,1},{1,0},{2,3},{3,2},{4,5},{5,4},{6,7},{7,6},{8,9},{9,8},{10,11... | collective-permute-start | bytes 2359304 | tf_op jit(solution)/shard_map/ppermute | solution.py:336
  181.4 19.9 %cross.4 = bf16[128,48,128]{2,1,0:T(8,128)(2,1)} custom-call(s32[128]{0:T(128)} %pad_add_fusion.slots_ref, bf16[96,256]{1,0:T(8,128)(2,1)} %constant.167.clone.v_ref, bf16[128,96,128]{2,1,0:T(8,128)(2,1)} %spectra.1.own_ref, bf16[16,96,128]{2,1,0:T(8,128)(2,1)} %copy-done.7, bf16[16,96,128]{2,1,0:T(8,128)(2,1)} %slice.182.refs_1_, ...), custom_call_target="tpu_custom_call" | custom-call | tf_op jit(solution)/shard_map/cross/pallas_call | solution.py:226
  202.7 2.9 %collective-permute-start.27 = (bf16[8,96,128]{2,1,0:T(8,128)(2,1)}, bf16[8,96,128]{2,1,0:T(8,128)(2,1)}, u32[]{:S(2)}, u32[]{:S(2)}) collective-permute-start(bf16[8,96,128]{2,1,0:T(8,128)(2,1)} %get-tuple-element.76), channel_id=1, source_target_pairs={{0,96},{4,100},{8,104},{12,108},{16,112},{20,116},{24,120},{28,124... | collective-permute-start | bytes 589832 | tf_op jit(solution)/shard_map/ppermute | solution.py:273
  205.6 2.7 collective-permute-start.29
  213.5 20.0 %cross.5 = bf16[128,48,128]{2,1,0:T(8,128)(2,1)} custom-call(s32[128]{0:T(128)} %pad_add_fusion.slots_ref, bf16[96,256]{1,0:T(8,128)(2,1)} %constant.167.clone.v_ref, bf16[128,96,128]{2,1,0:T(8,128)(2,1)} %spectra.1.own_ref, bf16[16,96,128]{2,1,0:T(8,128)(2,1)} %copy-done.5, bf16[16,96,128]{2,1,0:T(8,128)(2,1)} %slice.196.refs_1_, ...), custom_call_target="tpu_custom_call" | custom-call | tf_op jit(solution)/shard_map/cross/pallas_call | solution.py:226
  242.2 6.0 %collective-permute-done.19 = bf16[32,48,128]{2,1,0:T(8,128)(2,1)S(1)} collective-permute-done((bf16[32,48,128]{2,1,0:T(8,128)(2,1)S(1)}, bf16[32,48,128]{2,1,0:T(8,128)(2,1)S(1)}, u32[]{:S(2)}, u32[]{:S(2)}) %collective-permute-start.19) | collective-permute-done | bytes 393248 | tf_op jit(solution)/shard_map/ppermute | solution.py:340
  249.1 7.5 %collective-permute-done.25 = bf16[32,48,128]{2,1,0:T(8,128)(2,1)S(1)} collective-permute-done((bf16[32,48,128]{2,1,0:T(8,128)(2,1)S(1)}, bf16[32,48,128]{2,1,0:T(8,128)(2,1)S(1)}, u32[]{:S(2)}, u32[]{:S(2)}) %collective-permute-start.25) | collective-permute-done | bytes 393248 | tf_op jit(solution)/shard_map/ppermute | solution.py:340
  257.6 7.5 %collective-permute-done.31 = bf16[32,48,128]{2,1,0:T(8,128)(2,1)S(1)} collective-permute-done((bf16[32,48,128]{2,1,0:T(8,128)(2,1)S(1)}, bf16[32,48,128]{2,1,0:T(8,128)(2,1)S(1)}, u32[]{:S(2)}, u32[]{:S(2)}) %collective-permute-start.31) | collective-permute-done | bytes 393248 | tf_op jit(solution)/shard_map/ppermute | solution.py:340
  266.0 8.1 %expand.1 = f32[32,3,101,128]{3,2,1,0:T(8,128)} custom-call(bf16[104,144]{1,0:T(8,128)(2,1)} %constant.168.clone.u_ref, f32[32,48,128]{2,1,0:T(8,128)} %bitcast_add_fusion.2.refs_0_, f32[32,48,128]{2,1,0:T(8,128)} %bitcast_add_fusion.1.refs_1_, f32[32,48,128]{2,1,0:T(8,128)} %bitcast_add_fusion.refs_2_), custom_call_target="tpu_custom_call" | custom-call | tf_op jit(solution)/shard_map/expand/pallas_call | solution.py:257
  274.1 5.6 %copy.17 = f32[32,3,101,128]{3,0,2,1:T(8,128)} copy(f32[32,3,101,128]{3,2,1,0:T(8,128)} %expand.1) | data formatting | bytes 9928704 | tf_op jit(solution)/shard_map/expand/pallas_call | solution.py:257
  (161 shorter events, 66.7 us)
Async XLA Ops:
  0.9 8.9 %collective-permute-start = (bf16[128,512]{1,0:T(8,128)(2,1)S(1)}, bf16[128,512]{1,0:T(8,128)(2,1)S(1)}, u32[]{:S(2)}, u32[]{:S(2)}) collective-permute-start(bf16[128,512]{1,0:T(8,128)(2,1)S(1)} %slice.158), channel_id=1, source_target_pairs={{1,0},{2,1},{3,2},{5,4},{6,5},{7,6},{9,8},{10,9},{11,10},{13,12},{... | collective-permute-start | bytes 393224 | tf_op jit(solution)/shard_map/ppermute | solution.py:346
  29.9 48.1 %all-to-all-start = ((bf16[32,4,96,128]{3,2,1,0:T(8,128)(2,1)}), bf16[32,4,96,128]{3,2,1,0:T(8,128)(2,1)S(1)}, u32[]{:S(2)}, u32[]{:S(2)}) async-start(bf16[32,4,96,128]{3,2,1,0:T(8,128)(2,1)} %bitcast.52), calls=%async_computation | async-start | bytes 6291456 | tf_op jit(solution)/shard_map/all_to_all | solution.py:348
  85.1 9.5 %collective-permute-start.2 = (bf16[3,4,96,128]{3,2,1,0:T(8,128)(2,1)S(1)}, bf16[3,4,96,128]{3,2,1,0:T(8,128)(2,1)S(1)}, u32[]{:S(2)}, u32[]{:S(2)}) collective-permute-start(bf16[3,4,96,128]{3,2,1,0:T(8,128)(2,1)S(1)} %pad_maximum_fusion.9), channel_id=1, source_target_pairs={{0,8},{4,12},{8,16},{12,20},{16,24},{20,28},{24,0},{28,4},{32,40},... | collective-permute-start | bytes 884744 | tf_op jit(solution)/shard_map/ppermute | solution.py:273
  85.2 9.4 %collective-permute-start.3 = (bf16[3,4,96,128]{3,2,1,0:T(8,128)(2,1)S(1)}, bf16[3,4,96,128]{3,2,1,0:T(8,128)(2,1)S(1)}, u32[]{:S(2)}, u32[]{:S(2)}) collective-permute-start(bf16[3,4,96,128]{3,2,1,0:T(8,128)(2,1)S(1)} %pad_maximum_fusion.9), channel_id=1, source_target_pairs={{0,24},{4,28},{8,0},{12,4},{16,8},{20,12},{24,16},{28,20},{32,56},... | collective-permute-start | bytes 884744 | tf_op jit(solution)/shard_map/ppermute | solution.py:273
  87.9 8.9 %collective-permute-start.4 = (bf16[3,4,96,128]{3,2,1,0:T(8,128)(2,1)S(1)}, bf16[3,4,96,128]{3,2,1,0:T(8,128)(2,1)S(1)}, u32[]{:S(2)}, u32[]{:S(2)}) collective-permute-start(bf16[3,4,96,128]{3,2,1,0:T(8,128)(2,1)S(1)} %pad_maximum_fusion.10), channel_id=1, source_target_pairs={{0,32},{4,36},{8,40},{12,44},{16,48},{20,52},{24,56},{28,60},{32,6... | collective-permute-start | bytes 884744 | tf_op jit(solution)/shard_map/ppermute | solution.py:273
  105.7 8.4 %collective-permute-start.10 = (bf16[16,96,128]{2,1,0:T(8,128)(2,1)S(1)}, bf16[16,96,128]{2,1,0:T(8,128)(2,1)S(1)}, u32[]{:S(2)}, u32[]{:S(2)}) collective-permute-start(bf16[16,96,128]{2,1,0:T(8,128)(2,1)S(1)} %get-tuple-element.71.refs_0_), channel_id=1, source_target_pairs={{0,32},{4,36},{8,40},{12,44},{16,48},{20,52},{24,56},{28,60},{32,6... | collective-permute-start | bytes 1179656 | tf_op jit(solution)/shard_map/ppermute | solution.py:273
  106.1 8.0 %collective-permute-start.11 = (bf16[16,96,128]{2,1,0:T(8,128)(2,1)S(1)}, bf16[16,96,128]{2,1,0:T(8,128)(2,1)S(1)}, u32[]{:S(2)}, u32[]{:S(2)}) collective-permute-start(bf16[16,96,128]{2,1,0:T(8,128)(2,1)S(1)} %get-tuple-element.71.refs_0_), channel_id=1, source_target_pairs={{0,96},{4,100},{8,104},{12,108},{16,112},{20,116},{24,120},{28,124... | collective-permute-start | bytes 1179656 | tf_op jit(solution)/shard_map/ppermute | solution.py:273
  108.8 8.2 %collective-permute-start.12 = (bf16[16,96,128]{2,1,0:T(8,128)(2,1)S(1)}, bf16[16,96,128]{2,1,0:T(8,128)(2,1)S(1)}, u32[]{:S(2)}, u32[]{:S(2)}) collective-permute-start(bf16[16,96,128]{2,1,0:T(8,128)(2,1)S(1)} %get-tuple-element.68.refs_5_), channel_id=1, source_target_pairs={{0,8},{4,12},{8,16},{12,20},{16,24},{20,28},{24,0},{28,4},{32,40},... | collective-permute-start | bytes 1179656 | tf_op jit(solution)/shard_map/ppermute | solution.py:273
  108.9 8.1 %collective-permute-start.13 = (bf16[16,96,128]{2,1,0:T(8,128)(2,1)S(1)}, bf16[16,96,128]{2,1,0:T(8,128)(2,1)S(1)}, u32[]{:S(2)}, u32[]{:S(2)}) collective-permute-start(bf16[16,96,128]{2,1,0:T(8,128)(2,1)S(1)} %get-tuple-element.68.refs_5_), channel_id=1, source_target_pairs={{0,24},{4,28},{8,0},{12,4},{16,8},{20,12},{24,16},{28,20},{32,56},... | collective-permute-start | bytes 1179656 | tf_op jit(solution)/shard_map/ppermute | solution.py:273
  118.4 11.3 %collective-permute-start.14 = (bf16[24,96,128]{2,1,0:T(8,128)(2,1)}, bf16[24,96,128]{2,1,0:T(8,128)(2,1)S(1)}, u32[]{:S(2)}, u32[]{:S(2)}) collective-permute-start(bf16[24,96,128]{2,1,0:T(8,128)(2,1)} %get-tuple-element.95), channel_id=1, source_target_pairs={{0,32},{4,36},{8,40},{12,44},{16,48},{20,52},{24,56},{28,60},{32,6... | collective-permute-start | bytes 1769480 | tf_op jit(solution)/shard_map/ppermute | solution.py:273
  118.4 11.2 %collective-permute-start.15 = (bf16[24,96,128]{2,1,0:T(8,128)(2,1)}, bf16[24,96,128]{2,1,0:T(8,128)(2,1)S(1)}, u32[]{:S(2)}, u32[]{:S(2)}) collective-permute-start(bf16[24,96,128]{2,1,0:T(8,128)(2,1)} %get-tuple-element.94), channel_id=1, source_target_pairs={{0,96},{4,100},{8,104},{12,108},{16,112},{20,116},{24,120},{28,124... | collective-permute-start | bytes 1769480 | tf_op jit(solution)/shard_map/ppermute | solution.py:273
  122.3 10.7 %collective-permute-start.16 = (bf16[24,96,128]{2,1,0:T(8,128)(2,1)}, bf16[24,96,128]{2,1,0:T(8,128)(2,1)S(1)}, u32[]{:S(2)}, u32[]{:S(2)}) collective-permute-start(bf16[24,96,128]{2,1,0:T(8,128)(2,1)} %get-tuple-element.93), channel_id=1, source_target_pairs={{0,8},{4,12},{8,16},{12,20},{16,24},{20,28},{24,0},{28,4},{32,40},... | collective-permute-start | bytes 1769480 | tf_op jit(solution)/shard_map/ppermute | solution.py:273
  122.3 10.7 %collective-permute-start.17 = (bf16[24,96,128]{2,1,0:T(8,128)(2,1)}, bf16[24,96,128]{2,1,0:T(8,128)(2,1)S(1)}, u32[]{:S(2)}, u32[]{:S(2)}) collective-permute-start(bf16[24,96,128]{2,1,0:T(8,128)(2,1)} %get-tuple-element.92), channel_id=1, source_target_pairs={{0,24},{4,28},{8,0},{12,4},{16,8},{20,12},{24,16},{28,20},{32,56},... | collective-permute-start | bytes 1769480 | tf_op jit(solution)/shard_map/ppermute | solution.py:273
  136.9 39.2 %collective-permute-start.20 = (bf16[24,96,128]{2,1,0:T(8,128)(2,1)}, bf16[24,96,128]{2,1,0:T(8,128)(2,1)S(1)}, u32[]{:S(2)}, u32[]{:S(2)}) collective-permute-start(bf16[24,96,128]{2,1,0:T(8,128)(2,1)} %get-tuple-element.91), channel_id=1, source_target_pairs={{0,32},{4,36},{8,40},{12,44},{16,48},{20,52},{24,56},{28,60},{32,6... | collective-permute-start | bytes 1769480 | tf_op jit(solution)/shard_map/ppermute | solution.py:273
  137.0 39.1 %collective-permute-start.21 = (bf16[24,96,128]{2,1,0:T(8,128)(2,1)}, bf16[24,96,128]{2,1,0:T(8,128)(2,1)}, u32[]{:S(2)}, u32[]{:S(2)}) collective-permute-start(bf16[24,96,128]{2,1,0:T(8,128)(2,1)} %get-tuple-element.90), channel_id=1, source_target_pairs={{0,96},{4,100},{8,104},{12,108},{16,112},{20,116},{24,120},{28,124... | collective-permute-start | bytes 1769480 | tf_op jit(solution)/shard_map/ppermute | solution.py:273
  140.8 35.3 %collective-permute-start.22 = (bf16[24,96,128]{2,1,0:T(8,128)(2,1)}, bf16[24,96,128]{2,1,0:T(8,128)(2,1)S(1)}, u32[]{:S(2)}, u32[]{:S(2)}) collective-permute-start(bf16[24,96,128]{2,1,0:T(8,128)(2,1)} %get-tuple-element.89), channel_id=1, source_target_pairs={{0,8},{4,12},{8,16},{12,20},{16,24},{20,28},{24,0},{28,4},{32,40},... | collective-permute-start | bytes 1769480 | tf_op jit(solution)/shard_map/ppermute | solution.py:273
  141.0 35.1 %collective-permute-start.23 = (bf16[24,96,128]{2,1,0:T(8,128)(2,1)}, bf16[24,96,128]{2,1,0:T(8,128)(2,1)}, u32[]{:S(2)}, u32[]{:S(2)}) collective-permute-start(bf16[24,96,128]{2,1,0:T(8,128)(2,1)} %get-tuple-element.88), channel_id=1, source_target_pairs={{0,24},{4,28},{8,0},{12,4},{16,8},{20,12},{24,16},{28,20},{32,56},... | collective-permute-start | bytes 1769480 | tf_op jit(solution)/shard_map/ppermute | solution.py:273
  168.4 67.5 %collective-permute-start.18 = (bf16[2,32,48,128]{3,2,1,0:T(8,128)(2,1)S(1)}, bf16[2,32,48,128]{3,2,1,0:T(8,128)(2,1)S(1)}, u32[]{:S(2)}, u32[]{:S(2)}) collective-permute-start(bf16[2,32,48,128]{3,2,1,0:T(8,128)(2,1)S(1)} %dynamic-slice_bitcast_fusion.2), channel_id=1, source_target_pairs={{0,1},{1,0},{2,3},{3,2},{4,5},{5,4},{6,7},{7,6},{8,9},{9,8},{10,11... | collective-permute-start | bytes 2359304 | tf_op jit(solution)/shard_map/ppermute | solution.py:336
  179.6 26.0 %collective-permute-start.26 = (bf16[8,96,128]{2,1,0:T(8,128)(2,1)}, bf16[8,96,128]{2,1,0:T(8,128)(2,1)}, u32[]{:S(2)}, u32[]{:S(2)}) collective-permute-start(bf16[8,96,128]{2,1,0:T(8,128)(2,1)} %get-tuple-element.78), channel_id=1, source_target_pairs={{0,32},{4,36},{8,40},{12,44},{16,48},{20,52},{24,56},{28,60},{32,6... | collective-permute-start | bytes 589832 | tf_op jit(solution)/shard_map/ppermute | solution.py:273
  202.6 33.7 %collective-permute-start.24 = (bf16[2,32,48,128]{3,2,1,0:T(8,128)(2,1)S(1)}, bf16[2,32,48,128]{3,2,1,0:T(8,128)(2,1)}, u32[]{:S(2)}, u32[]{:S(2)}) collective-permute-start(bf16[2,32,48,128]{3,2,1,0:T(8,128)(2,1)S(1)} %dynamic-slice_bitcast_fusion.1), channel_id=1, source_target_pairs={{0,1},{1,0},{2,3},{3,2},{4,5},{5,4},{6,7},{7,6},{8,9},{9,8},{10,11... | collective-permute-start | bytes 2359304 | tf_op jit(solution)/shard_map/ppermute | solution.py:336
  202.7 10.8 %collective-permute-start.27 = (bf16[8,96,128]{2,1,0:T(8,128)(2,1)}, bf16[8,96,128]{2,1,0:T(8,128)(2,1)}, u32[]{:S(2)}, u32[]{:S(2)}) collective-permute-start(bf16[8,96,128]{2,1,0:T(8,128)(2,1)} %get-tuple-element.76), channel_id=1, source_target_pairs={{0,96},{4,100},{8,104},{12,108},{16,112},{20,116},{24,120},{28,124... | collective-permute-start | bytes 589832 | tf_op jit(solution)/shard_map/ppermute | solution.py:273
  236.1 12.0 %collective-permute-start.19 = (bf16[32,48,128]{2,1,0:T(8,128)(2,1)S(1)}, bf16[32,48,128]{2,1,0:T(8,128)(2,1)S(1)}, u32[]{:S(2)}, u32[]{:S(2)}) collective-permute-start(bf16[32,48,128]{2,1,0:T(8,128)(2,1)S(1)} %fusion), channel_id=1, source_target_pairs={{0,2},{2,0},{1,3},{3,1},{4,6},{6,4},{5,7},{7,5},{8,10},{10,8},{9,1... | collective-permute-start | bytes 1179656 | tf_op jit(solution)/shard_map/ppermute | solution.py:340
  238.8 17.8 %collective-permute-start.25 = (bf16[32,48,128]{2,1,0:T(8,128)(2,1)S(1)}, bf16[32,48,128]{2,1,0:T(8,128)(2,1)S(1)}, u32[]{:S(2)}, u32[]{:S(2)}) collective-permute-start(bf16[32,48,128]{2,1,0:T(8,128)(2,1)S(1)} %fusion.1), channel_id=1, source_target_pairs={{0,2},{2,0},{1,3},{3,1},{4,6},{6,4},{5,7},{7,5},{8,10},{10,8},{9,1... | collective-permute-start | bytes 1179656 | tf_op jit(solution)/shard_map/ppermute | solution.py:340
  241.0 24.0 %collective-permute-start.31 = (bf16[32,48,128]{2,1,0:T(8,128)(2,1)S(1)}, bf16[32,48,128]{2,1,0:T(8,128)(2,1)S(1)}, u32[]{:S(2)}, u32[]{:S(2)}) collective-permute-start(bf16[32,48,128]{2,1,0:T(8,128)(2,1)S(1)} %fusion.2), channel_id=1, source_target_pairs={{0,2},{2,0},{1,3},{3,1},{4,6},{6,4},{5,7},{7,5},{8,10},{10,8},{9,1... | collective-permute-start | bytes 1179656 | tf_op jit(solution)/shard_map/ppermute | solution.py:340
  (34 other events, 281.2 us)

commit v2 on v1

v2 whole, which is shorter than its diff:
```python
import functools
import math

import jax
import jax.numpy as jnp
import ml_dtypes
import numpy as np
from jax import lax
from jax.experimental import pallas as pl
from jax.experimental.pallas import tpu as pltpu
from jax.sharding import PartitionSpec as P

WINLEN = 1024
HOP = 512
BINS = 128
BIN0 = 16
SMOOTH = 4
LAGS = 101
STEPS = 3
HALF_RANK = 24
RANK = 2 * HALF_RANK
ROW = 136
GROUP = 8
magnitude_eps = 1e-06
water_level = 0.25
VMEM_BYTES = 60 * 1024 * 1024


def dft_table():
    n = np.arange(WINLEN)
    k = BIN0 + np.arange(BINS)
    angles = 2.0 * math.pi / WINLEN * (k[:, None] * n[None, :] % WINLEN)
    taper = 0.5 - 0.5 * np.cos(2.0 * math.pi / WINLEN * n)
    table = np.concatenate([np.cos(angles) * taper, -np.sin(angles) * taper], axis=0)
    return table.astype(np.float32).astype(ml_dtypes.bfloat16)


def band_tables():
    f = np.arange(BINS)
    inside = (np.abs(f[:, None] - f[None, :]) <= SMOOTH).astype(np.float32)
    counts = inside.sum(axis=1)
    return np.tile(inside, (1, 2)).astype(ml_dtypes.bfloat16), (1.0 / counts)[:, None].astype(np.float32)


def dot(a, b):
    return math.fsum(p * q for p, q in zip(a, b))


def row_basis(rows, count):
    left = [list(r) for r in rows]
    basis = []
    for _ in range(count):
        norms = [dot(r, r) for r in left]
        best = max(range(len(left)), key=lambda i: norms[i])
        q = left[best]
        for _ in range(2):
            for b in basis:
                d = dot(q, b)
                q = [x - d * y for x, y in zip(q, b)]
            size = math.sqrt(dot(q, q))
            q = [x / size for x in q]
        basis.append(q)
        for i, r in enumerate(left):
            d = dot(r, q)
            left[i] = [x - d * y for x, y in zip(r, q)]
    return basis


@functools.cache
def lag_factors(windows):
    factor = 1.0 / math.sqrt(BINS * windows)
    mid = LAGS // 2
    bins = range(BIN0, BIN0 + BINS)

    def angle(tau, k):
        return 2.0 * math.pi / WINLEN * (tau * k % WINLEN)

    even = [[math.cos(angle(t, k)) for k in bins] for t in range(mid + 1)]
    odd = [[-math.sin(angle(t, k)) for k in bins] for t in range(1, mid + 1)]
    even_basis = row_basis(even, HALF_RANK)
    odd_basis = row_basis(odd, HALF_RANK)
    even_u = np.array([[dot(r, b) for b in even_basis] for r in even])
    odd_u = np.array([[dot(r, b) for b in odd_basis] for r in odd])
    u = np.zeros((LAGS, RANK))
    for t in range(LAGS):
        tau = t - mid
        u[t, :HALF_RANK] = even_u[abs(tau)]
        if tau:
            u[t, HALF_RANK:] = math.copysign(1.0, tau) * odd_u[abs(tau) - 1]
    return u * factor, np.array(even_basis), np.array(odd_basis)


def split_bf16(value):
    high = value.astype(np.float32).astype(ml_dtypes.bfloat16)
    low = (value - high.astype(np.float64)).astype(np.float32).astype(ml_dtypes.bfloat16)
    return high, low


def bin_order():
    order = []
    for j in range(32):
        x, z, y = j // 8, j // 2 % 4, j % 2
        order += [2 * j, 2 * j + 1]
        order += [64 + 2 * ((z * 4 + x) * 2 + y), 65 + 2 * ((z * 4 + x) * 2 + y)]
    return np.array(order)


def spectra_kernel(chunk, x_ref, next_ref, edge_ref, table_ref, band_ref, inverse_ref, out_ref, rows):
    i = pl.program_id(0)
    tail = jnp.where(i == pl.num_programs(0) - 1, edge_ref[...], next_ref[...])
    pairs = range(chunk // 2)
    spectra, magnitudes, parts = [], [], []
    for pair in pairs:
        frames = []
        for w in (2 * pair, 2 * pair + 1):
            if w == chunk - 1:
                frames.append(jnp.concatenate([x_ref[:, w * HOP :], tail], axis=1))
            else:
                frames.append(x_ref[:, w * HOP : w * HOP + WINLEN])
        spectra.append(
            lax.dot_general(
                table_ref[...],
                jnp.concatenate(frames, axis=0),
                (((1,), (1,)), ((), ())),
                preferred_element_type=jnp.float32,
            )
        )
    for value in spectra:
        re, im = value[:BINS], value[BINS:]
        magnitude = jnp.sqrt(re * re + im * im + magnitude_eps)
        high = magnitude.astype(jnp.bfloat16)
        low = (magnitude - high.astype(jnp.float32)).astype(jnp.bfloat16)
        magnitudes.append(magnitude)
        parts.append(jnp.concatenate([high, low], axis=0))
    totals = [jnp.dot(band_ref[...], p, preferred_element_type=jnp.float32) for p in parts]
    for pair in pairs:
        mean = jnp.sum(magnitudes[pair], axis=0, keepdims=True) * (1.0 / BINS)
        scale = 1.0 / (totals[pair] * inverse_ref[...] + water_level * mean)
        for part in range(2):
            white = spectra[pair][part * BINS : (part + 1) * BINS] * scale
            for h in range(2):
                row = part * chunk + 2 * pair + h
                rows[pl.ds(row, BINS, stride=2 * chunk), :] = white[:, h * 128 : (h + 1) * 128]
    for q, f in enumerate(bin_order()):
        out_ref[q] = rows[2 * chunk * int(f) : 2 * chunk * (int(f) + 1), :].astype(jnp.bfloat16)


def whitened_spectra(samples, edge):
    channels, length = samples.shape
    windows = length // HOP
    band, inverse = band_tables()
    whole = lambda shape: pl.BlockSpec(shape, lambda i: (0,) * len(shape))
    return pl.pallas_call(
        functools.partial(spectra_kernel, GROUP),
        grid=(windows // GROUP,),
        out_shape=jax.ShapeDtypeStruct((BINS, 2 * windows, channels), jnp.bfloat16),
        in_specs=[
            pl.BlockSpec((channels, GROUP * HOP), lambda i: (0, i)),
            pl.BlockSpec((channels, HOP), lambda i: (0, jnp.minimum((i + 1) * GROUP, windows - 1))),
            whole((channels, HOP)),
            whole((2 * BINS, WINLEN)),
            whole((BINS, 2 * BINS)),
            whole((BINS, 1)),
        ],
        out_specs=pl.BlockSpec((BINS, 2 * GROUP, channels), lambda i: (0, i, 0)),
        scratch_shapes=[pltpu.VMEM((BINS * 2 * GROUP, channels), jnp.float32)],
        compiler_params=pltpu.CompilerParams(vmem_limit_bytes=VMEM_BYTES),
        name="spectra",
    )(samples, samples, edge, jnp.asarray(dft_table()), jnp.asarray(band), jnp.asarray(inverse))


def cross_kernel(count, slots_ref, v_ref, own_hbm, *refs):
    pieces = refs[:count]
    keep_ref, send_ref, own_ref, other_ref, real_rows, imag_rows, sems, own_sem = refs[count:]
    size = BINS // count
    own_copy = pltpu.make_async_copy(own_hbm, own_ref, own_sem)
    own_copy.start()
    for i, piece in enumerate(pieces):
        pltpu.make_async_copy(piece, other_ref.at[pl.ds(size * i, size)], sems.at[i]).start()
    own_copy.wait()
    per = 32 // size

    def one(k, carry):
        for i in range(per):
            landed = other_ref.at[pl.ds(size * (k * per + i), size)]
            pltpu.make_async_copy(landed, landed, sems.at[k * per + i]).wait()
        results = []
        for j in range(32):
            n = k * 32 + j
            own = own_ref[slots_ref[n]]
            turned = []
            for r in range(0, own.shape[0], 2 * GROUP):
                turned += [own[r + GROUP : r + 2 * GROUP], -own[r : r + GROUP]]
            results.append(
                lax.dot_general(
                    other_ref[n],
                    jnp.concatenate([own, jnp.concatenate(turned, axis=0)], axis=1),
                    (((0,), (0,)), ((), ())),
                    preferred_element_type=jnp.float32,
                )
            )
        for j, cross in enumerate(results):
            real_rows[pl.ds(k * 32 + j, 128, stride=ROW), :] = cross[:, :128]
            imag_rows[pl.ds(k * 32 + j, 128, stride=ROW), :] = cross[:, 128:]
        return carry

    lax.fori_loop(0, BINS // 32, one, 0)
    core = slots_ref[BINS]
    for out_ref, which in ((send_ref, 1 - core), (keep_ref, core)):

        def two(h, carry, out_ref=out_ref, which=which):
            results = []
            for j in range(16):
                halves = []
                for e in range(2):
                    start = pl.multiple_of((h * 64 + which * 32 + 2 * j + e) * ROW, 8)
                    halves.append(
                        jnp.concatenate(
                            [real_rows[pl.ds(start, 128), :], imag_rows[pl.ds(start, 128), :]], axis=0
                        ).astype(jnp.bfloat16)
                    )
                results.append(
                    jnp.dot(v_ref[...], jnp.concatenate(halves, axis=1), preferred_element_type=jnp.float32)
                )
            for j, both in enumerate(results):
                total = (both[:RANK] + both[RANK:]).astype(out_ref.dtype)
                out_ref[h, 2 * j] = total[:, :128]
                out_ref[h, 2 * j + 1] = total[:, 128:]
            return carry

        lax.fori_loop(0, 2, two, 0)


def lag_coefficients(own, pieces, slots, v):
    vmem = pl.BlockSpec(memory_space=pltpu.VMEM)
    hbm = pl.BlockSpec(memory_space=pl.ANY)
    rows = (2, 32, RANK, 128)
    return pl.pallas_call(
        functools.partial(cross_kernel, len(pieces)),
        out_shape=[jax.ShapeDtypeStruct(rows, jnp.float32), jax.ShapeDtypeStruct(rows, jnp.bfloat16)],
        in_specs=[pl.BlockSpec(memory_space=pltpu.SMEM), vmem] + [hbm] * (1 + len(pieces)),
        out_specs=[vmem, vmem],
        scratch_shapes=[pltpu.VMEM(own.shape, jnp.bfloat16)] * 2
        + [pltpu.VMEM((128 * ROW, 128), jnp.float32)] * 2
        + [pltpu.SemaphoreType.DMA((len(pieces),)), pltpu.SemaphoreType.DMA],
        compiler_params=pltpu.CompilerParams(vmem_limit_bytes=VMEM_BYTES),
        name="cross",
    )(slots, v, own, *pieces)


def expand_kernel(step, u_ref, kept_ref, got_ref, *refs):
    out_ref, lags_ref, sem = refs[-3:]
    count = kept_ref.shape[0]
    results = []
    for n in range(0, count, 2):
        value = jnp.concatenate(
            [kept_ref[b] + got_ref[b].astype(jnp.float32) for b in (n, n + 1)], axis=1
        )
        high = value.astype(jnp.bfloat16)
        low = (value - high.astype(jnp.float32)).astype(jnp.bfloat16)
        results.append(
            jnp.dot(u_ref[...], jnp.concatenate([high, high, low], axis=0), preferred_element_type=jnp.float32)
        )
    for n, lags in enumerate(results):
        lags_ref[pl.ds(2 * n, LAGS, stride=count), :] = lags[:LAGS, :128]
        lags_ref[pl.ds(2 * n + 1, LAGS, stride=count), :] = lags[:LAGS, 128:]
    copy = pltpu.make_async_copy(lags_ref, out_ref.at[step], sem)
    copy.start()
    copy.wait()


def expand(step, u, kept, got, before):
    vmem = pl.BlockSpec(memory_space=pltpu.VMEM)
    hbm = pl.BlockSpec(memory_space=pl.ANY)
    shape = (LAGS * kept.shape[0], 128)
    held = [] if before is None else [before]
    return pl.pallas_call(
        functools.partial(expand_kernel, step),
        out_shape=jax.ShapeDtypeStruct((STEPS,) + shape, jnp.float32),
        in_specs=[vmem] * 3 + [hbm] * len(held),
        out_specs=hbm,
        scratch_shapes=[pltpu.VMEM(shape, jnp.float32), pltpu.SemaphoreType.DMA],
        input_output_aliases={3: 0} if held else {},
        compiler_params=pltpu.CompilerParams(vmem_limit_bytes=VMEM_BYTES),
        name="expand",
    )(u, kept, got, *held)


def place(x, z, y):
    return (x % 4) * 8 + (z % 4) * 2 + y % 2


def shift(value, dx=0, dz=0, dy=0):
    pairs = [(place(x, z, y), place(x + dx, z + dz, y + dy)) for x in range(4) for z in range(4) for y in range(2)]
    return lax.ppermute(value, "chan", pairs)


def around(value, axis):
    return [value] + [shift(value, **{axis: step}) for step in (1, -1, 2)]


def gather_references(parts):
    other = shift(parts, dy=1)
    first = jnp.concatenate([parts[:, :2], other[:, :2]], axis=1)
    second = jnp.concatenate([parts[:, 2:], other[:, 2:]], axis=1)
    plane_a = jnp.concatenate(around(first, "dz"), axis=1)
    plane_b = jnp.concatenate(around(second, "dx"), axis=1)
    return [around(plane_a[s], "dx") + around(plane_b[s], "dz") for s in range(parts.shape[0])]


def slot_table():
    me = lax.axis_index("chan")
    x, z, y = me // 8, me // 2 % 4, me % 2
    offsets = np.array((0, -1, 1, 2))
    last, plane, dy, e = np.meshgrid(offsets, offsets, np.arange(2), np.arange(2), indexing="ij")
    last, plane, dy, e = (t.reshape(-1).astype(np.int32) for t in (last, plane, dy, e))
    y_of = (y + dy) % 2
    first = (((x + last + 4) % 4) * 8 + ((z + plane + 4) % 4) * 2 + y_of) * 4 + e
    second = (((x + plane + 4) % 4) * 8 + ((z + last + 4) % 4) * 2 + y_of) * 4 + 2 + e
    return jnp.concatenate([first, second]).astype(jnp.int32)


def sum_over_spans(keep, send):
    half = lax.axis_index("tm") // 2
    got = lax.ppermute(send, "tm", [(0, 1), (1, 0), (2, 3), (3, 2)])

    def chip(which):
        own = lax.dynamic_index_in_dim(keep, which, 0, keepdims=False)
        return own + lax.dynamic_index_in_dim(got, which, 0, keepdims=False).astype(jnp.float32)

    far = lax.ppermute(chip(1 - half).astype(jnp.bfloat16), "tm", [(0, 2), (2, 0), (1, 3), (3, 1)])
    return chip(half), far


def basis_columns(windows, slots):
    _, even, odd = lag_factors(windows)
    parts = [split_bf16(t[:, bin_order()]) for t in (even, odd)]
    table = np.concatenate([parts[0][0], parts[1][0], parts[0][1], parts[1][1]], axis=0)
    chosen = (jnp.arange(BINS, dtype=jnp.int32)[:, None] == slots[None, :]).astype(jnp.bfloat16)
    table = jnp.dot(jnp.asarray(table), chosen, preferred_element_type=jnp.float32).astype(jnp.bfloat16)
    is_odd = (np.arange(2 * RANK) // HALF_RANK % 2 == 1)[:, None]
    nothing = jnp.zeros_like(table)
    return jnp.concatenate([jnp.where(is_odd, nothing, table), jnp.where(is_odd, table, nothing)], axis=1)


def shards(samples, plan, owner_table):
    windows = samples.shape[1] // HOP * lax.axis_size("tm")
    edge = lax.ppermute(samples[:, :HOP], "tm", [(1, 0), (2, 1), (3, 2)])
    own = whitened_spectra(samples, edge)
    slots = slot_table()
    v = basis_columns(windows, slots)
    slots = jnp.concatenate([slots, (lax.axis_index("tm") % 2).astype(jnp.int32)[None]])
    padded = np.zeros((104, RANK))
    padded[:LAGS] = lag_factors(windows)[0]
    high, low = split_bf16(padded)
    u = jnp.asarray(np.concatenate([high, low, high], axis=1))
    everyone = lax.all_to_all(own.reshape((32, 4) + own.shape[1:]), "chan", 0, 0)
    roots = owner_table[plan]
    parts = jnp.stack([lax.dynamic_index_in_dim(everyone, roots[s], 0, keepdims=False) for s in range(STEPS)])
    out = None
    for s, pieces in enumerate(gather_references(parts)):
        keep, send = lag_coefficients(own, pieces, slots, v)
        out = expand(s, u, *sum_over_spans(keep, send), out)
    return out.reshape(STEPS, LAGS, 32, 128).transpose(2, 0, 1, 3)


def solution(mesh):
    placed = (P("chan", "tm"), P(), P())
    return jax.shard_map(
        shards, mesh=mesh, in_specs=placed, out_specs=P("tm", None, None, "chan"), check_vma=False
    )
```

time: 280 us -> 229 us (0.82)
  Pallas kernels: 87.3 us -> 52.9 us
  local copies, waits for them, and re-layouts: 30.6 us -> 8.29 us
  starting transfers between devices: 57.5 us -> 67.2 us
  waiting for transfers between devices: 87.9 us -> 84 us
  other arithmetic: 9.98 us -> 6.64 us
    pallas_call x5 -> x7, Pallas kernels: 87.3 us -> 52.9 us  [the longest x3 31.1 us: lag_coefficients(): pl.pallas_call(functools.partial(cross_kernel, len(pieces)), out_shape=[j...]
    slice x24 -> x2, local copies, waits for them, and re-layouts: 16.5 us -> 1.57 us  [gather_references(): second = jnp.concatenate([parts[:, 2:], other[:, 2:]], axis=1)]
    ppermute x25, starting transfers between devices: 33.3 us -> 40.9 us  [shift(): return lax.ppermute(value, 'chan', pairs)]
    ppermute x6, waiting for transfers between devices: 21 us -> 13.6 us  [the longest x3 13.6 us: sum_over_spans(): lax.ppermute(chip(1 - half).astype(jnp.bfloat16), 'tm', [(0, 2), (2, 0),...]
    pallas_call x1 -> x0, local copies, waits for them, and re-layouts: 5.58 us -> none  [expand(): pl.pallas_call(expand_kernel, out_shape=jax.ShapeDtypeStruct((coefs[0].sh...]
    add x8 -> x2, other arithmetic: 4.63 us -> 0.04 us  [the longest x1 0.02 us: slot_table(): first = ((x + last + 4) % 4 * 8 + (z + plane + 4) % 4 * 2 + y_of) * 4 + e]
    convert_element_type x0 -> x3, other arithmetic: none -> 4.44 us  [sum_over_spans(): chip(1 - half).astype(jnp.bfloat16)]
    squeeze x5 -> x2, local copies, waits for them, and re-layouts: 3.91 us -> 0.18 us  [the longest x1 0.09 us: gather_references(): plane_a[s]]
  transfers between devices with their start and end apart: 33 -> 33, of which waited for: 14 -> 12; matrix products, arithmetic and copies ran while one was open for 9% -> 4% of each run, Pallas kernels for 21% -> 17%
where the time goes in v2:
time: 229 us; the launch traced here: 226 us
  waiting for transfers between devices  84 us (37%)
  starting transfers between devices  67.2 us (29%)
  Pallas kernels  52.9 us (23%)
  local copies, waits for them, and re-layouts  8.29 us (4%)
  other arithmetic  6.64 us (3%)
  between operations  6.32 us (3%)
    ppermute x25, starting transfers between devices, shift(): return lax.ppermute(value, 'chan', pairs)  40.9 us
    ppermute x25, waiting for transfers between devices, shift(): return lax.ppermute(value, 'chan', pairs)  32.6 us
    all_to_all x1, waiting for transfers between devices, shards(): lax.all_to_all(own.reshape((32, 4) + own.shape[1:]), 'chan', 0, 0)  32.3 us
    pallas_call x3, Pallas kernels, lag_coefficients(): pl.pallas_call(functools.partial(cross_kernel, len(pieces)), out_shape=[j...  31.1 us
    ppermute x3, waiting for transfers between devices, sum_over_spans(): lax.ppermute(chip(1 - half).astype(jnp.bfloat16), 'tm', [(0, 2), (2, 0),...  13.6 us
    pallas_call x1, Pallas kernels, whitened_spectra(): pl.pallas_call(functools.partial(spectra_kernel, GROUP), grid=(windows //...  11 us
    ppermute x3, starting transfers between devices, sum_over_spans(): got = lax.ppermute(send, 'tm', [(0, 1), (1, 0), (2, 3), (3, 2)])  10.9 us
    pallas_call x3, Pallas kernels, expand(): pl.pallas_call(functools.partial(expand_kernel, step), out_shape=jax.Shap...  10.8 us
  transfers between devices with their start and end apart: 33, of which 12 were waited for; matrix products, arithmetic and copies ran while one was open for 4% of the time, Pallas kernels for 17%

profile of v2, /device:TPU:1, one launch (start us, length us, event | category | flops | bytes accessed | tf_op | source)
XLA Modules:
  0.0 226.1 jit_solution(9351027742327481223)
XLA Ops:
  0.9 3.3 %collective-permute-start = (bf16[128,512]{1,0:T(8,128)(2,1)S(1)}, bf16[128,512]{1,0:T(8,128)(2,1)S(1)}, u32[]{:S(2)}, u32[]{:S(2)}) collective-permute-start(bf16[128,512]{1,0:T(8,128)(2,1)S(1)} %slice.42), channel_id=1, source_target_pairs={{1,0},{2,1},{3,2},{5,4},{6,5},{7,6},{9,8},{10,9},{11,10},{13,12},{... | collective-permute-start | bytes 393224 | tf_op jit(solution)/shard_map/ppermute | solution.py:348
  4.3 5.5 %collective-permute-done.edge_ref = bf16[128,512]{1,0:T(8,128)(2,1)S(1)} collective-permute-done((bf16[128,512]{1,0:T(8,128)(2,1)S(1)}, bf16[128,512]{1,0:T(8,128)(2,1)S(1)}, u32[]{:S(2)}, u32[]{:S(2)}) %collective-permute-start) | collective-permute-done | bytes 131104 | tf_op jit(solution)/shard_map/ppermute | solution.py:348
  10.4 11.0 %spectra.1.own_hbm = bf16[128,96,128]{2,1,0:T(8,128)(2,1)} custom-call(bf16[128,24576]{1,0:T(8,128)(2,1)} %next_ref.1, bf16[128,24576]{1,0:T(8,128)(2,1)} %next_ref.1, bf16[128,512]{1,0:T(8,128)(2,1)} %copy-done.25, bf16[256,1024]{1,0:T(8,128)(2,1)} %constant.163.clone.table_ref, bf16[128,256]{1,0:T(8,128)(2,1)} %constant.164.clone.band_ref, ...), custom_call_target="tpu_custom_call" | custom-call | tf_op jit(solution)/shard_map/spectra/pallas_call | solution.py:153
  21.4 8.8 %all-to-all-start = ((bf16[32,4,96,128]{3,2,1,0:T(8,128)(2,1)}), bf16[32,4,96,128]{3,2,1,0:T(8,128)(2,1)S(1)}, u32[]{:S(2)}, u32[]{:S(2)}) async-start(bf16[32,4,96,128]{3,2,1,0:T(8,128)(2,1)} %bitcast.37), calls=%async_computation | async-start | bytes 6291456 | tf_op jit(solution)/shard_map/all_to_all | solution.py:357
  37.2 32.3 %all-to-all-done = bf16[32,4,96,128]{3,2,1,0:T(8,128)(2,1)S(1)} async-done(((bf16[32,4,96,128]{3,2,1,0:T(8,128)(2,1)}), bf16[32,4,96,128]{3,2,1,0:T(8,128)(2,1)S(1)}, u32[]{:S(2)}, u32[]{:S(2)}) %all-to-all-start) | async-done | bytes 3145760 | tf_op jit(solution)/shard_map/all_to_all | solution.py:357
  70.4 6.0 %collective-permute-done.1 = bf16[3,4,96,128]{3,2,1,0:T(8,128)(2,1)S(1)} collective-permute-done((bf16[3,4,96,128]{3,2,1,0:T(8,128)(2,1)S(1)}, bf16[3,4,96,128]{3,2,1,0:T(8,128)(2,1)S(1)}, u32[]{:S(2)}, u32[]{:S(2)}) %collective-permute-start.1) | collective-permute-done | bytes 294944 | tf_op jit(solution)/shard_map/ppermute | solution.py:295
  84.2 3.4 %collective-permute-done.2 = bf16[3,4,96,128]{3,2,1,0:T(8,128)(2,1)S(1)} collective-permute-done((bf16[3,4,96,128]{3,2,1,0:T(8,128)(2,1)S(1)}, bf16[3,4,96,128]{3,2,1,0:T(8,128)(2,1)S(1)}, u32[]{:S(2)}, u32[]{:S(2)}) %collective-permute-start.2) | collective-permute-done | bytes 294944 | tf_op jit(solution)/shard_map/ppermute | solution.py:295
  89.3 3.3 %collective-permute-done.3 = bf16[3,4,96,128]{3,2,1,0:T(8,128)(2,1)S(1)} collective-permute-done((bf16[3,4,96,128]{3,2,1,0:T(8,128)(2,1)S(1)}, bf16[3,4,96,128]{3,2,1,0:T(8,128)(2,1)S(1)}, u32[]{:S(2)}, u32[]{:S(2)}) %collective-permute-start.3) | collective-permute-done | bytes 294944 | tf_op jit(solution)/shard_map/ppermute | solution.py:295
  93.0 3.2 %collective-permute-start.5 = (bf16[16,96,128]{2,1,0:T(8,128)(2,1)S(1)}, bf16[16,96,128]{2,1,0:T(8,128)(2,1)S(1)}, u32[]{:S(2)}, u32[]{:S(2)}) collective-permute-start(bf16[16,96,128]{2,1,0:T(8,128)(2,1)S(1)} %get-tuple-element.33.refs_0_), channel_id=1, source_target_pairs={{0,32},{4,36},{8,40},{12,44},{16,48},{20,52},{24,56},{28,60},{32,6... | collective-permute-start | bytes 1179656 | tf_op jit(solution)/shard_map/ppermute | solution.py:295
  100.1 6.9 %collective-permute-done.5.refs_1_ = bf16[16,96,128]{2,1,0:T(8,128)(2,1)S(1)} collective-permute-done((bf16[16,96,128]{2,1,0:T(8,128)(2,1)S(1)}, bf16[16,96,128]{2,1,0:T(8,128)(2,1)S(1)}, u32[]{:S(2)}, u32[]{:S(2)}) %collective-permute-start.5) | collective-permute-done | bytes 393248 | tf_op jit(solution)/shard_map/ppermute | solution.py:295
  110.0 6.7 %collective-permute-done.16.refs_1_ = bf16[16,96,128]{2,1,0:T(8,128)(2,1)S(1)} collective-permute-done((bf16[16,96,128]{2,1,0:T(8,128)(2,1)S(1)}, bf16[16,96,128]{2,1,0:T(8,128)(2,1)S(1)}, u32[]{:S(2)}, u32[]{:S(2)}) %collective-permute-start.16) | collective-permute-done | bytes 393248 | tf_op jit(solution)/shard_map/ppermute | solution.py:295
  116.6 5.6 %collective-permute-start.21 = (bf16[16,96,128]{2,1,0:T(8,128)(2,1)S(1)}, bf16[16,96,128]{2,1,0:T(8,128)(2,1)S(1)}, u32[]{:S(2)}, u32[]{:S(2)}) collective-permute-start(bf16[16,96,128]{2,1,0:T(8,128)(2,1)S(1)} %get-tuple-element.29.refs_4_), channel_id=1, source_target_pairs={{0,16},{4,20},{8,24},{12,28},{16,0},{20,4},{24,8},{28,12},{32,48},... | collective-permute-start | bytes 1179656 | tf_op jit(solution)/shard_map/ppermute | solution.py:295
  126.5 4.5 %collective-permute-done.21.refs_7_ = bf16[16,96,128]{2,1,0:T(8,128)(2,1)S(1)} collective-permute-done((bf16[16,96,128]{2,1,0:T(8,128)(2,1)S(1)}, bf16[16,96,128]{2,1,0:T(8,128)(2,1)S(1)}, u32[]{:S(2)}, u32[]{:S(2)}) %collective-permute-start.21) | collective-permute-done | bytes 393248 | tf_op jit(solution)/shard_map/ppermute | solution.py:295
  133.1 3.4 %collective-permute-start.7 = (bf16[16,96,128]{2,1,0:T(8,128)(2,1)S(1)}, bf16[16,96,128]{2,1,0:T(8,128)(2,1)}, u32[]{:S(2)}, u32[]{:S(2)}) collective-permute-start(bf16[16,96,128]{2,1,0:T(8,128)(2,1)S(1)} %get-tuple-element.33.refs_0_), channel_id=1, source_target_pairs={{0,64},{4,68},{8,72},{12,76},{16,80},{20,84},{24,88},{28,92},{32,9... | collective-permute-start | bytes 1179656 | tf_op jit(solution)/shard_map/ppermute | solution.py:295
  136.5 4.1 %collective-permute-start.29 = (bf16[16,96,128]{2,1,0:T(8,128)(2,1)S(1)}, bf16[16,96,128]{2,1,0:T(8,128)(2,1)}, u32[]{:S(2)}, u32[]{:S(2)}) collective-permute-start(bf16[16,96,128]{2,1,0:T(8,128)(2,1)S(1)} %get-tuple-element.28.refs_4_), channel_id=1, source_target_pairs={{0,16},{4,20},{8,24},{12,28},{16,0},{20,4},{24,8},{28,12},{32,48},... | collective-permute-start | bytes 1179656 | tf_op jit(solution)/shard_map/ppermute | solution.py:295
  142.8 3.1 %collective-permute-start.11 = (bf16[16,96,128]{2,1,0:T(8,128)(2,1)S(1)}, bf16[16,96,128]{2,1,0:T(8,128)(2,1)S(1)}, u32[]{:S(2)}, u32[]{:S(2)}) collective-permute-start(bf16[16,96,128]{2,1,0:T(8,128)(2,1)S(1)} %get-tuple-element.30.refs_4_), channel_id=1, source_target_pairs={{0,8},{4,12},{8,16},{12,20},{16,24},{20,28},{24,0},{28,4},{32,40},... | collective-permute-start | bytes 1179656 | tf_op jit(solution)/shard_map/ppermute | solution.py:295
  148.4 10.4 %cross.4 = (f32[2,32,48,128]{3,2,1,0:T(8,128)}, bf16[2,32,48,128]{3,2,1,0:T(8,128)(2,1)}) custom-call(s32[129]{0:T(256)} %pad_add_fusion.slots_ref, bf16[96,256]{1,0:T(8,128)(2,1)} %pad_maximum_fusion.3.v_ref, bf16[128,96,128]{2,1,0:T(8,128)(2,1)} %spectra.1.own_hbm, bf16[16,96,128]{2,1,0:T(8,128)(2,1)} %copy-done.7, bf16[16,96,128]{2,1,0:T(8,128)(2,1)} %copy-done.15, ...), custom_call_target="tpu_custom_call" | custom-call | tf_op jit(solution)/shard_map/cross/pallas_call | solution.py:238
  158.8 10.2 %collective-permute-start.22 = (bf16[2,32,48,128]{3,2,1,0:T(8,128)(2,1)}, bf16[2,32,48,128]{3,2,1,0:T(8,128)(2,1)S(1)}, u32[]{:S(2)}, u32[]{:S(2)}) collective-permute-start(bf16[2,32,48,128]{3,2,1,0:T(8,128)(2,1)} %get-tuple-element.14), channel_id=1, source_target_pairs={{0,1},{1,0},{2,3},{3,2},{4,5},{5,4},{6,7},{7,6},{8,9},{9,8},{10,11... | collective-permute-start | bytes 2359304 | tf_op jit(solution)/shard_map/ppermute | solution.py:325
  169.0 10.4 %cross.5 = (f32[2,32,48,128]{3,2,1,0:T(8,128)}, bf16[2,32,48,128]{3,2,1,0:T(8,128)(2,1)}) custom-call(s32[129]{0:T(256)} %pad_add_fusion.slots_ref, bf16[96,256]{1,0:T(8,128)(2,1)} %pad_maximum_fusion.3.v_ref, bf16[128,96,128]{2,1,0:T(8,128)(2,1)} %spectra.1.own_hbm, bf16[16,96,128]{2,1,0:T(8,128)(2,1)} %copy-done.5, bf16[16,96,128]{2,1,0:T(8,128)(2,1)} %copy-done.20, ...), custom_call_target="tpu_custom_call" | custom-call | tf_op jit(solution)/shard_map/cross/pallas_call | solution.py:238
  180.2 10.4 %cross.3 = (f32[2,32,48,128]{3,2,1,0:T(8,128)}, bf16[2,32,48,128]{3,2,1,0:T(8,128)(2,1)}) custom-call(s32[129]{0:T(256)} %pad_add_fusion.slots_ref, bf16[96,256]{1,0:T(8,128)(2,1)} %pad_maximum_fusion.3.v_ref, bf16[128,96,128]{2,1,0:T(8,128)(2,1)} %spectra.1.own_hbm, bf16[16,96,128]{2,1,0:T(8,128)(2,1)} %copy-done.4, bf16[16,96,128]{2,1,0:T(8,128)(2,1)} %copy-done.13, ...), custom_call_target="tpu_custom_call" | custom-call | tf_op jit(solution)/shard_map/cross/pallas_call | solution.py:238
  199.2 13.6 %collective-permute-done.31.got_ref = bf16[32,48,128]{2,1,0:T(8,128)(2,1)S(1)} collective-permute-done((bf16[32,48,128]{2,1,0:T(8,128)(2,1)S(1)}, bf16[32,48,128]{2,1,0:T(8,128)(2,1)S(1)}, u32[]{:S(2)}, u32[]{:S(2)}) %collective-permute-start.31) | collective-permute-done | bytes 393248 | tf_op jit(solution)/shard_map/ppermute | solution.py:331
  213.6 3.6 %expand.3.refs_0_ = f32[3,3232,128]{2,1,0:T(8,128)} custom-call(bf16[104,144]{1,0:T(8,128)(2,1)} %constant.172.clone.u_ref, f32[32,48,128]{2,1,0:T(8,128)} %get-tuple-element.23.kept_ref, bf16[32,48,128]{2,1,0:T(8,128)(2,1)} %copy-done.24), custom_call_target="tpu_custom_call" | custom-call | tf_op jit(solution)/shard_map/expand/pallas_call | solution.py:277
  218.0 3.6 %expand.4.refs_0_ = f32[3,3232,128]{2,1,0:T(8,128)} custom-call(bf16[104,144]{1,0:T(8,128)(2,1)} %constant.172.clone.u_ref, f32[32,48,128]{2,1,0:T(8,128)} %get-tuple-element.25.kept_ref, bf16[32,48,128]{2,1,0:T(8,128)(2,1)} %copy-done.11, f32[3,3232,128]{2,1,0:T(8,128)} %expand.3.refs_0_), custom_call_target="tpu_custom_call", output_to_operand_aliasing={{}: (3, {})} | custom-call | tf_op jit(solution)/shard_map/expand/pallas_call | solution.py:277
  222.3 3.6 %expand.5 = f32[3,3232,128]{2,1,0:T(8,128)} custom-call(bf16[104,144]{1,0:T(8,128)(2,1)} %constant.172.clone.u_ref, f32[32,48,128]{2,1,0:T(8,128)} %get-tuple-element.27.kept_ref, bf16[32,48,128]{2,1,0:T(8,128)(2,1)} %copy-done.12, f32[3,3232,128]{2,1,0:T(8,128)} %expand.4.refs_0_), custom_call_target="tpu_custom_call", output_to_operand_aliasing={{}: (3, {})} | custom-call | tf_op jit(solution)/shard_map/expand/pallas_call | solution.py:277
  (143 shorter events, 43.0 us)
Async XLA Ops:
  21.4 48.1 %all-to-all-start = ((bf16[32,4,96,128]{3,2,1,0:T(8,128)(2,1)}), bf16[32,4,96,128]{3,2,1,0:T(8,128)(2,1)S(1)}, u32[]{:S(2)}, u32[]{:S(2)}) async-start(bf16[32,4,96,128]{3,2,1,0:T(8,128)(2,1)} %bitcast.37), calls=%async_computation | async-start | bytes 6291456 | tf_op jit(solution)/shard_map/all_to_all | solution.py:357
  77.4 15.2 %collective-permute-start.3 = (bf16[3,4,96,128]{3,2,1,0:T(8,128)(2,1)S(1)}, bf16[3,4,96,128]{3,2,1,0:T(8,128)(2,1)S(1)}, u32[]{:S(2)}, u32[]{:S(2)}) collective-permute-start(bf16[3,4,96,128]{3,2,1,0:T(8,128)(2,1)S(1)} %pad_maximum_fusion.1), channel_id=1, source_target_pairs={{0,24},{4,28},{8,0},{12,4},{16,8},{20,12},{24,16},{28,20},{32,56},... | collective-permute-start | bytes 884744 | tf_op jit(solution)/shard_map/ppermute | solution.py:295
  80.5 15.7 %collective-permute-start.8 = (bf16[3,4,96,128]{3,2,1,0:T(8,128)(2,1)S(1)}, bf16[3,4,96,128]{3,2,1,0:T(8,128)(2,1)S(1)}, u32[]{:S(2)}, u32[]{:S(2)}) collective-permute-start(bf16[3,4,96,128]{3,2,1,0:T(8,128)(2,1)S(1)} %pad_maximum_fusion.2), channel_id=1, source_target_pairs={{0,32},{4,36},{8,40},{12,44},{16,48},{20,52},{24,56},{28,60},{32,6... | collective-permute-start | bytes 884744 | tf_op jit(solution)/shard_map/ppermute | solution.py:295
  83.0 14.7 %collective-permute-start.9 = (bf16[3,4,96,128]{3,2,1,0:T(8,128)(2,1)S(1)}, bf16[3,4,96,128]{3,2,1,0:T(8,128)(2,1)S(1)}, u32[]{:S(2)}, u32[]{:S(2)}) collective-permute-start(bf16[3,4,96,128]{3,2,1,0:T(8,128)(2,1)S(1)} %pad_maximum_fusion.2), channel_id=1, source_target_pairs={{0,96},{4,100},{8,104},{12,108},{16,112},{20,116},{24,120},{28,124... | collective-permute-start | bytes 884744 | tf_op jit(solution)/shard_map/ppermute | solution.py:295
  93.0 14.0 %collective-permute-start.5 = (bf16[16,96,128]{2,1,0:T(8,128)(2,1)S(1)}, bf16[16,96,128]{2,1,0:T(8,128)(2,1)S(1)}, u32[]{:S(2)}, u32[]{:S(2)}) collective-permute-start(bf16[16,96,128]{2,1,0:T(8,128)(2,1)S(1)} %get-tuple-element.33.refs_0_), channel_id=1, source_target_pairs={{0,32},{4,36},{8,40},{12,44},{16,48},{20,52},{24,56},{28,60},{32,6... | collective-permute-start | bytes 1179656 | tf_op jit(solution)/shard_map/ppermute | solution.py:295
  96.2 20.4 %collective-permute-start.16 = (bf16[16,96,128]{2,1,0:T(8,128)(2,1)S(1)}, bf16[16,96,128]{2,1,0:T(8,128)(2,1)S(1)}, u32[]{:S(2)}, u32[]{:S(2)}) collective-permute-start(bf16[16,96,128]{2,1,0:T(8,128)(2,1)S(1)} %get-tuple-element.32.refs_0_), channel_id=1, source_target_pairs={{0,32},{4,36},{8,40},{12,44},{16,48},{20,52},{24,56},{28,60},{32,6... | collective-permute-start | bytes 1179656 | tf_op jit(solution)/shard_map/ppermute | solution.py:295
  97.7 24.5 %collective-permute-start.17 = (bf16[16,96,128]{2,1,0:T(8,128)(2,1)S(1)}, bf16[16,96,128]{2,1,0:T(8,128)(2,1)S(1)}, u32[]{:S(2)}, u32[]{:S(2)}) collective-permute-start(bf16[16,96,128]{2,1,0:T(8,128)(2,1)S(1)} %get-tuple-element.32.refs_0_), channel_id=1, source_target_pairs={{0,96},{4,100},{8,104},{12,108},{16,112},{20,116},{24,120},{28,124... | collective-permute-start | bytes 1179656 | tf_op jit(solution)/shard_map/ppermute | solution.py:295
  99.0 23.6 %collective-permute-start.18 = (bf16[16,96,128]{2,1,0:T(8,128)(2,1)S(1)}, bf16[16,96,128]{2,1,0:T(8,128)(2,1)S(1)}, u32[]{:S(2)}, u32[]{:S(2)}) collective-permute-start(bf16[16,96,128]{2,1,0:T(8,128)(2,1)S(1)} %get-tuple-element.32.refs_0_), channel_id=1, source_target_pairs={{0,64},{4,68},{8,72},{12,76},{16,80},{20,84},{24,88},{28,92},{32,9... | collective-permute-start | bytes 1179656 | tf_op jit(solution)/shard_map/ppermute | solution.py:295
  107.0 18.0 %collective-permute-start.19 = (bf16[16,96,128]{2,1,0:T(8,128)(2,1)S(1)}, bf16[16,96,128]{2,1,0:T(8,128)(2,1)S(1)}, u32[]{:S(2)}, u32[]{:S(2)}) collective-permute-start(bf16[16,96,128]{2,1,0:T(8,128)(2,1)S(1)} %get-tuple-element.29.refs_4_), channel_id=1, source_target_pairs={{0,8},{4,12},{8,16},{12,20},{16,24},{20,28},{24,0},{28,4},{32,40},... | collective-permute-start | bytes 1179656 | tf_op jit(solution)/shard_map/ppermute | solution.py:295
  110.0 16.5 %collective-permute-start.20 = (bf16[16,96,128]{2,1,0:T(8,128)(2,1)S(1)}, bf16[16,96,128]{2,1,0:T(8,128)(2,1)S(1)}, u32[]{:S(2)}, u32[]{:S(2)}) collective-permute-start(bf16[16,96,128]{2,1,0:T(8,128)(2,1)S(1)} %get-tuple-element.29.refs_4_), channel_id=1, source_target_pairs={{0,24},{4,28},{8,0},{12,4},{16,8},{20,12},{24,16},{28,20},{32,56},... | collective-permute-start | bytes 1179656 | tf_op jit(solution)/shard_map/ppermute | solution.py:295
  116.6 14.4 %collective-permute-start.21 = (bf16[16,96,128]{2,1,0:T(8,128)(2,1)S(1)}, bf16[16,96,128]{2,1,0:T(8,128)(2,1)S(1)}, u32[]{:S(2)}, u32[]{:S(2)}) collective-permute-start(bf16[16,96,128]{2,1,0:T(8,128)(2,1)S(1)} %get-tuple-element.29.refs_4_), channel_id=1, source_target_pairs={{0,16},{4,20},{8,24},{12,28},{16,0},{20,4},{24,8},{28,12},{32,48},... | collective-permute-start | bytes 1179656 | tf_op jit(solution)/shard_map/ppermute | solution.py:295
  122.6 13.9 %collective-permute-start.25 = (bf16[16,96,128]{2,1,0:T(8,128)(2,1)S(1)}, bf16[16,96,128]{2,1,0:T(8,128)(2,1)S(1)}, u32[]{:S(2)}, u32[]{:S(2)}) collective-permute-start(bf16[16,96,128]{2,1,0:T(8,128)(2,1)S(1)} %get-tuple-element.31.refs_0_), channel_id=1, source_target_pairs={{0,96},{4,100},{8,104},{12,108},{16,112},{20,116},{24,120},{28,124... | collective-permute-start | bytes 1179656 | tf_op jit(solution)/shard_map/ppermute | solution.py:295
  125.0 17.8 %collective-permute-start.26 = (bf16[16,96,128]{2,1,0:T(8,128)(2,1)S(1)}, bf16[16,96,128]{2,1,0:T(8,128)(2,1)}, u32[]{:S(2)}, u32[]{:S(2)}) collective-permute-start(bf16[16,96,128]{2,1,0:T(8,128)(2,1)S(1)} %get-tuple-element.31.refs_0_), channel_id=1, source_target_pairs={{0,64},{4,68},{8,72},{12,76},{16,80},{20,84},{24,88},{28,92},{32,9... | collective-permute-start | bytes 1179656 | tf_op jit(solution)/shard_map/ppermute | solution.py:295
  126.5 19.4 %collective-permute-start.27 = (bf16[16,96,128]{2,1,0:T(8,128)(2,1)S(1)}, bf16[16,96,128]{2,1,0:T(8,128)(2,1)}, u32[]{:S(2)}, u32[]{:S(2)}) collective-permute-start(bf16[16,96,128]{2,1,0:T(8,128)(2,1)S(1)} %get-tuple-element.28.refs_4_), channel_id=1, source_target_pairs={{0,8},{4,12},{8,16},{12,20},{16,24},{20,28},{24,0},{28,4},{32,40},... | collective-permute-start | bytes 1179656 | tf_op jit(solution)/shard_map/ppermute | solution.py:295
  131.0 15.0 %collective-permute-start.28 = (bf16[16,96,128]{2,1,0:T(8,128)(2,1)S(1)}, bf16[16,96,128]{2,1,0:T(8,128)(2,1)}, u32[]{:S(2)}, u32[]{:S(2)}) collective-permute-start(bf16[16,96,128]{2,1,0:T(8,128)(2,1)S(1)} %get-tuple-element.28.refs_4_), channel_id=1, source_target_pairs={{0,24},{4,28},{8,0},{12,4},{16,8},{20,12},{24,16},{28,20},{32,56},... | collective-permute-start | bytes 1179656 | tf_op jit(solution)/shard_map/ppermute | solution.py:295
  133.1 46.2 %collective-permute-start.7 = (bf16[16,96,128]{2,1,0:T(8,128)(2,1)S(1)}, bf16[16,96,128]{2,1,0:T(8,128)(2,1)}, u32[]{:S(2)}, u32[]{:S(2)}) collective-permute-start(bf16[16,96,128]{2,1,0:T(8,128)(2,1)S(1)} %get-tuple-element.33.refs_0_), channel_id=1, source_target_pairs={{0,64},{4,68},{8,72},{12,76},{16,80},{20,84},{24,88},{28,92},{32,9... | collective-permute-start | bytes 1179656 | tf_op jit(solution)/shard_map/ppermute | solution.py:295
  136.5 22.3 %collective-permute-start.29 = (bf16[16,96,128]{2,1,0:T(8,128)(2,1)S(1)}, bf16[16,96,128]{2,1,0:T(8,128)(2,1)}, u32[]{:S(2)}, u32[]{:S(2)}) collective-permute-start(bf16[16,96,128]{2,1,0:T(8,128)(2,1)S(1)} %get-tuple-element.28.refs_4_), channel_id=1, source_target_pairs={{0,16},{4,20},{8,24},{12,28},{16,0},{20,4},{24,8},{28,12},{32,48},... | collective-permute-start | bytes 1179656 | tf_op jit(solution)/shard_map/ppermute | solution.py:295
  142.8 36.7 %collective-permute-start.11 = (bf16[16,96,128]{2,1,0:T(8,128)(2,1)S(1)}, bf16[16,96,128]{2,1,0:T(8,128)(2,1)S(1)}, u32[]{:S(2)}, u32[]{:S(2)}) collective-permute-start(bf16[16,96,128]{2,1,0:T(8,128)(2,1)S(1)} %get-tuple-element.30.refs_4_), channel_id=1, source_target_pairs={{0,8},{4,12},{8,16},{12,20},{16,24},{20,28},{24,0},{28,4},{32,40},... | collective-permute-start | bytes 1179656 | tf_op jit(solution)/shard_map/ppermute | solution.py:295
  145.9 33.6 %collective-permute-start.12 = (bf16[16,96,128]{2,1,0:T(8,128)(2,1)S(1)}, bf16[16,96,128]{2,1,0:T(8,128)(2,1)}, u32[]{:S(2)}, u32[]{:S(2)}) collective-permute-start(bf16[16,96,128]{2,1,0:T(8,128)(2,1)S(1)} %get-tuple-element.30.refs_4_), channel_id=1, source_target_pairs={{0,24},{4,28},{8,0},{12,4},{16,8},{20,12},{24,16},{28,20},{32,56},... | collective-permute-start | bytes 1179656 | tf_op jit(solution)/shard_map/ppermute | solution.py:295
  146.0 33.5 %collective-permute-start.13 = (bf16[16,96,128]{2,1,0:T(8,128)(2,1)S(1)}, bf16[16,96,128]{2,1,0:T(8,128)(2,1)}, u32[]{:S(2)}, u32[]{:S(2)}) collective-permute-start(bf16[16,96,128]{2,1,0:T(8,128)(2,1)S(1)} %get-tuple-element.30.refs_4_), channel_id=1, source_target_pairs={{0,16},{4,20},{8,24},{12,28},{16,0},{20,4},{24,8},{28,12},{32,48},... | collective-permute-start | bytes 1179656 | tf_op jit(solution)/shard_map/ppermute | solution.py:295
  158.8 32.4 %collective-permute-start.22 = (bf16[2,32,48,128]{3,2,1,0:T(8,128)(2,1)}, bf16[2,32,48,128]{3,2,1,0:T(8,128)(2,1)S(1)}, u32[]{:S(2)}, u32[]{:S(2)}) collective-permute-start(bf16[2,32,48,128]{3,2,1,0:T(8,128)(2,1)} %get-tuple-element.14), channel_id=1, source_target_pairs={{0,1},{1,0},{2,3},{3,2},{4,5},{5,4},{6,7},{7,6},{8,9},{9,8},{10,11... | collective-permute-start | bytes 2359304 | tf_op jit(solution)/shard_map/ppermute | solution.py:325
  192.2 25.0 %collective-permute-start.23 = (bf16[32,48,128]{2,1,0:T(8,128)(2,1)S(1)}, bf16[32,48,128]{2,1,0:T(8,128)(2,1)S(1)}, u32[]{:S(2)}, u32[]{:S(2)}) collective-permute-start(bf16[32,48,128]{2,1,0:T(8,128)(2,1)S(1)} %get-tuple-element.24), channel_id=1, source_target_pairs={{0,2},{2,0},{1,3},{3,1},{4,6},{6,4},{5,7},{7,5},{8,10},{10,8},{9,1... | collective-permute-start | bytes 1179656 | tf_op jit(solution)/shard_map/ppermute | solution.py:331
  195.1 17.7 %collective-permute-start.31 = (bf16[32,48,128]{2,1,0:T(8,128)(2,1)S(1)}, bf16[32,48,128]{2,1,0:T(8,128)(2,1)S(1)}, u32[]{:S(2)}, u32[]{:S(2)}) collective-permute-start(bf16[32,48,128]{2,1,0:T(8,128)(2,1)S(1)} %get-tuple-element.22), channel_id=1, source_target_pairs={{0,2},{2,0},{1,3},{3,1},{4,6},{6,4},{5,7},{7,5},{8,10},{10,8},{9,1... | collective-permute-start | bytes 1179656 | tf_op jit(solution)/shard_map/ppermute | solution.py:331
  198.6 23.0 %collective-permute-start.15 = (bf16[32,48,128]{2,1,0:T(8,128)(2,1)S(1)}, bf16[32,48,128]{2,1,0:T(8,128)(2,1)S(1)}, u32[]{:S(2)}, u32[]{:S(2)}) collective-permute-start(bf16[32,48,128]{2,1,0:T(8,128)(2,1)S(1)} %get-tuple-element.26), channel_id=1, source_target_pairs={{0,2},{2,0},{1,3},{3,1},{4,6},{6,4},{5,7},{7,5},{8,10},{10,8},{9,1... | collective-permute-start | bytes 1179656 | tf_op jit(solution)/shard_map/ppermute | solution.py:331
  (42 other events, 820.7 us)

commit v3 on v2

--- a/solution.py
+++ b/solution.py
@@ -19,7 +19,6 @@
 STEPS = 3
 HALF_RANK = 24
 RANK = 2 * HALF_RANK
-ROW = 136
 GROUP = 8
 magnitude_eps = 1e-06
 water_level = 0.25
@@ -169,93 +168,154 @@
     )(samples, samples, edge, jnp.asarray(dft_table()), jnp.asarray(band), jnp.asarray(inverse))
 
 
-def cross_kernel(count, slots_ref, v_ref, own_hbm, *refs):
-    pieces = refs[:count]
-    keep_ref, send_ref, own_ref, other_ref, real_rows, imag_rows, sems, own_sem = refs[count:]
-    size = BINS // count
-    own_copy = pltpu.make_async_copy(own_hbm, own_ref, own_sem)
-    own_copy.start()
-    for i, piece in enumerate(pieces):
-        pltpu.make_async_copy(piece, other_ref.at[pl.ds(size * i, size)], sems.at[i]).start()
-    own_copy.wait()
-    per = 32 // size
-
-    def one(k, carry):
-        for i in range(per):
-            landed = other_ref.at[pl.ds(size * (k * per + i), size)]
-            pltpu.make_async_copy(landed, landed, sems.at[k * per + i]).wait()
-        results = []
-        for j in range(32):
-            n = k * 32 + j
-            own = own_ref[slots_ref[n]]
-            turned = []
-            for r in range(0, own.shape[0], 2 * GROUP):
-                turned += [own[r + GROUP : r + 2 * GROUP], -own[r : r + GROUP]]
-            results.append(
-                lax.dot_general(
-                    other_ref[n],
+def add_cross(spans, pieces, slots, base, row, real_rows, imag_rows):
+    results = []
+    for piece, size in pieces:
+        for j in range(size):
+            slot = slots[base + len(results)]
+            width = piece.shape[3] // len(spans)
+            total = None
+            for n, span in enumerate(spans):
+                own = span[slot]
+                turned = []
+                for r in range(0, own.shape[0], 2 * GROUP):
+                    turned += [own[r + GROUP : r + 2 * GROUP], -own[r : r + GROUP]]
+                cross = lax.dot_general(
+                    piece[0, j][:, n * width : (n + 1) * width],
                     jnp.concatenate([own, jnp.concatenate(turned, axis=0)], axis=1),
                     (((0,), (0,)), ((), ())),
                     preferred_element_type=jnp.float32,
                 )
+                total = cross if total is None else total + cross
+            results.append(total)
+    for j, cross in enumerate(results):
+        real_rows[pl.ds(base + j, cross.shape[0], stride=row), :] = cross[:, :128]
+        imag_rows[pl.ds(base + j, cross.shape[0], stride=row), :] = cross[:, 128:]
+
+
+def coefficients(v_ref, real_rows, imag_rows, row, bins, channels):
+    results = []
+    for n in range(0, len(channels), 2):
+        halves = []
+        for b in channels[n : n + 2]:
+            start = pl.multiple_of(b * row, 8)
+            halves.append(
+                jnp.concatenate(
+                    [real_rows[pl.ds(start, bins), :], imag_rows[pl.ds(start, bins), :]], axis=0
+                ).astype(jnp.bfloat16)
             )
-        for j, cross in enumerate(results):
-            real_rows[pl.ds(k * 32 + j, 128, stride=ROW), :] = cross[:, :128]
-            imag_rows[pl.ds(k * 32 + j, 128, stride=ROW), :] = cross[:, 128:]
+        results.append(jnp.dot(v_ref[...], jnp.concatenate(halves, axis=1), preferred_element_type=jnp.float32))
+    totals = []
+    for both in results:
+        total = both[:RANK] + both[RANK:]
+        totals += [total[:, :128], total[:, 128:]]
+    return totals
+
+
+def near_kernel(count, slots_ref, v_ref, own_ref, next_ref, *refs):
+    pieces, (out_ref, real_rows, imag_rows) = refs[:count], refs[count:]
+    size = pieces[0].shape[1]
+    bins = count * size
+    row = bins + 8
+    for n in range(0, count, 2):
+        chosen = [(p, size) for p in pieces[n : n + 2]]
+        add_cross((own_ref, next_ref), chosen, slots_ref, n * size, row, real_rows, imag_rows)
+
+    def some(n, carry):
+        channels = [n * 32 + j for j in range(32)]
+        totals = coefficients(v_ref, real_rows, imag_rows, row, bins, channels)
+        for b, total in zip(channels, totals):
+            out_ref[0, b] = total
         return carry
 
-    lax.fori_loop(0, BINS // 32, one, 0)
-    core = slots_ref[BINS]
+    lax.fori_loop(0, 2, some, 0)
+
+
+def far_kernel(step, count, slots_ref, v_ref, own_hbm, next_hbm, near_hbm, *refs):
+    pieces = refs[:count]
+    keep_ref, send_ref, own_ref, next_ref, near_ref, other_ref, real_rows, imag_rows, own_sems, near_sem, sems = refs[
+        count:
+    ]
+    size = pieces[0].shape[1]
+    bins = count * size
+    row = bins + 8
+    copies = [
+        pltpu.make_async_copy(p.at[step], other_ref.at[0, pl.ds(size * i, size)], sems.at[i])
+        for i, p in enumerate(pieces)
+    ]
+    for n, (source, target) in enumerate(((own_hbm, own_ref), (next_hbm, next_ref))):
+        copies += [
+            pltpu.make_async_copy(source.at[slots_ref[j]], target.at[j], own_sems.at[n * bins + j])
+            for j in range(bins)
+        ]
+    near_copy = pltpu.make_async_copy(near_hbm.at[step], near_ref, near_sem)
+    for copy in copies + [near_copy]:
+        copy.start()
+    for copy in copies:
+        copy.wait()
+    add_cross((own_ref, next_ref), [(other_ref, bins)], range(bins), 0, row, real_rows, imag_rows)
+    near_copy.wait()
+    core = slots_ref[bins]
     for out_ref, which in ((send_ref, 1 - core), (keep_ref, core)):
-
-        def two(h, carry, out_ref=out_ref, which=which):
-            results = []
-            for j in range(16):
-                halves = []
-                for e in range(2):
-                    start = pl.multiple_of((h * 64 + which * 32 + 2 * j + e) * ROW, 8)
-                    halves.append(
-                        jnp.concatenate(
-                            [real_rows[pl.ds(start, 128), :], imag_rows[pl.ds(start, 128), :]], axis=0
-                        ).astype(jnp.bfloat16)
-                    )
-                results.append(
-                    jnp.dot(v_ref[...], jnp.concatenate(halves, axis=1), preferred_element_type=jnp.float32)
-                )
-            for j, both in enumerate(results):
-                total = (both[:RANK] + both[RANK:]).astype(out_ref.dtype)
-                out_ref[h, 2 * j] = total[:, :128]
-                out_ref[h, 2 * j + 1] = total[:, 128:]
-            return carry
-
-        lax.fori_loop(0, 2, two, 0)
-
-
-def lag_coefficients(own, pieces, slots, v):
+        channels = [which * 32 + j for j in range(32)]
+        totals = coefficients(v_ref, real_rows, imag_rows, row, bins, channels)
+        for j, total in enumerate(totals):
+            out_ref[j] = (near_ref[channels[j]] + total).astype(out_ref.dtype)
+
+
+def step_block(shape):
+    return pl.BlockSpec((1,) + shape, lambda s: (s,) + (0,) * len(shape))
+
+
+def near_coefficients(own, across, pieces, slots, v):
+    bins = sum(p.shape[1] for p in pieces)
+    whole = lambda a: pl.BlockSpec(a.shape, lambda s: (0,) * a.ndim)
+    return pl.pallas_call(
+        functools.partial(near_kernel, len(pieces)),
+        grid=(STEPS,),
+        out_shape=jax.ShapeDtypeStruct((STEPS, 64, RANK, 128), jnp.float32),
+        in_specs=[pl.BlockSpec(memory_space=pltpu.SMEM), whole(v), whole(own), whole(across)]
+        + [step_block(p.shape[1:]) for p in pieces],
+        out_specs=step_block((64, RANK, 128)),
+        scratch_shapes=[pltpu.VMEM((64 * (bins + 8), 128), jnp.float32)] * 2,
+        compiler_params=pltpu.CompilerParams(vmem_limit_bytes=VMEM_BYTES),
+        name="near",
+    )(slots, v, own, across, *pieces)
+
+
+def all_coefficients(step, own, across, near, pieces, slots, v):
     vmem = pl.BlockSpec(memory_space=pltpu.VMEM)
     hbm = pl.BlockSpec(memory_space=pl.ANY)
-    rows = (2, 32, RANK, 128)
+    bins = sum(p.shape[1] for p in pieces)
+    rows = (32, RANK, 128)
     return pl.pallas_call(
-        functools.partial(cross_kernel, len(pieces)),
+        functools.partial(far_kernel, step, len(pieces)),
         out_shape=[jax.ShapeDtypeStruct(rows, jnp.float32), jax.ShapeDtypeStruct(rows, jnp.bfloat16)],
-        in_specs=[pl.BlockSpec(memory_space=pltpu.SMEM), vmem] + [hbm] * (1 + len(pieces)),
+        in_specs=[pl.BlockSpec(memory_space=pltpu.SMEM), vmem] + [hbm] * (3 + len(pieces)),
         out_specs=[vmem, vmem],
-        scratch_shapes=[pltpu.VMEM(own.shape, jnp.bfloat16)] * 2
-        + [pltpu.VMEM((128 * ROW, 128), jnp.float32)] * 2
-        + [pltpu.SemaphoreType.DMA((len(pieces),)), pltpu.SemaphoreType.DMA],
+        scratch_shapes=[
+            pltpu.VMEM((bins,) + own.shape[1:], jnp.bfloat16),
+            pltpu.VMEM((bins,) + own.shape[1:], jnp.bfloat16),
+            pltpu.VMEM(near.shape[1:], jnp.float32),
+            pltpu.VMEM((1, bins) + own.shape[1:], jnp.bfloat16),
+        ]
+        + [pltpu.VMEM((64 * (bins + 8), 128), jnp.float32)] * 2
+        + [
+            pltpu.SemaphoreType.DMA((2 * bins,)),
+            pltpu.SemaphoreType.DMA,
+            pltpu.SemaphoreType.DMA((len(pieces),)),
+        ],
         compiler_params=pltpu.CompilerParams(vmem_limit_bytes=VMEM_BYTES),
-        name="cross",
-    )(slots, v, own, *pieces)
-
-
-def expand_kernel(step, u_ref, kept_ref, got_ref, *refs):
+        name="far",
+    )(slots, v, own, across, near, *pieces)
+
+
+def expand_kernel(step, u_ref, keep_ref, got_ref, *refs):
     out_ref, lags_ref, sem = refs[-3:]
-    count = kept_ref.shape[0]
+    count = keep_ref.shape[0]
     results = []
     for n in range(0, count, 2):
-        value = jnp.concatenate(
-            [kept_ref[b] + got_ref[b].astype(jnp.float32) for b in (n, n + 1)], axis=1
-        )
+        value = jnp.concatenate([keep_ref[b] + got_ref[b].astype(jnp.float32) for b in (n, n + 1)], axis=1)
         high = value.astype(jnp.bfloat16)
         low = (value - high.astype(jnp.float32)).astype(jnp.bfloat16)
         results.append(
@@ -269,10 +329,10 @@
     copy.wait()
 
 
-def expand(step, u, kept, got, before):
+def expand(step, u, keep, got, before):
     vmem = pl.BlockSpec(memory_space=pltpu.VMEM)
     hbm = pl.BlockSpec(memory_space=pl.ANY)
-    shape = (LAGS * kept.shape[0], 128)
+    shape = (LAGS * keep.shape[0], 128)
     held = [] if before is None else [before]
     return pl.pallas_call(
         functools.partial(expand_kernel, step),
@@ -283,7 +343,7 @@
         input_output_aliases={3: 0} if held else {},
         compiler_params=pltpu.CompilerParams(vmem_limit_bytes=VMEM_BYTES),
         name="expand",
-    )(u, kept, got, *held)
+    )(u, keep, got, *held)
 
 
 def place(x, z, y):
@@ -305,31 +365,35 @@
     second = jnp.concatenate([parts[:, 2:], other[:, 2:]], axis=1)
     plane_a = jnp.concatenate(around(first, "dz"), axis=1)
     plane_b = jnp.concatenate(around(second, "dx"), axis=1)
-    return [around(plane_a[s], "dx") + around(plane_b[s], "dz") for s in range(parts.shape[0])]
-
-
-def slot_table():
+    return plane_a, plane_b
+
+
+def plane_slots(last):
     me = lax.axis_index("chan")
     x, z, y = me // 8, me // 2 % 4, me % 2
-    offsets = np.array((0, -1, 1, 2))
-    last, plane, dy, e = np.meshgrid(offsets, offsets, np.arange(2), np.arange(2), indexing="ij")
-    last, plane, dy, e = (t.reshape(-1).astype(np.int32) for t in (last, plane, dy, e))
+    plane, dy, e = np.meshgrid(np.array((0, -1, 1, 2)), np.arange(2), np.arange(2), indexing="ij")
+    plane, dy, e = (t.reshape(-1).astype(np.int32) for t in (plane, dy, e))
     y_of = (y + dy) % 2
     first = (((x + last + 4) % 4) * 8 + ((z + plane + 4) % 4) * 2 + y_of) * 4 + e
     second = (((x + plane + 4) % 4) * 8 + ((z + last + 4) % 4) * 2 + y_of) * 4 + 2 + e
-    return jnp.concatenate([first, second]).astype(jnp.int32)
-
-
-def sum_over_spans(keep, send):
-    half = lax.axis_index("tm") // 2
-    got = lax.ppermute(send, "tm", [(0, 1), (1, 0), (2, 3), (3, 2)])
-
-    def chip(which):
-        own = lax.dynamic_index_in_dim(keep, which, 0, keepdims=False)
-        return own + lax.dynamic_index_in_dim(got, which, 0, keepdims=False).astype(jnp.float32)
-
-    far = lax.ppermute(chip(1 - half).astype(jnp.bfloat16), "tm", [(0, 2), (2, 0), (1, 3), (3, 1)])
-    return chip(half), far
+    return [first, second]
+
+
+def from_other_core(value):
+    return lax.ppermute(value, "tm", [(0, 1), (1, 0), (2, 3), (3, 2)])
+
+
+def from_other_chip(value):
+    return lax.ppermute(value, "tm", [(0, 2), (2, 0), (1, 3), (3, 1)])
+
+
+def windows_of_both_chips(parts):
+    got = from_other_chip(parts)
+    lower = lax.axis_index("tm") < 2
+    middle = parts.shape[-1] // 2
+    own = jnp.where(lower, parts, jnp.roll(parts, middle, axis=-1))
+    other = jnp.where(lower, jnp.roll(got, middle, axis=-1), got)
+    return jnp.where(jnp.arange(parts.shape[-1]) < middle, own, other)
 
 
 def basis_columns(windows, slots):
@@ -340,27 +404,56 @@
     table = jnp.dot(jnp.asarray(table), chosen, preferred_element_type=jnp.float32).astype(jnp.bfloat16)
     is_odd = (np.arange(2 * RANK) // HALF_RANK % 2 == 1)[:, None]
     nothing = jnp.zeros_like(table)
-    return jnp.concatenate([jnp.where(is_odd, nothing, table), jnp.where(is_odd, table, nothing)], axis=1)
+    real, imag = jnp.where(is_odd, nothing, table), jnp.where(is_odd, table, nothing)
+    return lambda start, stop: jnp.concatenate([real[:, start:stop], imag[:, start:stop]], axis=1)
 
 
 def shards(samples, plan, owner_table):
     windows = samples.shape[1] // HOP * lax.axis_size("tm")
     edge = lax.ppermute(samples[:, :HOP], "tm", [(1, 0), (2, 1), (3, 2)])
     own = whitened_spectra(samples, edge)
-    slots = slot_table()
+    slots = jnp.concatenate(sum([plane_slots(last) for last in (0, -1, 1, 2)], [])).astype(jnp.int32)
     v = basis_columns(windows, slots)
-    slots = jnp.concatenate([slots, (lax.axis_index("tm") % 2).astype(jnp.int32)[None]])
+    core = (lax.axis_index("tm") % 2).astype(jnp.int32)[None]
+    near_bins = BINS * 3 // 4
     padded = np.zeros((104, RANK))
     padded[:LAGS] = lag_factors(windows)[0]
     high, low = split_bf16(padded)
     u = jnp.asarray(np.concatenate([high, low, high], axis=1))
+    tables = (slots[:near_bins], jnp.concatenate([slots[near_bins:], core]), v(0, near_bins), v(near_bins, BINS))
     everyone = lax.all_to_all(own.reshape((32, 4) + own.shape[1:]), "chan", 0, 0)
+    everyone, tables = lax.optimization_barrier((everyone, tables))
+    near_slots, far_slots, near_v, far_v = tables
     roots = owner_table[plan]
     parts = jnp.stack([lax.dynamic_index_in_dim(everyone, roots[s], 0, keepdims=False) for s in range(STEPS)])
+    parts, own = lax.optimization_barrier((parts, own))
+    across = from_other_chip(own)
+    plane_a, plane_b = gather_references(windows_of_both_chips(parts))
+    near = [
+        shift(plane_a, dx=1),
+        shift(plane_b, dz=1),
+        shift(plane_a, dx=-1),
+        shift(plane_b, dz=-1),
+    ]
+    near = lax.optimization_barrier(near)
+    half = plane_a.shape[1] // 2
+    far = [
+        shift(near[0][:, :half], dx=1),
+        shift(near[2][:, half:], dx=-1),
+        shift(near[1][:, :half], dz=1),
+        shift(near[3][:, half:], dz=-1),
+    ]
+    partial = near_coefficients(own, across, [plane_a, plane_b] + near, near_slots, near_v)
+    far, partial = lax.optimization_barrier((far, partial))
+    keep, got = [None] * STEPS, [None] * STEPS
+    for s in range(STEPS):
+        keep[s], send = all_coefficients(s, own, across, partial, far, far_slots, far_v)
+        got[s] = from_other_core(send)
+        if s + 1 < STEPS:
+            partial, _ = lax.optimization_barrier((partial, send))
     out = None
-    for s, pieces in enumerate(gather_references(parts)):
-        keep, send = lag_coefficients(own, pieces, slots, v)
-        out = expand(s, u, *sum_over_spans(keep, send), out)
+    for s in range(STEPS):
+        out = expand(s, u, keep[s], got[s], out)
     return out.reshape(STEPS, LAGS, 32, 128).transpose(2, 0, 1, 3)
 
 

time: 229 us -> 204 us (0.89)
  starting transfers between devices: 67.2 us -> 25.4 us
  waiting for transfers between devices: 84 us -> 100 us
  local copies, waits for them, and re-layouts: 8.29 us -> 12.7 us
  other arithmetic: 6.64 us -> 2.61 us
    ppermute x25 -> x15, starting transfers between devices: 40.9 us -> 11.4 us  [shift(): return lax.ppermute(value, 'chan', pairs)]
    ppermute x25 -> x15, waiting for transfers between devices: 32.6 us -> 50.9 us  [shift(): return lax.ppermute(value, 'chan', pairs)]
    ppermute x6 -> x5, starting transfers between devices: 14.2 us -> 1.95 us  [the longest x3 1.86 us: from_other_core(): return lax.ppermute(value, 'tm', [(0, 1), (1, 0), (2, 3), (3, 2)])]
    convert_element_type x3 -> x0, other arithmetic: 4.44 us -> none  [sum_over_spans(): chip(1 - half).astype(jnp.bfloat16)]
    slice x0 -> x8, local copies, waits for them, and re-layouts: none -> 4.33 us  [the longest x1 1.1 us: shards(): near[2][:, half:]]
    all_to_all x1, waiting for transfers between devices: 32.3 us -> 28.9 us  [shards(): lax.all_to_all(own.reshape((32, 4) + own.shape[1:]), 'chan', 0, 0)]
    pallas_call x3 -> x4, Pallas kernels: 31.1 us -> 32.7 us  [the longest x3 17.2 us: all_coefficients(): pl.pallas_call(functools.partial(far_kernel, step, len(pieces)), out_shap...]
    ppermute x6 -> x5, waiting for transfers between devices: 13.6 us -> 14.9 us  [the longest x2 14.9 us: from_other_chip(): return lax.ppermute(value, 'tm', [(0, 2), (2, 0), (1, 3), (3, 1)])]
  transfers between devices with their start and end apart: 33 -> 22, of which waited for: 12 -> 9; matrix products, arithmetic and copies ran while one was open for 4% -> 4% of each run, Pallas kernels for 17% -> 17%
where the time goes in v3:
time: 204 us; the launch traced here: 202 us
  waiting for transfers between devices  100 us (49%)
  Pallas kernels  54.6 us (27%)
  starting transfers between devices  25.4 us (12%)
  local copies, waits for them, and re-layouts  12.7 us (6%)
  between operations  6.51 us (3%)
  other arithmetic  2.61 us (1%)
    ppermute x15, waiting for transfers between devices, shift(): return lax.ppermute(value, 'chan', pairs)  50.9 us
    all_to_all x1, waiting for transfers between devices, shards(): lax.all_to_all(own.reshape((32, 4) + own.shape[1:]), 'chan', 0, 0)  28.9 us
    pallas_call x3, Pallas kernels, all_coefficients(): pl.pallas_call(functools.partial(far_kernel, step, len(pieces)), out_shap...  17.2 us
    pallas_call x1, Pallas kernels, near_coefficients(): pl.pallas_call(functools.partial(near_kernel, len(pieces)), grid=(STEPS,)...  15.6 us
    ppermute x2, waiting for transfers between devices, from_other_chip(): return lax.ppermute(value, 'tm', [(0, 2), (2, 0), (1, 3), (3, 1)])  14.9 us
    ppermute x15, starting transfers between devices, shift(): return lax.ppermute(value, 'chan', pairs)  11.4 us
    pallas_call x1, Pallas kernels, whitened_spectra(): pl.pallas_call(functools.partial(spectra_kernel, GROUP), grid=(windows //...  11.1 us
    pallas_call x3, Pallas kernels, expand(): pl.pallas_call(functools.partial(expand_kernel, step), out_shape=jax.Shap...  10.8 us
  transfers between devices with their start and end apart: 22, of which 9 were waited for; matrix products, arithmetic and copies ran while one was open for 4% of the time, Pallas kernels for 17%

profile of v3, /device:TPU:1, one launch (start us, length us, event | category | flops | bytes accessed | tf_op | source)
XLA Modules:
  0.0 202.2 jit_solution(12088482478801531711)
XLA Ops:
  0.9 3.3 %collective-permute-start = (bf16[128,512]{1,0:T(8,128)(2,1)S(1)}, bf16[128,512]{1,0:T(8,128)(2,1)S(1)}, u32[]{:S(2)}, u32[]{:S(2)}) collective-permute-start(bf16[128,512]{1,0:T(8,128)(2,1)S(1)} %slice.66), channel_id=1, source_target_pairs={{1,0},{2,1},{3,2},{5,4},{6,5},{7,6},{9,8},{10,9},{11,10},{13,12},{... | collective-permute-start | bytes 393224 | tf_op jit(solution)/shard_map/ppermute | solution.py:413
  4.3 5.5 %collective-permute-done.edge_ref = bf16[128,512]{1,0:T(8,128)(2,1)S(1)} collective-permute-done((bf16[128,512]{1,0:T(8,128)(2,1)S(1)}, bf16[128,512]{1,0:T(8,128)(2,1)S(1)}, u32[]{:S(2)}, u32[]{:S(2)}) %collective-permute-start) | collective-permute-done | bytes 131104 | tf_op jit(solution)/shard_map/ppermute | solution.py:413
  10.4 11.1 %spectra.1.own_ref.own_hbm = bf16[128,96,128]{2,1,0:T(8,128)(2,1)} custom-call(bf16[128,24576]{1,0:T(8,128)(2,1)} %next_ref.1, bf16[128,24576]{1,0:T(8,128)(2,1)} %next_ref.1, bf16[128,512]{1,0:T(8,128)(2,1)} %copy-done.12, bf16[256,1024]{1,0:T(8,128)(2,1)} %constant.223.clone.table_ref, bf16[128,256]{1,0:T(8,128)(2,1)} %constant.224.clone.band_ref, ...), custom_call_target="tpu_custom_call" | custom-call | tf_op jit(solution)/shard_map/spectra/pallas_call | solution.py:152
  21.6 8.8 %all-to-all-start = ((bf16[32,4,96,128]{3,2,1,0:T(8,128)(2,1)}), bf16[32,4,96,128]{3,2,1,0:T(8,128)(2,1)S(1)}, u32[]{:S(2)}, u32[]{:S(2)}) async-start(bf16[32,4,96,128]{3,2,1,0:T(8,128)(2,1)} %bitcast.15), calls=%async_computation | async-start | bytes 6291456 | tf_op jit(solution)/shard_map/all_to_all | solution.py:424
  40.8 28.9 %all-to-all-done = bf16[32,4,96,128]{3,2,1,0:T(8,128)(2,1)S(1)} async-done(((bf16[32,4,96,128]{3,2,1,0:T(8,128)(2,1)}), bf16[32,4,96,128]{3,2,1,0:T(8,128)(2,1)S(1)}, u32[]{:S(2)}, u32[]{:S(2)}) %all-to-all-start) | async-done | bytes 3145760 | tf_op jit(solution)/shard_map/all_to_all | solution.py:424
  70.0 8.9 %collective-permute-done.2 = bf16[3,4,96,128]{3,2,1,0:T(8,128)(2,1)S(1)} collective-permute-done((bf16[3,4,96,128]{3,2,1,0:T(8,128)(2,1)S(1)}, bf16[3,4,96,128]{3,2,1,0:T(8,128)(2,1)S(1)}, u32[]{:S(2)}, u32[]{:S(2)}) %collective-permute-start.2) | collective-permute-done | bytes 294944 | tf_op jit(solution)/shard_map/ppermute | solution.py:387
  79.6 1.2 copy-done.1
  80.9 7.8 %collective-permute-done.3 = bf16[3,4,96,128]{3,2,1,0:T(8,128)(2,1)S(1)} collective-permute-done((bf16[3,4,96,128]{3,2,1,0:T(8,128)(2,1)S(1)}, bf16[3,4,96,128]{3,2,1,0:T(8,128)(2,1)S(1)}, u32[]{:S(2)}, u32[]{:S(2)}) %collective-permute-start.3) | collective-permute-done | bytes 294944 | tf_op jit(solution)/shard_map/ppermute | solution.py:355
  88.9 2.7 %collective-permute-start.9 = (bf16[3,4,96,128]{3,2,1,0:T(8,128)(2,1)S(1)}, bf16[3,4,96,128]{3,2,1,0:T(8,128)(2,1)S(1)}, u32[]{:S(2)}, u32[]{:S(2)}) collective-permute-start(bf16[3,4,96,128]{3,2,1,0:T(8,128)(2,1)S(1)} %pad_maximum_fusion.2), channel_id=1, source_target_pairs={{0,96},{4,100},{8,104},{12,108},{16,112},{20,116},{24,120},{28,124... | collective-permute-start | bytes 884744 | tf_op jit(solution)/shard_map/ppermute | solution.py:355
  91.6 1.2 collective-permute-start.6
  92.8 12.0 %collective-permute-done.8 = bf16[3,4,96,128]{3,2,1,0:T(8,128)(2,1)S(1)} collective-permute-done((bf16[3,4,96,128]{3,2,1,0:T(8,128)(2,1)S(1)}, bf16[3,4,96,128]{3,2,1,0:T(8,128)(2,1)S(1)}, u32[]{:S(2)}, u32[]{:S(2)}) %collective-permute-start.8) | collective-permute-done | bytes 294944 | tf_op jit(solution)/shard_map/ppermute | solution.py:355
  104.9 2.7 %collective-permute-start.5 = (bf16[3,4,96,128]{3,2,1,0:T(8,128)(2,1)S(1)}, bf16[3,4,96,128]{3,2,1,0:T(8,128)(2,1)S(1)}, u32[]{:S(2)}, u32[]{:S(2)}) collective-permute-start(bf16[3,4,96,128]{3,2,1,0:T(8,128)(2,1)S(1)} %pad_maximum_fusion.1), channel_id=1, source_target_pairs={{0,24},{4,28},{8,0},{12,4},{16,8},{20,12},{24,16},{28,20},{32,56},... | collective-permute-start | bytes 884744 | tf_op jit(solution)/shard_map/ppermute | solution.py:355
  107.8 5.8 %collective-permute-done.4 = bf16[3,4,96,128]{3,2,1,0:T(8,128)(2,1)S(1)} collective-permute-done((bf16[3,4,96,128]{3,2,1,0:T(8,128)(2,1)S(1)}, bf16[3,4,96,128]{3,2,1,0:T(8,128)(2,1)S(1)}, u32[]{:S(2)}, u32[]{:S(2)}) %collective-permute-start.4) | collective-permute-done | bytes 294944 | tf_op jit(solution)/shard_map/ppermute | solution.py:355
  115.4 22.6 %collective-permute-done.13.refs_5_ = bf16[3,16,96,128]{3,2,1,0:T(8,128)(2,1)S(1)} collective-permute-done((bf16[3,16,96,128]{3,2,1,0:T(8,128)(2,1)S(1)}, bf16[3,16,96,128]{3,2,1,0:T(8,128)(2,1)S(1)}, u32[]{:S(2)}, u32[]{:S(2)}) %collective-permute-start.13) | collective-permute-done | bytes 1179680 | tf_op jit(solution)/shard_map/ppermute | solution.py:355
  137.9 2.7 %collective-permute-done.11.refs_3_ = bf16[3,16,96,128]{3,2,1,0:T(8,128)(2,1)S(1)} collective-permute-done((bf16[3,16,96,128]{3,2,1,0:T(8,128)(2,1)S(1)}, bf16[3,16,96,128]{3,2,1,0:T(8,128)(2,1)S(1)}, u32[]{:S(2)}, u32[]{:S(2)}) %collective-permute-start.11) | collective-permute-done | bytes 1179680 | tf_op jit(solution)/shard_map/ppermute | solution.py:355
  146.0 1.5 collective-permute-start.14
  147.5 6.0 %collective-permute-done.1.next_ref.next_hbm = bf16[128,96,128]{2,1,0:T(8,128)(2,1)} collective-permute-done((bf16[128,96,128]{2,1,0:T(8,128)(2,1)S(1)}, bf16[128,96,128]{2,1,0:T(8,128)(2,1)}, u32[]{:S(2)}, u32[]{:S(2)}) %collective-permute-start.1) | collective-permute-done | bytes 3145760 | tf_op jit(solution)/shard_map/ppermute | solution.py:387
  153.5 15.6 %near.1.near_hbm = f32[3,64,48,128]{3,2,1,0:T(8,128)} custom-call(s32[96]{0:T(128)} %concatenate.38.slots_ref, bf16[96,192]{1,0:T(8,128)(2,1)} %pad_maximum_fusion.3.v_ref, bf16[128,96,128]{2,1,0:T(8,128)(2,1)} %spectra.1.own_ref.own_hbm, bf16[128,96,128]{2,1,0:T(8,128)(2,1)} %collective-permute-done.1.next_ref.next_hbm, bf16[3,16,96,128]{3,2,1,0:T(8,128)(2,1)} %copy-done.7, ...), custom_call_target="tpu_custom_call" | custom-call | tf_op jit(solution)/shard_map/near/pallas_call | solution.py:273
  169.9 5.8 %far.3 = (f32[32,48,128]{2,1,0:T(8,128)}, bf16[32,48,128]{2,1,0:T(8,128)(2,1)}) custom-call(s32[33]{0:T(128)} %pad_add_fusion.slots_ref, bf16[96,64]{1,0:T(8,128)(2,1)} %pad_maximum_fusion.4.v_ref, bf16[128,96,128]{2,1,0:T(8,128)(2,1)} %spectra.1.own_ref.own_hbm, bf16[128,96,128]{2,1,0:T(8,128)(2,1)} %collective-permute-done.1.next_ref.next_hbm, ...), custom_call_target="tpu_custom_call" | custom-call | tf_op jit(solution)/shard_map/far/pallas_call | solution.py:291
  176.8 5.7 %far.4 = (f32[32,48,128]{2,1,0:T(8,128)}, bf16[32,48,128]{2,1,0:T(8,128)(2,1)}) custom-call(s32[33]{0:T(128)} %pad_add_fusion.slots_ref, bf16[96,64]{1,0:T(8,128)(2,1)} %pad_maximum_fusion.4.v_ref, bf16[128,96,128]{2,1,0:T(8,128)(2,1)} %spectra.1.own_ref.own_hbm, bf16[128,96,128]{2,1,0:T(8,128)(2,1)} %collective-permute-done.1.next_ref.next_hbm, ...), custom_call_target="tpu_custom_call" | custom-call | tf_op jit(solution)/shard_map/far/pallas_call | solution.py:291
  182.7 5.7 %far.5 = (f32[32,48,128]{2,1,0:T(8,128)}, bf16[32,48,128]{2,1,0:T(8,128)(2,1)}) custom-call(s32[33]{0:T(128)} %pad_add_fusion.slots_ref, bf16[96,64]{1,0:T(8,128)(2,1)} %pad_maximum_fusion.4.v_ref, bf16[128,96,128]{2,1,0:T(8,128)(2,1)} %spectra.1.own_ref.own_hbm, bf16[128,96,128]{2,1,0:T(8,128)(2,1)} %collective-permute-done.1.next_ref.next_hbm, ...), custom_call_target="tpu_custom_call" | custom-call | tf_op jit(solution)/shard_map/far/pallas_call | solution.py:291
  189.7 3.6 %expand.3.refs_0_ = f32[3,3232,128]{2,1,0:T(8,128)} custom-call(bf16[104,144]{1,0:T(8,128)(2,1)} %constant.231.clone.u_ref, f32[32,48,128]{2,1,0:T(8,128)} %get-tuple-element.52.keep_ref, bf16[32,48,128]{2,1,0:T(8,128)(2,1)} %copy-done.11), custom_call_target="tpu_custom_call" | custom-call | tf_op jit(solution)/shard_map/expand/pallas_call | solution.py:337
  194.1 3.6 %expand.4.refs_0_ = f32[3,3232,128]{2,1,0:T(8,128)} custom-call(bf16[104,144]{1,0:T(8,128)(2,1)} %constant.231.clone.u_ref, f32[32,48,128]{2,1,0:T(8,128)} %get-tuple-element.51.keep_ref, bf16[32,48,128]{2,1,0:T(8,128)(2,1)} %copy-done.9, f32[3,3232,128]{2,1,0:T(8,128)} %expand.3.refs_0_), custom_call_target="tpu_custom_call", output_to_operand_aliasing={{}: (3, {})} | custom-call | tf_op jit(solution)/shard_map/expand/pallas_call | solution.py:337
  198.5 3.6 %expand.5 = f32[3,3232,128]{2,1,0:T(8,128)} custom-call(bf16[104,144]{1,0:T(8,128)(2,1)} %constant.231.clone.u_ref, f32[32,48,128]{2,1,0:T(8,128)} %get-tuple-element.49.keep_ref, bf16[32,48,128]{2,1,0:T(8,128)(2,1)} %copy-done.10, f32[3,3232,128]{2,1,0:T(8,128)} %expand.4.refs_0_), custom_call_target="tpu_custom_call", output_to_operand_aliasing={{}: (3, {})} | custom-call | tf_op jit(solution)/shard_map/expand/pallas_call | solution.py:337
  (102 shorter events, 19.4 us)
Async XLA Ops:
  0.0 30.6 %copy-start = (s32[32]{0:T(128)S(1)}, s32[32]{0:T(128)}, u32[]{:S(2)}) copy-start(s32[32]{0:T(128)} %param.23) | copy-start | bytes 388
  0.9 8.9 %collective-permute-start = (bf16[128,512]{1,0:T(8,128)(2,1)S(1)}, bf16[128,512]{1,0:T(8,128)(2,1)S(1)}, u32[]{:S(2)}, u32[]{:S(2)}) collective-permute-start(bf16[128,512]{1,0:T(8,128)(2,1)S(1)} %slice.66), channel_id=1, source_target_pairs={{1,0},{2,1},{3,2},{5,4},{6,5},{7,6},{9,8},{10,9},{11,10},{13,12},{... | collective-permute-start | bytes 393224 | tf_op jit(solution)/shard_map/ppermute | solution.py:413
  21.6 48.1 %all-to-all-start = ((bf16[32,4,96,128]{3,2,1,0:T(8,128)(2,1)}), bf16[32,4,96,128]{3,2,1,0:T(8,128)(2,1)S(1)}, u32[]{:S(2)}, u32[]{:S(2)}) async-start(bf16[32,4,96,128]{3,2,1,0:T(8,128)(2,1)} %bitcast.15), calls=%async_computation | async-start | bytes 6291456 | tf_op jit(solution)/shard_map/all_to_all | solution.py:424
  69.7 9.2 %collective-permute-start.2 = (bf16[3,4,96,128]{3,2,1,0:T(8,128)(2,1)S(1)}, bf16[3,4,96,128]{3,2,1,0:T(8,128)(2,1)S(1)}, u32[]{:S(2)}, u32[]{:S(2)}) collective-permute-start(bf16[3,4,96,128]{3,2,1,0:T(8,128)(2,1)S(1)} %pad_maximum_fusion), channel_id=1, source_target_pairs={{0,2},{2,0},{1,3},{3,1},{4,6},{6,4},{5,7},{7,5},{8,10},{10,8},{9,1... | collective-permute-start | bytes 884744 | tf_op jit(solution)/shard_map/ppermute | solution.py:387
  79.5 9.2 %collective-permute-start.3 = (bf16[3,4,96,128]{3,2,1,0:T(8,128)(2,1)S(1)}, bf16[3,4,96,128]{3,2,1,0:T(8,128)(2,1)S(1)}, u32[]{:S(2)}, u32[]{:S(2)}) collective-permute-start(bf16[3,4,96,128]{3,2,1,0:T(8,128)(2,1)S(1)} %fusion), channel_id=1, source_target_pairs={{0,4},{4,0},{8,12},{12,8},{16,20},{20,16},{24,28},{28,24},{32,36},... | collective-permute-start | bytes 884744 | tf_op jit(solution)/shard_map/ppermute | solution.py:355
  80.8 72.7 %collective-permute-start.1 = (bf16[128,96,128]{2,1,0:T(8,128)(2,1)S(1)}, bf16[128,96,128]{2,1,0:T(8,128)(2,1)}, u32[]{:S(2)}, u32[]{:S(2)}) collective-permute-start(bf16[128,96,128]{2,1,0:T(8,128)(2,1)S(1)} %copy-done.1), channel_id=1, source_target_pairs={{0,2},{2,0},{1,3},{3,1},{4,6},{6,4},{5,7},{7,5},{8,10},{10,8},{9,1... | collective-permute-start | bytes 9437192 | tf_op jit(solution)/shard_map/ppermute | solution.py:387
  88.8 16.0 %collective-permute-start.8 = (bf16[3,4,96,128]{3,2,1,0:T(8,128)(2,1)S(1)}, bf16[3,4,96,128]{3,2,1,0:T(8,128)(2,1)S(1)}, u32[]{:S(2)}, u32[]{:S(2)}) collective-permute-start(bf16[3,4,96,128]{3,2,1,0:T(8,128)(2,1)S(1)} %pad_maximum_fusion.2), channel_id=1, source_target_pairs={{0,32},{4,36},{8,40},{12,44},{16,48},{20,52},{24,56},{28,60},{32,6... | collective-permute-start | bytes 884744 | tf_op jit(solution)/shard_map/ppermute | solution.py:355
  88.9 16.0 %collective-permute-start.9 = (bf16[3,4,96,128]{3,2,1,0:T(8,128)(2,1)S(1)}, bf16[3,4,96,128]{3,2,1,0:T(8,128)(2,1)S(1)}, u32[]{:S(2)}, u32[]{:S(2)}) collective-permute-start(bf16[3,4,96,128]{3,2,1,0:T(8,128)(2,1)S(1)} %pad_maximum_fusion.2), channel_id=1, source_target_pairs={{0,96},{4,100},{8,104},{12,108},{16,112},{20,116},{24,120},{28,124... | collective-permute-start | bytes 884744 | tf_op jit(solution)/shard_map/ppermute | solution.py:355
  91.6 16.1 %collective-permute-start.10 = (bf16[3,4,96,128]{3,2,1,0:T(8,128)(2,1)S(1)}, bf16[3,4,96,128]{3,2,1,0:T(8,128)(2,1)S(1)}, u32[]{:S(2)}, u32[]{:S(2)}) collective-permute-start(bf16[3,4,96,128]{3,2,1,0:T(8,128)(2,1)S(1)} %pad_maximum_fusion.2), channel_id=1, source_target_pairs={{0,64},{4,68},{8,72},{12,76},{16,80},{20,84},{24,88},{28,92},{32,9... | collective-permute-start | bytes 884744 | tf_op jit(solution)/shard_map/ppermute | solution.py:355
  91.6 22.2 %collective-permute-start.6 = (bf16[3,4,96,128]{3,2,1,0:T(8,128)(2,1)S(1)}, bf16[3,4,96,128]{3,2,1,0:T(8,128)(2,1)S(1)}, u32[]{:S(2)}, u32[]{:S(2)}) collective-permute-start(bf16[3,4,96,128]{3,2,1,0:T(8,128)(2,1)S(1)} %pad_maximum_fusion.1), channel_id=1, source_target_pairs={{0,16},{4,20},{8,24},{12,28},{16,0},{20,4},{24,8},{28,12},{32,48},... | collective-permute-start | bytes 884744 | tf_op jit(solution)/shard_map/ppermute | solution.py:355
  104.8 8.8 %collective-permute-start.4 = (bf16[3,4,96,128]{3,2,1,0:T(8,128)(2,1)S(1)}, bf16[3,4,96,128]{3,2,1,0:T(8,128)(2,1)S(1)}, u32[]{:S(2)}, u32[]{:S(2)}) collective-permute-start(bf16[3,4,96,128]{3,2,1,0:T(8,128)(2,1)S(1)} %pad_maximum_fusion.1), channel_id=1, source_target_pairs={{0,8},{4,12},{8,16},{12,20},{16,24},{20,28},{24,0},{28,4},{32,40},... | collective-permute-start | bytes 884744 | tf_op jit(solution)/shard_map/ppermute | solution.py:355
  104.9 8.8 %collective-permute-start.5 = (bf16[3,4,96,128]{3,2,1,0:T(8,128)(2,1)S(1)}, bf16[3,4,96,128]{3,2,1,0:T(8,128)(2,1)S(1)}, u32[]{:S(2)}, u32[]{:S(2)}) collective-permute-start(bf16[3,4,96,128]{3,2,1,0:T(8,128)(2,1)S(1)} %pad_maximum_fusion.1), channel_id=1, source_target_pairs={{0,24},{4,28},{8,0},{12,4},{16,8},{20,12},{24,16},{28,20},{32,56},... | collective-permute-start | bytes 884744 | tf_op jit(solution)/shard_map/ppermute | solution.py:355
  107.7 33.9 %copy-start.8 = (bf16[3,16,96,128]{3,2,1,0:T(8,128)(2,1)}, bf16[3,16,96,128]{3,2,1,0:T(8,128)(2,1)S(1)}, u32[]{:S(2)}) copy-start(bf16[3,16,96,128]{3,2,1,0:T(8,128)(2,1)S(1)} %constant_dynamic-update-slice_fusion.5.refs_1_) | copy-start | bytes 3538948
  107.8 30.2 %collective-permute-start.13 = (bf16[3,16,96,128]{3,2,1,0:T(8,128)(2,1)S(1)}, bf16[3,16,96,128]{3,2,1,0:T(8,128)(2,1)S(1)}, u32[]{:S(2)}, u32[]{:S(2)}) collective-permute-start(bf16[3,16,96,128]{3,2,1,0:T(8,128)(2,1)S(1)} %constant_dynamic-update-slice_fusion.5.refs_1_), channel_id=1, source_target_pairs={{0,24},{4,28},{8,0},{12,4},{16,8},{20,12},{24,16},{28,20},{32,56},... | collective-permute-start | bytes 3538952 | tf_op jit(solution)/shard_map/ppermute | solution.py:355
  113.7 27.0 %collective-permute-start.11 = (bf16[3,16,96,128]{3,2,1,0:T(8,128)(2,1)S(1)}, bf16[3,16,96,128]{3,2,1,0:T(8,128)(2,1)S(1)}, u32[]{:S(2)}, u32[]{:S(2)}) collective-permute-start(bf16[3,16,96,128]{3,2,1,0:T(8,128)(2,1)S(1)} %constant_dynamic-update-slice_fusion.5.refs_1_), channel_id=1, source_target_pairs={{0,8},{4,12},{8,16},{12,20},{16,24},{20,28},{24,0},{28,4},{32,40},... | collective-permute-start | bytes 3538952 | tf_op jit(solution)/shard_map/ppermute | solution.py:355
  113.8 26.8 %collective-permute-start.12 = (bf16[3,16,96,128]{3,2,1,0:T(8,128)(2,1)S(1)}, bf16[3,16,96,128]{3,2,1,0:T(8,128)(2,1)S(1)}, u32[]{:S(2)}, u32[]{:S(2)}) collective-permute-start(bf16[3,16,96,128]{3,2,1,0:T(8,128)(2,1)S(1)} %constant_dynamic-update-slice_fusion.refs_0_), channel_id=1, source_target_pairs={{0,96},{4,100},{8,104},{12,108},{16,112},{20,116},{24,120},{28,124... | collective-permute-start | bytes 3538952 | tf_op jit(solution)/shard_map/ppermute | solution.py:355
  114.5 26.1 %collective-permute-start.7 = (bf16[3,16,96,128]{3,2,1,0:T(8,128)(2,1)S(1)}, bf16[3,16,96,128]{3,2,1,0:T(8,128)(2,1)S(1)}, u32[]{:S(2)}, u32[]{:S(2)}) collective-permute-start(bf16[3,16,96,128]{3,2,1,0:T(8,128)(2,1)S(1)} %constant_dynamic-update-slice_fusion.refs_0_), channel_id=1, source_target_pairs={{0,32},{4,36},{8,40},{12,44},{16,48},{20,52},{24,56},{28,60},{32,6... | collective-permute-start | bytes 3538952 | tf_op jit(solution)/shard_map/ppermute | solution.py:355
  144.5 24.5 %collective-permute-start.17 = (bf16[3,8,96,128]{3,2,1,0:T(8,128)(2,1)}, bf16[3,8,96,128]{3,2,1,0:T(8,128)(2,1)S(1)}, u32[]{:S(2)}, u32[]{:S(2)}) collective-permute-start(bf16[3,8,96,128]{3,2,1,0:T(8,128)(2,1)} %slice.85), channel_id=1, source_target_pairs={{0,24},{4,28},{8,0},{12,4},{16,8},{20,12},{24,16},{28,20},{32,56},... | collective-permute-start | bytes 1769480 | tf_op jit(solution)/shard_map/ppermute | solution.py:355
  145.7 23.4 %collective-permute-start.16 = (bf16[3,8,96,128]{3,2,1,0:T(8,128)(2,1)}, bf16[3,8,96,128]{3,2,1,0:T(8,128)(2,1)}, u32[]{:S(2)}, u32[]{:S(2)}) collective-permute-start(bf16[3,8,96,128]{3,2,1,0:T(8,128)(2,1)} %slice.84), channel_id=1, source_target_pairs={{0,8},{4,12},{8,16},{12,20},{16,24},{20,28},{24,0},{28,4},{32,40},... | collective-permute-start | bytes 1769480 | tf_op jit(solution)/shard_map/ppermute | solution.py:355
  146.0 23.1 %collective-permute-start.15 = (bf16[3,8,96,128]{3,2,1,0:T(8,128)(2,1)}, bf16[3,8,96,128]{3,2,1,0:T(8,128)(2,1)}, u32[]{:S(2)}, u32[]{:S(2)}) collective-permute-start(bf16[3,8,96,128]{3,2,1,0:T(8,128)(2,1)} %slice.83), channel_id=1, source_target_pairs={{0,96},{4,100},{8,104},{12,108},{16,112},{20,116},{24,120},{28,124... | collective-permute-start | bytes 1769480 | tf_op jit(solution)/shard_map/ppermute | solution.py:355
  146.0 23.1 %collective-permute-start.14 = (bf16[3,8,96,128]{3,2,1,0:T(8,128)(2,1)}, bf16[3,8,96,128]{3,2,1,0:T(8,128)(2,1)}, u32[]{:S(2)}, u32[]{:S(2)}) collective-permute-start(bf16[3,8,96,128]{3,2,1,0:T(8,128)(2,1)} %slice.82), channel_id=1, source_target_pairs={{0,32},{4,36},{8,40},{12,44},{16,48},{20,52},{24,56},{28,60},{32,6... | collective-permute-start | bytes 1769480 | tf_op jit(solution)/shard_map/ppermute | solution.py:355
  175.7 13.3 %collective-permute-start.20 = (bf16[32,48,128]{2,1,0:T(8,128)(2,1)}, bf16[32,48,128]{2,1,0:T(8,128)(2,1)S(1)}, u32[]{:S(2)}, u32[]{:S(2)}) collective-permute-start(bf16[32,48,128]{2,1,0:T(8,128)(2,1)} %get-tuple-element.45), channel_id=1, source_target_pairs={{0,1},{1,0},{2,3},{3,2},{4,5},{5,4},{6,7},{7,6},{8,9},{9,8},{10,11... | collective-permute-start | bytes 1179656 | tf_op jit(solution)/shard_map/ppermute | solution.py:383
  182.6 10.7 %collective-permute-start.19 = (bf16[32,48,128]{2,1,0:T(8,128)(2,1)}, bf16[32,48,128]{2,1,0:T(8,128)(2,1)S(1)}, u32[]{:S(2)}, u32[]{:S(2)}) collective-permute-start(bf16[32,48,128]{2,1,0:T(8,128)(2,1)} %get-tuple-element.47), channel_id=1, source_target_pairs={{0,1},{1,0},{2,3},{3,2},{4,5},{5,4},{6,7},{7,6},{8,9},{9,8},{10,11... | collective-permute-start | bytes 1179656 | tf_op jit(solution)/shard_map/ppermute | solution.py:383
  188.4 9.3 %collective-permute-start.18 = (bf16[32,48,128]{2,1,0:T(8,128)(2,1)}, bf16[32,48,128]{2,1,0:T(8,128)(2,1)S(1)}, u32[]{:S(2)}, u32[]{:S(2)}) collective-permute-start(bf16[32,48,128]{2,1,0:T(8,128)(2,1)} %get-tuple-element.50), channel_id=1, source_target_pairs={{0,1},{1,0},{2,3},{3,2},{4,5},{5,4},{6,7},{7,6},{8,9},{9,8},{10,11... | collective-permute-start | bytes 1179656 | tf_op jit(solution)/shard_map/ppermute | solution.py:383
  (17 other events, 130.9 us)

commit v4 on v3

--- a/solution.py
+++ b/solution.py
@@ -173,10 +173,10 @@
     for piece, size in pieces:
         for j in range(size):
             slot = slots[base + len(results)]
-            width = piece.shape[3] // len(spans)
+            width = piece.shape[-1] // len(spans)
             total = None
             for n, span in enumerate(spans):
-                own = span[slot]
+                own = span(slot)
                 turned = []
                 for r in range(0, own.shape[0], 2 * GROUP):
                     turned += [own[r + GROUP : r + 2 * GROUP], -own[r : r + GROUP]]
@@ -212,14 +212,28 @@
     return totals
 
 
-def near_kernel(count, slots_ref, v_ref, own_ref, next_ref, *refs):
+def both_spans(own_ref, across_refs):
+    middle = own_ref.shape[1] // 2
+    return [
+        lambda slot, start=start, across=across: jnp.concatenate(
+            [own_ref[slot, start : start + middle], across[slot]], axis=0
+        )
+        for start, across in zip((0, middle), across_refs)
+    ]
+
+
+def halves_of(planes):
+    return [(plane.at[half], plane.shape[2]) for plane in planes for half in range(2)]
+
+
+def near_kernel(count, slots_ref, v_ref, own_ref, upper_ref, lower_ref, *refs):
     pieces, (out_ref, real_rows, imag_rows) = refs[:count], refs[count:]
-    size = pieces[0].shape[1]
-    bins = count * size
+    spans = both_spans(own_ref, (upper_ref, lower_ref))
+    size = pieces[0].shape[2]
+    bins = 2 * count * size
     row = bins + 8
     for n in range(0, count, 2):
-        chosen = [(p, size) for p in pieces[n : n + 2]]
-        add_cross((own_ref, next_ref), chosen, slots_ref, n * size, row, real_rows, imag_rows)
+        add_cross(spans, halves_of(pieces[n : n + 2]), slots_ref, 2 * n * size, row, real_rows, imag_rows)
 
     def some(n, carry):
         channels = [n * 32 + j for j in range(32)]
@@ -231,36 +245,34 @@
     lax.fori_loop(0, 2, some, 0)
 
 
-def far_kernel(step, count, slots_ref, v_ref, own_hbm, next_hbm, near_hbm, *refs):
-    pieces = refs[:count]
-    keep_ref, send_ref, own_ref, next_ref, near_ref, other_ref, real_rows, imag_rows, own_sems, near_sem, sems = refs[
-        count:
-    ]
+def far_kernel(count, slots_ref, v_ref, own_hbm, upper_hbm, lower_hbm, near_ref, *refs):
+    pieces, refs = refs[:count], refs[count:]
+    keep_ref, send_ref, own_ref, upper_ref, lower_ref, real_rows, imag_rows, sems = refs
     size = pieces[0].shape[1]
     bins = count * size
     row = bins + 8
-    copies = [
-        pltpu.make_async_copy(p.at[step], other_ref.at[0, pl.ds(size * i, size)], sems.at[i])
-        for i, p in enumerate(pieces)
-    ]
-    for n, (source, target) in enumerate(((own_hbm, own_ref), (next_hbm, next_ref))):
-        copies += [
-            pltpu.make_async_copy(source.at[slots_ref[j]], target.at[j], own_sems.at[n * bins + j])
-            for j in range(bins)
-        ]
-    near_copy = pltpu.make_async_copy(near_hbm.at[step], near_ref, near_sem)
-    for copy in copies + [near_copy]:
-        copy.start()
-    for copy in copies:
-        copy.wait()
-    add_cross((own_ref, next_ref), [(other_ref, bins)], range(bins), 0, row, real_rows, imag_rows)
-    near_copy.wait()
+
+    @pl.when(pl.program_id(0) == 0)
+    def _():
+        copies = []
+        for n, (source, target) in enumerate(((own_hbm, own_ref), (upper_hbm, upper_ref), (lower_hbm, lower_ref))):
+            copies += [
+                pltpu.make_async_copy(source.at[slots_ref[j]], target.at[j], sems.at[n * bins + j])
+                for j in range(bins)
+            ]
+        for copy in copies:
+            copy.start()
+        for copy in copies:
+            copy.wait()
+
+    spans = both_spans(own_ref, (upper_ref, lower_ref))
+    add_cross(spans, [(p, size) for p in pieces], range(bins), 0, row, real_rows, imag_rows)
     core = slots_ref[bins]
     for out_ref, which in ((send_ref, 1 - core), (keep_ref, core)):
         channels = [which * 32 + j for j in range(32)]
         totals = coefficients(v_ref, real_rows, imag_rows, row, bins, channels)
         for j, total in enumerate(totals):
-            out_ref[j] = (near_ref[channels[j]] + total).astype(out_ref.dtype)
+            out_ref[0, j] = (near_ref[0, channels[j]] + total).astype(out_ref.dtype)
 
 
 def step_block(shape):
@@ -268,82 +280,71 @@
 
 
 def near_coefficients(own, across, pieces, slots, v):
-    bins = sum(p.shape[1] for p in pieces)
+    bins = sum(p.shape[0] * p.shape[2] for p in pieces)
     whole = lambda a: pl.BlockSpec(a.shape, lambda s: (0,) * a.ndim)
     return pl.pallas_call(
         functools.partial(near_kernel, len(pieces)),
         grid=(STEPS,),
         out_shape=jax.ShapeDtypeStruct((STEPS, 64, RANK, 128), jnp.float32),
-        in_specs=[pl.BlockSpec(memory_space=pltpu.SMEM), whole(v), whole(own), whole(across)]
-        + [step_block(p.shape[1:]) for p in pieces],
+        in_specs=[pl.BlockSpec(memory_space=pltpu.SMEM), whole(v), whole(own)]
+        + [whole(a) for a in across]
+        + [pl.BlockSpec((2, 1) + p.shape[2:], lambda s: (0, s, 0, 0, 0)) for p in pieces],
         out_specs=step_block((64, RANK, 128)),
         scratch_shapes=[pltpu.VMEM((64 * (bins + 8), 128), jnp.float32)] * 2,
         compiler_params=pltpu.CompilerParams(vmem_limit_bytes=VMEM_BYTES),
         name="near",
-    )(slots, v, own, across, *pieces)
-
-
-def all_coefficients(step, own, across, near, pieces, slots, v):
-    vmem = pl.BlockSpec(memory_space=pltpu.VMEM)
+    )(slots, v, own, *across, *pieces)
+
+
+def all_coefficients(own, across, near, pieces, slots, v):
     hbm = pl.BlockSpec(memory_space=pl.ANY)
     bins = sum(p.shape[1] for p in pieces)
     rows = (32, RANK, 128)
     return pl.pallas_call(
-        functools.partial(far_kernel, step, len(pieces)),
-        out_shape=[jax.ShapeDtypeStruct(rows, jnp.float32), jax.ShapeDtypeStruct(rows, jnp.bfloat16)],
-        in_specs=[pl.BlockSpec(memory_space=pltpu.SMEM), vmem] + [hbm] * (3 + len(pieces)),
-        out_specs=[vmem, vmem],
-        scratch_shapes=[
-            pltpu.VMEM((bins,) + own.shape[1:], jnp.bfloat16),
-            pltpu.VMEM((bins,) + own.shape[1:], jnp.bfloat16),
-            pltpu.VMEM(near.shape[1:], jnp.float32),
-            pltpu.VMEM((1, bins) + own.shape[1:], jnp.bfloat16),
-        ]
+        functools.partial(far_kernel, len(pieces)),
+        grid=(STEPS,),
+        out_shape=[
+            jax.ShapeDtypeStruct((STEPS,) + rows, jnp.float32),
+            jax.ShapeDtypeStruct((STEPS,) + rows, jnp.bfloat16),
+        ],
+        in_specs=[pl.BlockSpec(memory_space=pltpu.SMEM), pl.BlockSpec(v.shape, lambda s: (0, 0))]
+        + [hbm] * 3
+        + [step_block(a.shape[1:]) for a in [near] + pieces],
+        out_specs=[step_block(rows)] * 2,
+        scratch_shapes=[pltpu.VMEM((bins,) + a.shape[1:], jnp.bfloat16) for a in (own,) + across]
         + [pltpu.VMEM((64 * (bins + 8), 128), jnp.float32)] * 2
-        + [
-            pltpu.SemaphoreType.DMA((2 * bins,)),
-            pltpu.SemaphoreType.DMA,
-            pltpu.SemaphoreType.DMA((len(pieces),)),
-        ],
+        + [pltpu.SemaphoreType.DMA((3 * bins,))],
         compiler_params=pltpu.CompilerParams(vmem_limit_bytes=VMEM_BYTES),
         name="far",
-    )(slots, v, own, across, near, *pieces)
-
-
-def expand_kernel(step, u_ref, keep_ref, got_ref, *refs):
-    out_ref, lags_ref, sem = refs[-3:]
-    count = keep_ref.shape[0]
+    )(slots, v, own, *across, near, *pieces)
+
+
+def expand_kernel(u_ref, keep_ref, got_ref, out_ref):
+    count = keep_ref.shape[1]
     results = []
     for n in range(0, count, 2):
-        value = jnp.concatenate([keep_ref[b] + got_ref[b].astype(jnp.float32) for b in (n, n + 1)], axis=1)
+        value = jnp.concatenate([keep_ref[0, b] + got_ref[0, b].astype(jnp.float32) for b in (n, n + 1)], axis=1)
         high = value.astype(jnp.bfloat16)
         low = (value - high.astype(jnp.float32)).astype(jnp.bfloat16)
         results.append(
             jnp.dot(u_ref[...], jnp.concatenate([high, high, low], axis=0), preferred_element_type=jnp.float32)
         )
     for n, lags in enumerate(results):
-        lags_ref[pl.ds(2 * n, LAGS, stride=count), :] = lags[:LAGS, :128]
-        lags_ref[pl.ds(2 * n + 1, LAGS, stride=count), :] = lags[:LAGS, 128:]
-    copy = pltpu.make_async_copy(lags_ref, out_ref.at[step], sem)
-    copy.start()
-    copy.wait()
-
-
-def expand(step, u, keep, got, before):
-    vmem = pl.BlockSpec(memory_space=pltpu.VMEM)
-    hbm = pl.BlockSpec(memory_space=pl.ANY)
-    shape = (LAGS * keep.shape[0], 128)
-    held = [] if before is None else [before]
+        out_ref[0, pl.ds(2 * n, LAGS, stride=count), :] = lags[:LAGS, :128]
+        out_ref[0, pl.ds(2 * n + 1, LAGS, stride=count), :] = lags[:LAGS, 128:]
+
+
+def expand(u, keep, got):
+    shape = (LAGS * keep.shape[1], 128)
     return pl.pallas_call(
-        functools.partial(expand_kernel, step),
+        expand_kernel,
+        grid=(STEPS,),
         out_shape=jax.ShapeDtypeStruct((STEPS,) + shape, jnp.float32),
-        in_specs=[vmem] * 3 + [hbm] * len(held),
-        out_specs=hbm,
-        scratch_shapes=[pltpu.VMEM(shape, jnp.float32), pltpu.SemaphoreType.DMA],
-        input_output_aliases={3: 0} if held else {},
+        in_specs=[pl.BlockSpec(u.shape, lambda s: (0, 0)), step_block(keep.shape[1:]), step_block(got.shape[1:])],
+        out_specs=step_block(shape),
         compiler_params=pltpu.CompilerParams(vmem_limit_bytes=VMEM_BYTES),
         name="expand",
-    )(u, keep, got, *held)
+    )(u, keep, got)
 
 
 def place(x, z, y):
@@ -355,17 +356,30 @@
     return lax.ppermute(value, "chan", pairs)
 
 
-def around(value, axis):
-    return [value] + [shift(value, **{axis: step}) for step in (1, -1, 2)]
-
-
-def gather_references(parts):
-    other = shift(parts, dy=1)
-    first = jnp.concatenate([parts[:, :2], other[:, :2]], axis=1)
-    second = jnp.concatenate([parts[:, 2:], other[:, 2:]], axis=1)
-    plane_a = jnp.concatenate(around(first, "dz"), axis=1)
-    plane_b = jnp.concatenate(around(second, "dx"), axis=1)
-    return plane_a, plane_b
+def plane(own, axis):
+    ahead, behind, far = [shift(own, **{axis: step}) for step in (1, -1, 2)]
+    return jnp.stack([jnp.concatenate([own, ahead], axis=1), jnp.concatenate([behind, far], axis=1)])
+
+
+def gather_planes(parts):
+    pairs = [(4 * c + t, 4 * (c ^ 1) + (t ^ 2)) for c in range(32) for t in range(4)]
+    middle, columns = parts.shape[2] // 2, parts.shape[3] // 2
+    lower = lax.axis_index("tm") < 2
+    sides = parts[..., :columns], parts[..., columns:]
+
+    def packed(side):
+        return jnp.concatenate([side[:, :, :middle], side[:, :, middle:]], axis=3)
+
+    mine = packed(jnp.where(lower, sides[0], sides[1]))
+    theirs = packed(jnp.where(lower, sides[1], sides[0]))
+    beside = shift(mine, dy=1)
+    beyond = from_other_chip(theirs)
+    across = lax.ppermute(theirs, ("chan", "tm"), pairs)
+    own = jnp.concatenate([mine, beyond], axis=2)
+    other = jnp.concatenate([beside, across], axis=2)
+    first = jnp.concatenate([own[:, :2], other[:, :2]], axis=1)
+    second = jnp.concatenate([own[:, 2:], other[:, 2:]], axis=1)
+    return lax.optimization_barrier((first, second))
 
 
 def plane_slots(last):
@@ -385,15 +399,6 @@
 
 def from_other_chip(value):
     return lax.ppermute(value, "tm", [(0, 2), (2, 0), (1, 3), (3, 1)])
-
-
-def windows_of_both_chips(parts):
-    got = from_other_chip(parts)
-    lower = lax.axis_index("tm") < 2
-    middle = parts.shape[-1] // 2
-    own = jnp.where(lower, parts, jnp.roll(parts, middle, axis=-1))
-    other = jnp.where(lower, jnp.roll(got, middle, axis=-1), got)
-    return jnp.where(jnp.arange(parts.shape[-1]) < middle, own, other)
 
 
 def basis_columns(windows, slots):
@@ -422,38 +427,33 @@
     u = jnp.asarray(np.concatenate([high, low, high], axis=1))
     tables = (slots[:near_bins], jnp.concatenate([slots[near_bins:], core]), v(0, near_bins), v(near_bins, BINS))
     everyone = lax.all_to_all(own.reshape((32, 4) + own.shape[1:]), "chan", 0, 0)
-    everyone, tables = lax.optimization_barrier((everyone, tables))
+    middle = own.shape[1] // 2
+    leaving = own[:, :middle], own[:, middle:]
+    everyone, tables, leaving = lax.optimization_barrier((everyone, tables, leaving))
+    upper = from_other_chip(leaving[0])
     near_slots, far_slots, near_v, far_v = tables
     roots = owner_table[plan]
     parts = jnp.stack([lax.dynamic_index_in_dim(everyone, roots[s], 0, keepdims=False) for s in range(STEPS)])
-    parts, own = lax.optimization_barrier((parts, own))
-    across = from_other_chip(own)
-    plane_a, plane_b = gather_references(windows_of_both_chips(parts))
+    first, second = gather_planes(parts)
+    plane_a, plane_b = plane(first, "dz"), plane(second, "dx")
+    plane_a, plane_b, upper, lower = lax.optimization_barrier((plane_a, plane_b, upper, leaving[1]))
+    across = upper, from_other_chip(lower)
     near = [
         shift(plane_a, dx=1),
         shift(plane_b, dz=1),
         shift(plane_a, dx=-1),
         shift(plane_b, dz=-1),
     ]
-    near = lax.optimization_barrier(near)
-    half = plane_a.shape[1] // 2
     far = [
-        shift(near[0][:, :half], dx=1),
-        shift(near[2][:, half:], dx=-1),
-        shift(near[1][:, :half], dz=1),
-        shift(near[3][:, half:], dz=-1),
+        shift(near[0][0], dx=1),
+        shift(near[2][1], dx=-1),
+        shift(near[1][0], dz=1),
+        shift(near[3][1], dz=-1),
     ]
     partial = near_coefficients(own, across, [plane_a, plane_b] + near, near_slots, near_v)
     far, partial = lax.optimization_barrier((far, partial))
-    keep, got = [None] * STEPS, [None] * STEPS
-    for s in range(STEPS):
-        keep[s], send = all_coefficients(s, own, across, partial, far, far_slots, far_v)
-        got[s] = from_other_core(send)
-        if s + 1 < STEPS:
-            partial, _ = lax.optimization_barrier((partial, send))
-    out = None
-    for s in range(STEPS):
-        out = expand(s, u, keep[s], got[s], out)
+    keep, send = all_coefficients(own, across, partial, far, far_slots, far_v)
+    out = expand(u, keep, from_other_core(send))
     return out.reshape(STEPS, LAGS, 32, 128).transpose(2, 0, 1, 3)
 
 

time: 204 us -> 197 us (0.966)
  starting transfers between devices: 25.4 us -> 38.7 us
  Pallas kernels: 54.6 us -> 43.6 us
  waiting for transfers between devices: 100 us -> 89.1 us
  local copies, waits for them, and re-layouts: 12.7 us -> 15 us
    ppermute x15, waiting for transfers between devices: 50.9 us -> 34.2 us  [shift(): return lax.ppermute(value, 'chan', pairs)]
    pallas_call x6 -> x2, Pallas kernels: 27.9 us -> 17.3 us  [the longest x1 10.4 us: all_coefficients(): pl.pallas_call(functools.partial(far_kernel, len(pieces)), grid=(STEPS,),...]
    ppermute x15, starting transfers between devices: 11.4 us -> 16.6 us  [shift(): return lax.ppermute(value, 'chan', pairs)]
    ppermute x2 -> x3, starting transfers between devices: 0.09 us -> 3.82 us  [from_other_chip(): return lax.ppermute(value, 'tm', [(0, 2), (2, 0), (1, 3), (3, 1)])]
    squeeze x0 -> x4, local copies, waits for them, and re-layouts: none -> 3.69 us  [the longest x1 0.94 us: shards(): near[2][1]]
    ppermute x0 -> x1, waiting for transfers between devices: none -> 3.36 us  [gather_planes(): across = lax.ppermute(theirs, ('chan', 'tm'), pairs)]
    ppermute x3 -> x1, waiting for transfers between devices: 0.01 us -> 2.68 us  [from_other_core(): return lax.ppermute(value, 'tm', [(0, 1), (1, 0), (2, 3), (3, 2)])]
    all_to_all x1, waiting for transfers between devices: 28.9 us -> 26.6 us  [shards(): lax.all_to_all(own.reshape((32, 4) + own.shape[1:]), 'chan', 0, 0)]
  transfers between devices with their start and end apart: 22 -> 22, of which waited for: 9 -> 13; matrix products, arithmetic and copies ran while one was open for 4% -> 6% of each run, Pallas kernels for 17% -> 8%
where the time goes in v4:
time: 197 us; the launch traced here: 196 us
  waiting for transfers between devices  89.1 us (45%)
  Pallas kernels  43.6 us (22%)
  starting transfers between devices  38.7 us (20%)
  local copies, waits for them, and re-layouts  15 us (8%)
  between operations  6.37 us (3%)
  other arithmetic  3.04 us (2%)
    ppermute x15, waiting for transfers between devices, shift(): return lax.ppermute(value, 'chan', pairs)  34.2 us
    all_to_all x1, waiting for transfers between devices, shards(): lax.all_to_all(own.reshape((32, 4) + own.shape[1:]), 'chan', 0, 0)  26.6 us
    ppermute x3, waiting for transfers between devices, from_other_chip(): return lax.ppermute(value, 'tm', [(0, 2), (2, 0), (1, 3), (3, 1)])  16.7 us
    ppermute x15, starting transfers between devices, shift(): return lax.ppermute(value, 'chan', pairs)  16.6 us
    pallas_call x1, Pallas kernels, near_coefficients(): pl.pallas_call(functools.partial(near_kernel, len(pieces)), grid=(STEPS,)...  15.2 us
    pallas_call x1, Pallas kernels, whitened_spectra(): pl.pallas_call(functools.partial(spectra_kernel, GROUP), grid=(windows //...  11 us
    pallas_call x1, Pallas kernels, all_coefficients(): pl.pallas_call(functools.partial(far_kernel, len(pieces)), grid=(STEPS,),...  10.4 us
    all_to_all x1, starting transfers between devices, shards(): lax.all_to_all(own.reshape((32, 4) + own.shape[1:]), 'chan', 0, 0)  9.05 us
  transfers between devices with their start and end apart: 22, of which 13 were waited for; matrix products, arithmetic and copies ran while one was open for 6% of the time, Pallas kernels for 8%

profile of v4, /device:TPU:1, one launch (start us, length us, event | category | flops | bytes accessed | tf_op | source)
XLA Modules:
  0.0 196.0 jit_solution(3441925497272490528)
XLA Ops:
  0.9 3.3 %collective-permute-start = (bf16[128,512]{1,0:T(8,128)(2,1)S(1)}, bf16[128,512]{1,0:T(8,128)(2,1)S(1)}, u32[]{:S(2)}, u32[]{:S(2)}) collective-permute-start(bf16[128,512]{1,0:T(8,128)(2,1)S(1)} %slice.76), channel_id=1, source_target_pairs={{1,0},{2,1},{3,2},{5,4},{6,5},{7,6},{9,8},{10,9},{11,10},{13,12},{... | collective-permute-start | bytes 393224 | tf_op jit(solution)/shard_map/ppermute | solution.py:418
  4.3 5.5 %collective-permute-done.edge_ref = bf16[128,512]{1,0:T(8,128)(2,1)S(1)} collective-permute-done((bf16[128,512]{1,0:T(8,128)(2,1)S(1)}, bf16[128,512]{1,0:T(8,128)(2,1)S(1)}, u32[]{:S(2)}, u32[]{:S(2)}) %collective-permute-start) | collective-permute-done | bytes 131104 | tf_op jit(solution)/shard_map/ppermute | solution.py:418
  10.4 11.0 %spectra.1.own_ref.own_hbm = bf16[128,96,128]{2,1,0:T(8,128)(2,1)} custom-call(bf16[128,24576]{1,0:T(8,128)(2,1)} %next_ref.1, bf16[128,24576]{1,0:T(8,128)(2,1)} %next_ref.1, bf16[128,512]{1,0:T(8,128)(2,1)} %copy-done.16, bf16[256,1024]{1,0:T(8,128)(2,1)} %constant.221.clone.table_ref, bf16[128,256]{1,0:T(8,128)(2,1)} %constant.222.clone.band_ref, ...), custom_call_target="tpu_custom_call" | custom-call | tf_op jit(solution)/shard_map/spectra/pallas_call | solution.py:152
  21.6 9.1 %all-to-all-start = ((bf16[32,4,96,128]{3,2,1,0:T(8,128)(2,1)}), bf16[32,4,96,128]{3,2,1,0:T(8,128)(2,1)}, u32[]{:S(2)}, u32[]{:S(2)}) async-start(bf16[32,4,96,128]{3,2,1,0:T(8,128)(2,1)} %bitcast.31), calls=%async_computation | async-start | bytes 6291456 | tf_op jit(solution)/shard_map/all_to_all | solution.py:429
  41.0 2.3 %fusion.8 = (bf16[128,48,128]{2,1,0:T(8,128)(2,1)}, bf16[128,48,128]{2,1,0:T(8,128)(2,1)}) fusion(bf16[128,96,128]{2,1,0:T(8,128)(2,1)S(1)} %copy-done.1), kind=kLoop, calls=%fused_computation.56 | loop fusion | bytes 6291456 | tf_op jit(solution)/shard_map/slice | solution.py:431
  43.3 26.6 %all-to-all-done = bf16[32,4,96,128]{3,2,1,0:T(8,128)(2,1)} async-done(((bf16[32,4,96,128]{3,2,1,0:T(8,128)(2,1)}), bf16[32,4,96,128]{3,2,1,0:T(8,128)(2,1)}, u32[]{:S(2)}, u32[]{:S(2)}) %all-to-all-start) | async-done | bytes 3145760 | tf_op jit(solution)/shard_map/all_to_all | solution.py:429
  78.9 3.4 %collective-permute-done.3 = bf16[3,4,48,128]{3,2,1,0:T(8,128)(2,1)S(1)} collective-permute-done((bf16[3,4,48,128]{3,2,1,0:T(8,128)(2,1)S(1)}, bf16[3,4,48,128]{3,2,1,0:T(8,128)(2,1)S(1)}, u32[]{:S(2)}, u32[]{:S(2)}) %collective-permute-start.3) | collective-permute-done | bytes 147488 | tf_op jit(solution)/shard_map/ppermute | solution.py:377
  83.1 2.0 collective-permute-start.8
  85.7 6.7 %collective-permute-done.7 = bf16[3,4,96,128]{3,2,1,0:T(8,128)(2,1)S(1)} collective-permute-done((bf16[3,4,96,128]{3,2,1,0:T(8,128)(2,1)S(1)}, bf16[3,4,96,128]{3,2,1,0:T(8,128)(2,1)S(1)}, u32[]{:S(2)}, u32[]{:S(2)}) %collective-permute-start.7) | collective-permute-done | bytes 294944 | tf_op jit(solution)/shard_map/ppermute | solution.py:356
  93.9 3.2 %collective-permute-done.9 = bf16[3,4,96,128]{3,2,1,0:T(8,128)(2,1)S(1)} collective-permute-done((bf16[3,4,96,128]{3,2,1,0:T(8,128)(2,1)S(1)}, bf16[3,4,96,128]{3,2,1,0:T(8,128)(2,1)S(1)}, u32[]{:S(2)}, u32[]{:S(2)}) %collective-permute-start.9) | collective-permute-done | bytes 294944 | tf_op jit(solution)/shard_map/ppermute | solution.py:356
  98.4 2.7 %collective-permute-done.6 = bf16[3,4,96,128]{3,2,1,0:T(8,128)(2,1)S(1)} collective-permute-done((bf16[3,4,96,128]{3,2,1,0:T(8,128)(2,1)S(1)}, bf16[3,4,96,128]{3,2,1,0:T(8,128)(2,1)S(1)}, u32[]{:S(2)}, u32[]{:S(2)}) %collective-permute-start.6) | collective-permute-done | bytes 294944 | tf_op jit(solution)/shard_map/ppermute | solution.py:356
  101.4 11.2 %collective-permute-done.10.upper_ref.upper_hbm = bf16[128,48,128]{2,1,0:T(8,128)(2,1)S(1)} collective-permute-done((bf16[128,48,128]{2,1,0:T(8,128)(2,1)S(1)}, bf16[128,48,128]{2,1,0:T(8,128)(2,1)S(1)}, u32[]{:S(2)}, u32[]{:S(2)}) %collective-permute-start.10) | collective-permute-done | bytes 1572896 | tf_op jit(solution)/shard_map/ppermute | solution.py:401
  113.4 2.1 %collective-permute-start.14 = (bf16[2,3,8,96,128]{4,3,2,1,0:T(8,128)(2,1)S(1)}, bf16[2,3,8,96,128]{4,3,2,1,0:T(8,128)(2,1)S(1)}, u32[]{:S(2)}, u32[]{:S(2)}) collective-permute-start(bf16[2,3,8,96,128]{4,3,2,1,0:T(8,128)(2,1)S(1)} %pad_maximum_fusion.refs_0_), channel_id=1, source_target_pairs={{0,96},{4,100},{8,104},{12,108},{16,112},{20,116},{24,120},{28,124... | collective-permute-start | bytes 3538952 | tf_op jit(solution)/shard_map/ppermute | solution.py:356
  116.1 2.1 %collective-permute-start.18 = (bf16[2,3,8,96,128]{4,3,2,1,0:T(8,128)(2,1)S(1)}, bf16[2,3,8,96,128]{4,3,2,1,0:T(8,128)(2,1)S(1)}, u32[]{:S(2)}, u32[]{:S(2)}) collective-permute-start(bf16[2,3,8,96,128]{4,3,2,1,0:T(8,128)(2,1)S(1)} %pad_maximum_fusion.1.refs_1_), channel_id=1, source_target_pairs={{0,24},{4,28},{8,0},{12,4},{16,8},{20,12},{24,16},{28,20},{32,56},... | collective-permute-start | bytes 3538952 | tf_op jit(solution)/shard_map/ppermute | solution.py:356
  118.2 2.4 %collective-permute-start.11 = (bf16[128,48,128]{2,1,0:T(8,128)(2,1)S(1)}, bf16[128,48,128]{2,1,0:T(8,128)(2,1)S(1)}, u32[]{:S(2)}, u32[]{:S(2)}) collective-permute-start(bf16[128,48,128]{2,1,0:T(8,128)(2,1)S(1)} %copy-done.10), channel_id=1, source_target_pairs={{0,2},{2,0},{1,3},{3,1},{4,6},{6,4},{5,7},{7,5},{8,10},{10,8},{9,1... | collective-permute-start | bytes 4718600 | tf_op jit(solution)/shard_map/ppermute | solution.py:401
  120.6 18.8 %collective-permute-done.12.refs_2_ = bf16[2,3,8,96,128]{4,3,2,1,0:T(8,128)(2,1)S(1)} collective-permute-done((bf16[2,3,8,96,128]{4,3,2,1,0:T(8,128)(2,1)S(1)}, bf16[2,3,8,96,128]{4,3,2,1,0:T(8,128)(2,1)S(1)}, u32[]{:S(2)}, u32[]{:S(2)}) %collective-permute-start.12) | collective-permute-done | bytes 1179680 | tf_op jit(solution)/shard_map/ppermute | solution.py:356
  141.3 2.7 %collective-permute-start.15 = (bf16[3,8,96,128]{3,2,1,0:T(8,128)(2,1)}, bf16[3,8,96,128]{3,2,1,0:T(8,128)(2,1)}, u32[]{:S(2)}, u32[]{:S(2)}) collective-permute-start(bf16[3,8,96,128]{3,2,1,0:T(8,128)(2,1)} %slice_bitcast_fusion.2), channel_id=1, source_target_pairs={{0,96},{4,100},{8,104},{12,108},{16,112},{20,116},{24,120},{28,124... | collective-permute-start | bytes 1769480 | tf_op jit(solution)/shard_map/ppermute | solution.py:356
  146.9 1.9 collective-permute-start.19
  148.8 3.7 %collective-permute-done.11.lower_ref.lower_hbm = bf16[128,48,128]{2,1,0:T(8,128)(2,1)S(1)} collective-permute-done((bf16[128,48,128]{2,1,0:T(8,128)(2,1)S(1)}, bf16[128,48,128]{2,1,0:T(8,128)(2,1)S(1)}, u32[]{:S(2)}, u32[]{:S(2)}) %collective-permute-start.11) | collective-permute-done | bytes 1572896 | tf_op jit(solution)/shard_map/ppermute | solution.py:401
  153.7 15.2 %near.1.near_ref = f32[3,64,48,128]{3,2,1,0:T(8,128)} custom-call(s32[96]{0:T(128)} %concatenate.47.slots_ref, bf16[96,192]{1,0:T(8,128)(2,1)} %pad_maximum_fusion.8.v_ref, bf16[128,96,128]{2,1,0:T(8,128)(2,1)} %spectra.1.own_ref.own_hbm, bf16[128,48,128]{2,1,0:T(8,128)(2,1)} %copy-done.2, bf16[128,48,128]{2,1,0:T(8,128)(2,1)} %copy-done.3, ...), custom_call_target="tpu_custom_call" | custom-call | tf_op jit(solution)/shard_map/near/pallas_call | solution.py:285
  170.7 10.4 %far.1 = (f32[3,32,48,128]{3,2,1,0:T(8,128)}, bf16[3,32,48,128]{3,2,1,0:T(8,128)(2,1)}) custom-call(s32[33]{0:T(128)} %pad_add_fusion.slots_ref, bf16[96,64]{1,0:T(8,128)(2,1)} %pad_maximum_fusion.9.v_ref, bf16[128,96,128]{2,1,0:T(8,128)(2,1)} %spectra.1.own_ref.own_hbm, bf16[128,48,128]{2,1,0:T(8,128)(2,1)} %copy-done.2, bf16[128,48,128]{2,1,0:T(8,128)(2,1)} %copy-done.3, ...), custom_call_target="tpu_custom_call" | custom-call | tf_op jit(solution)/shard_map/far/pallas_call | solution.py:303
  181.2 4.1 %collective-permute-start.20 = (bf16[3,32,48,128]{3,2,1,0:T(8,128)(2,1)}, bf16[3,32,48,128]{3,2,1,0:T(8,128)(2,1)S(1)}, u32[]{:S(2)}, u32[]{:S(2)}) collective-permute-start(bf16[3,32,48,128]{3,2,1,0:T(8,128)(2,1)} %get-tuple-element.44), channel_id=1, source_target_pairs={{0,1},{1,0},{2,3},{3,2},{4,5},{5,4},{6,7},{7,6},{8,9},{9,8},{10,11... | collective-permute-start | bytes 3538952 | tf_op jit(solution)/shard_map/ppermute | solution.py:397
  185.3 2.7 %collective-permute-done.20.got_ref = bf16[3,32,48,128]{3,2,1,0:T(8,128)(2,1)S(1)} collective-permute-done((bf16[3,32,48,128]{3,2,1,0:T(8,128)(2,1)}, bf16[3,32,48,128]{3,2,1,0:T(8,128)(2,1)S(1)}, u32[]{:S(2)}, u32[]{:S(2)}) %collective-permute-start.20) | collective-permute-done | bytes 1179680 | tf_op jit(solution)/shard_map/ppermute | solution.py:397
  189.1 6.9 %expand.1 = f32[3,3232,128]{2,1,0:T(8,128)} custom-call(bf16[104,144]{1,0:T(8,128)(2,1)} %constant.229.clone.u_ref, f32[3,32,48,128]{3,2,1,0:T(8,128)} %get-tuple-element.43.keep_ref, bf16[3,32,48,128]{3,2,1,0:T(8,128)(2,1)} %copy-done.12), custom_call_target="tpu_custom_call" | custom-call | tf_op jit(solution)/shard_map/expand/pallas_call | solution.py:339
  (110 shorter events, 29.5 us)
Async XLA Ops:
  0.0 30.8 %copy-start = (s32[32]{0:T(128)S(1)}, s32[32]{0:T(128)}, u32[]{:S(2)}) copy-start(s32[32]{0:T(128)} %param.23) | copy-start | bytes 388
  0.9 8.9 %collective-permute-start = (bf16[128,512]{1,0:T(8,128)(2,1)S(1)}, bf16[128,512]{1,0:T(8,128)(2,1)S(1)}, u32[]{:S(2)}, u32[]{:S(2)}) collective-permute-start(bf16[128,512]{1,0:T(8,128)(2,1)S(1)} %slice.76), channel_id=1, source_target_pairs={{1,0},{2,1},{3,2},{5,4},{6,5},{7,6},{9,8},{10,9},{11,10},{13,12},{... | collective-permute-start | bytes 393224 | tf_op jit(solution)/shard_map/ppermute | solution.py:418
  21.6 48.3 %all-to-all-start = ((bf16[32,4,96,128]{3,2,1,0:T(8,128)(2,1)}), bf16[32,4,96,128]{3,2,1,0:T(8,128)(2,1)}, u32[]{:S(2)}, u32[]{:S(2)}) async-start(bf16[32,4,96,128]{3,2,1,0:T(8,128)(2,1)} %bitcast.31), calls=%async_computation | async-start | bytes 6291456 | tf_op jit(solution)/shard_map/all_to_all | solution.py:429
  71.3 6.1 %collective-permute-start.1 = (bf16[3,4,48,128]{3,2,1,0:T(8,128)(2,1)S(1)}, bf16[3,4,48,128]{3,2,1,0:T(8,128)(2,1)S(1)}, u32[]{:S(2)}, u32[]{:S(2)}) collective-permute-start(bf16[3,4,48,128]{3,2,1,0:T(8,128)(2,1)S(1)} %pad_maximum_fusion.7), channel_id=1, source_target_pairs={{0,2},{2,0},{1,3},{3,1},{4,6},{6,4},{5,7},{7,5},{8,10},{10,8},{9,1... | collective-permute-start | bytes 442376 | tf_op jit(solution)/shard_map/ppermute | solution.py:401
  71.3 10.9 %collective-permute-start.3 = (bf16[3,4,48,128]{3,2,1,0:T(8,128)(2,1)S(1)}, bf16[3,4,48,128]{3,2,1,0:T(8,128)(2,1)S(1)}, u32[]{:S(2)}, u32[]{:S(2)}) collective-permute-start(bf16[3,4,48,128]{3,2,1,0:T(8,128)(2,1)S(1)} %pad_maximum_fusion.7), channel_id=1, source_target_pairs={{0,6},{1,7},{2,4},{3,5},{4,2},{5,3},{6,0},{7,1},{8,14},{9,15},{10,... | collective-permute-start | bytes 442376 | tf_op jit(solution)/shard_map/ppermute | solution.py:377
  73.3 5.5 %collective-permute-start.2 = (bf16[3,4,48,128]{3,2,1,0:T(8,128)(2,1)S(1)}, bf16[3,4,48,128]{3,2,1,0:T(8,128)(2,1)S(1)}, u32[]{:S(2)}, u32[]{:S(2)}) collective-permute-start(bf16[3,4,48,128]{3,2,1,0:T(8,128)(2,1)S(1)} %pad_maximum_fusion.6), channel_id=1, source_target_pairs={{0,4},{4,0},{8,12},{12,8},{16,20},{20,16},{24,28},{28,24},{32,36},... | collective-permute-start | bytes 442376 | tf_op jit(solution)/shard_map/ppermute | solution.py:356
  74.2 38.5 %collective-permute-start.10 = (bf16[128,48,128]{2,1,0:T(8,128)(2,1)S(1)}, bf16[128,48,128]{2,1,0:T(8,128)(2,1)S(1)}, u32[]{:S(2)}, u32[]{:S(2)}) collective-permute-start(bf16[128,48,128]{2,1,0:T(8,128)(2,1)S(1)} %copy-done.11), channel_id=1, source_target_pairs={{0,2},{2,0},{1,3},{3,1},{4,6},{6,4},{5,7},{7,5},{8,10},{10,8},{9,1... | collective-permute-start | bytes 4718600 | tf_op jit(solution)/shard_map/ppermute | solution.py:401
  82.4 10.1 %collective-permute-start.7 = (bf16[3,4,96,128]{3,2,1,0:T(8,128)(2,1)S(1)}, bf16[3,4,96,128]{3,2,1,0:T(8,128)(2,1)S(1)}, u32[]{:S(2)}, u32[]{:S(2)}) collective-permute-start(bf16[3,4,96,128]{3,2,1,0:T(8,128)(2,1)S(1)} %get-tuple-element.29), channel_id=1, source_target_pairs={{0,32},{4,36},{8,40},{12,44},{16,48},{20,52},{24,56},{28,60},{32,6... | collective-permute-start | bytes 884744 | tf_op jit(solution)/shard_map/ppermute | solution.py:356
  83.1 10.6 %collective-permute-start.4 = (bf16[3,4,96,128]{3,2,1,0:T(8,128)(2,1)S(1)}, bf16[3,4,96,128]{3,2,1,0:T(8,128)(2,1)S(1)}, u32[]{:S(2)}, u32[]{:S(2)}) collective-permute-start(bf16[3,4,96,128]{3,2,1,0:T(8,128)(2,1)S(1)} %get-tuple-element.28), channel_id=1, source_target_pairs={{0,8},{4,12},{8,16},{12,20},{16,24},{20,28},{24,0},{28,4},{32,40},... | collective-permute-start | bytes 884744 | tf_op jit(solution)/shard_map/ppermute | solution.py:356
  83.1 10.7 %collective-permute-start.8 = (bf16[3,4,96,128]{3,2,1,0:T(8,128)(2,1)S(1)}, bf16[3,4,96,128]{3,2,1,0:T(8,128)(2,1)S(1)}, u32[]{:S(2)}, u32[]{:S(2)}) collective-permute-start(bf16[3,4,96,128]{3,2,1,0:T(8,128)(2,1)S(1)} %get-tuple-element.29), channel_id=1, source_target_pairs={{0,96},{4,100},{8,104},{12,108},{16,112},{20,116},{24,120},{28,124... | collective-permute-start | bytes 884744 | tf_op jit(solution)/shard_map/ppermute | solution.py:356
  85.1 12.0 %collective-permute-start.9 = (bf16[3,4,96,128]{3,2,1,0:T(8,128)(2,1)S(1)}, bf16[3,4,96,128]{3,2,1,0:T(8,128)(2,1)S(1)}, u32[]{:S(2)}, u32[]{:S(2)}) collective-permute-start(bf16[3,4,96,128]{3,2,1,0:T(8,128)(2,1)S(1)} %get-tuple-element.29), channel_id=1, source_target_pairs={{0,64},{4,68},{8,72},{12,76},{16,80},{20,84},{24,88},{28,92},{32,9... | collective-permute-start | bytes 884744 | tf_op jit(solution)/shard_map/ppermute | solution.py:356
  92.5 5.9 %collective-permute-start.5 = (bf16[3,4,96,128]{3,2,1,0:T(8,128)(2,1)S(1)}, bf16[3,4,96,128]{3,2,1,0:T(8,128)(2,1)S(1)}, u32[]{:S(2)}, u32[]{:S(2)}) collective-permute-start(bf16[3,4,96,128]{3,2,1,0:T(8,128)(2,1)S(1)} %get-tuple-element.28), channel_id=1, source_target_pairs={{0,24},{4,28},{8,0},{12,4},{16,8},{20,12},{24,16},{28,20},{32,56},... | collective-permute-start | bytes 884744 | tf_op jit(solution)/shard_map/ppermute | solution.py:356
  93.7 7.4 %collective-permute-start.6 = (bf16[3,4,96,128]{3,2,1,0:T(8,128)(2,1)S(1)}, bf16[3,4,96,128]{3,2,1,0:T(8,128)(2,1)S(1)}, u32[]{:S(2)}, u32[]{:S(2)}) collective-permute-start(bf16[3,4,96,128]{3,2,1,0:T(8,128)(2,1)S(1)} %get-tuple-element.28), channel_id=1, source_target_pairs={{0,16},{4,20},{8,24},{12,28},{16,0},{20,4},{24,8},{28,12},{32,48},... | collective-permute-start | bytes 884744 | tf_op jit(solution)/shard_map/ppermute | solution.py:356
  101.4 45.4 %copy-start.5 = (bf16[2,3,8,96,128]{4,3,2,1,0:T(8,128)(2,1)}, bf16[2,3,8,96,128]{4,3,2,1,0:T(8,128)(2,1)S(1)}, u32[]{:S(2)}) copy-start(bf16[2,3,8,96,128]{4,3,2,1,0:T(8,128)(2,1)S(1)} %pad_maximum_fusion.refs_0_) | copy-start | bytes 3538948
  112.7 26.8 %collective-permute-start.12 = (bf16[2,3,8,96,128]{4,3,2,1,0:T(8,128)(2,1)S(1)}, bf16[2,3,8,96,128]{4,3,2,1,0:T(8,128)(2,1)S(1)}, u32[]{:S(2)}, u32[]{:S(2)}) collective-permute-start(bf16[2,3,8,96,128]{4,3,2,1,0:T(8,128)(2,1)S(1)} %pad_maximum_fusion.refs_0_), channel_id=1, source_target_pairs={{0,32},{4,36},{8,40},{12,44},{16,48},{20,52},{24,56},{28,60},{32,6... | collective-permute-start | bytes 3538952 | tf_op jit(solution)/shard_map/ppermute | solution.py:356
  113.4 27.0 %collective-permute-start.14 = (bf16[2,3,8,96,128]{4,3,2,1,0:T(8,128)(2,1)S(1)}, bf16[2,3,8,96,128]{4,3,2,1,0:T(8,128)(2,1)S(1)}, u32[]{:S(2)}, u32[]{:S(2)}) collective-permute-start(bf16[2,3,8,96,128]{4,3,2,1,0:T(8,128)(2,1)S(1)} %pad_maximum_fusion.refs_0_), channel_id=1, source_target_pairs={{0,96},{4,100},{8,104},{12,108},{16,112},{20,116},{24,120},{28,124... | collective-permute-start | bytes 3538952 | tf_op jit(solution)/shard_map/ppermute | solution.py:356
  115.5 28.5 %collective-permute-start.16 = (bf16[2,3,8,96,128]{4,3,2,1,0:T(8,128)(2,1)S(1)}, bf16[2,3,8,96,128]{4,3,2,1,0:T(8,128)(2,1)S(1)}, u32[]{:S(2)}, u32[]{:S(2)}) collective-permute-start(bf16[2,3,8,96,128]{4,3,2,1,0:T(8,128)(2,1)S(1)} %pad_maximum_fusion.1.refs_1_), channel_id=1, source_target_pairs={{0,8},{4,12},{8,16},{12,20},{16,24},{20,28},{24,0},{28,4},{32,40},... | collective-permute-start | bytes 3538952 | tf_op jit(solution)/shard_map/ppermute | solution.py:356
  116.1 29.8 %collective-permute-start.18 = (bf16[2,3,8,96,128]{4,3,2,1,0:T(8,128)(2,1)S(1)}, bf16[2,3,8,96,128]{4,3,2,1,0:T(8,128)(2,1)S(1)}, u32[]{:S(2)}, u32[]{:S(2)}) collective-permute-start(bf16[2,3,8,96,128]{4,3,2,1,0:T(8,128)(2,1)S(1)} %pad_maximum_fusion.1.refs_1_), channel_id=1, source_target_pairs={{0,24},{4,28},{8,0},{12,4},{16,8},{20,12},{24,16},{28,20},{32,56},... | collective-permute-start | bytes 3538952 | tf_op jit(solution)/shard_map/ppermute | solution.py:356
  118.2 34.2 %collective-permute-start.11 = (bf16[128,48,128]{2,1,0:T(8,128)(2,1)S(1)}, bf16[128,48,128]{2,1,0:T(8,128)(2,1)S(1)}, u32[]{:S(2)}, u32[]{:S(2)}) collective-permute-start(bf16[128,48,128]{2,1,0:T(8,128)(2,1)S(1)} %copy-done.10), channel_id=1, source_target_pairs={{0,2},{2,0},{1,3},{3,1},{4,6},{6,4},{5,7},{7,5},{8,10},{10,8},{9,1... | collective-permute-start | bytes 4718600 | tf_op jit(solution)/shard_map/ppermute | solution.py:401
  140.4 28.5 %collective-permute-start.13 = (bf16[3,8,96,128]{3,2,1,0:T(8,128)(2,1)}, bf16[3,8,96,128]{3,2,1,0:T(8,128)(2,1)S(1)}, u32[]{:S(2)}, u32[]{:S(2)}) collective-permute-start(bf16[3,8,96,128]{3,2,1,0:T(8,128)(2,1)} %slice_bitcast_fusion.3), channel_id=1, source_target_pairs={{0,32},{4,36},{8,40},{12,44},{16,48},{20,52},{24,56},{28,60},{32,6... | collective-permute-start | bytes 1769480 | tf_op jit(solution)/shard_map/ppermute | solution.py:356
  141.3 27.6 %collective-permute-start.15 = (bf16[3,8,96,128]{3,2,1,0:T(8,128)(2,1)}, bf16[3,8,96,128]{3,2,1,0:T(8,128)(2,1)}, u32[]{:S(2)}, u32[]{:S(2)}) collective-permute-start(bf16[3,8,96,128]{3,2,1,0:T(8,128)(2,1)} %slice_bitcast_fusion.2), channel_id=1, source_target_pairs={{0,96},{4,100},{8,104},{12,108},{16,112},{20,116},{24,120},{28,124... | collective-permute-start | bytes 1769480 | tf_op jit(solution)/shard_map/ppermute | solution.py:356
  144.9 24.0 %collective-permute-start.17 = (bf16[3,8,96,128]{3,2,1,0:T(8,128)(2,1)}, bf16[3,8,96,128]{3,2,1,0:T(8,128)(2,1)S(1)}, u32[]{:S(2)}, u32[]{:S(2)}) collective-permute-start(bf16[3,8,96,128]{3,2,1,0:T(8,128)(2,1)} %slice_bitcast_fusion.1), channel_id=1, source_target_pairs={{0,8},{4,12},{8,16},{12,20},{16,24},{20,28},{24,0},{28,4},{32,40},... | collective-permute-start | bytes 1769480 | tf_op jit(solution)/shard_map/ppermute | solution.py:356
  146.9 22.1 %collective-permute-start.19 = (bf16[3,8,96,128]{3,2,1,0:T(8,128)(2,1)}, bf16[3,8,96,128]{3,2,1,0:T(8,128)(2,1)S(1)}, u32[]{:S(2)}, u32[]{:S(2)}) collective-permute-start(bf16[3,8,96,128]{3,2,1,0:T(8,128)(2,1)} %slice_bitcast_fusion), channel_id=1, source_target_pairs={{0,24},{4,28},{8,0},{12,4},{16,8},{20,12},{24,16},{28,20},{32,56},... | collective-permute-start | bytes 1769480 | tf_op jit(solution)/shard_map/ppermute | solution.py:356
  181.2 6.8 %collective-permute-start.20 = (bf16[3,32,48,128]{3,2,1,0:T(8,128)(2,1)}, bf16[3,32,48,128]{3,2,1,0:T(8,128)(2,1)S(1)}, u32[]{:S(2)}, u32[]{:S(2)}) collective-permute-start(bf16[3,32,48,128]{3,2,1,0:T(8,128)(2,1)} %get-tuple-element.44), channel_id=1, source_target_pairs={{0,1},{1,0},{2,3},{3,2},{4,5},{5,4},{6,7},{7,6},{8,9},{9,8},{10,11... | collective-permute-start | bytes 3538952 | tf_op jit(solution)/shard_map/ppermute | solution.py:397
  (21 other events, 197.2 us)

commit v5 on v4

--- a/solution.py
+++ b/solution.py
@@ -436,7 +436,7 @@
     parts = jnp.stack([lax.dynamic_index_in_dim(everyone, roots[s], 0, keepdims=False) for s in range(STEPS)])
     first, second = gather_planes(parts)
     plane_a, plane_b = plane(first, "dz"), plane(second, "dx")
-    plane_a, plane_b, upper, lower = lax.optimization_barrier((plane_a, plane_b, upper, leaving[1]))
+    plane_b, upper, lower = lax.optimization_barrier((plane_b, upper, leaving[1]))
     across = upper, from_other_chip(lower)
     near = [
         shift(plane_a, dx=1),

time: 197 us -> 194 us (0.985)
  waiting for transfers between devices: 89.1 us -> 84.2 us
  starting transfers between devices: 38.7 us -> 40.7 us
    ppermute x15, waiting for transfers between devices: 34.2 us -> 27.1 us  [shift(): return lax.ppermute(value, 'chan', pairs)]
    ppermute x3, waiting for transfers between devices: 16.7 us -> 19 us  [from_other_chip(): return lax.ppermute(value, 'tm', [(0, 2), (2, 0), (1, 3), (3, 1)])]
    ppermute x15, starting transfers between devices: 16.6 us -> 18.8 us  [shift(): return lax.ppermute(value, 'chan', pairs)]
  transfers between devices with their start and end apart: 22 -> 22, of which waited for: 13 -> 12; matrix products, arithmetic and copies ran while one was open for 6% -> 6% of each run, Pallas kernels for 8% -> 8%
where the time goes in v5:
time: 194 us; the launch traced here: 193 us
  waiting for transfers between devices  84.2 us (43%)
  Pallas kernels  43.6 us (22%)
  starting transfers between devices  40.7 us (21%)
  local copies, waits for them, and re-layouts  15 us (8%)
  between operations  6.41 us (3%)
  other arithmetic  3.04 us (2%)
    ppermute x15, waiting for transfers between devices, shift(): return lax.ppermute(value, 'chan', pairs)  27.1 us
    all_to_all x1, waiting for transfers between devices, shards(): lax.all_to_all(own.reshape((32, 4) + own.shape[1:]), 'chan', 0, 0)  26.6 us
    ppermute x3, waiting for transfers between devices, from_other_chip(): return lax.ppermute(value, 'tm', [(0, 2), (2, 0), (1, 3), (3, 1)])  19 us
    ppermute x15, starting transfers between devices, shift(): return lax.ppermute(value, 'chan', pairs)  18.8 us
    pallas_call x1, Pallas kernels, near_coefficients(): pl.pallas_call(functools.partial(near_kernel, len(pieces)), grid=(STEPS,)...  15.2 us
    pallas_call x1, Pallas kernels, whitened_spectra(): pl.pallas_call(functools.partial(spectra_kernel, GROUP), grid=(windows //...  11 us
    pallas_call x1, Pallas kernels, all_coefficients(): pl.pallas_call(functools.partial(far_kernel, len(pieces)), grid=(STEPS,),...  10.4 us
    all_to_all x1, starting transfers between devices, shards(): lax.all_to_all(own.reshape((32, 4) + own.shape[1:]), 'chan', 0, 0)  9.05 us
  transfers between devices with their start and end apart: 22, of which 12 were waited for; matrix products, arithmetic and copies ran while one was open for 6% of the time, Pallas kernels for 8%

profile of v5, /device:TPU:1, one launch (start us, length us, event | category | flops | bytes accessed | tf_op | source)
XLA Modules:
  0.0 193.1 jit_solution(3337427878753696363)
XLA Ops:
  0.9 3.3 %collective-permute-start = (bf16[128,512]{1,0:T(8,128)(2,1)S(1)}, bf16[128,512]{1,0:T(8,128)(2,1)S(1)}, u32[]{:S(2)}, u32[]{:S(2)}) collective-permute-start(bf16[128,512]{1,0:T(8,128)(2,1)S(1)} %slice.76), channel_id=1, source_target_pairs={{1,0},{2,1},{3,2},{5,4},{6,5},{7,6},{9,8},{10,9},{11,10},{13,12},{... | collective-permute-start | bytes 393224 | tf_op jit(solution)/shard_map/ppermute | solution.py:418
  4.3 5.5 %collective-permute-done.edge_ref = bf16[128,512]{1,0:T(8,128)(2,1)S(1)} collective-permute-done((bf16[128,512]{1,0:T(8,128)(2,1)S(1)}, bf16[128,512]{1,0:T(8,128)(2,1)S(1)}, u32[]{:S(2)}, u32[]{:S(2)}) %collective-permute-start) | collective-permute-done | bytes 131104 | tf_op jit(solution)/shard_map/ppermute | solution.py:418
  10.4 11.0 %spectra.1.own_ref.own_hbm = bf16[128,96,128]{2,1,0:T(8,128)(2,1)} custom-call(bf16[128,24576]{1,0:T(8,128)(2,1)} %next_ref.1, bf16[128,24576]{1,0:T(8,128)(2,1)} %next_ref.1, bf16[128,512]{1,0:T(8,128)(2,1)} %copy-done.16, bf16[256,1024]{1,0:T(8,128)(2,1)} %constant.221.clone.table_ref, bf16[128,256]{1,0:T(8,128)(2,1)} %constant.222.clone.band_ref, ...), custom_call_target="tpu_custom_call" | custom-call | tf_op jit(solution)/shard_map/spectra/pallas_call | solution.py:152
  21.6 9.1 %all-to-all-start = ((bf16[32,4,96,128]{3,2,1,0:T(8,128)(2,1)}), bf16[32,4,96,128]{3,2,1,0:T(8,128)(2,1)}, u32[]{:S(2)}, u32[]{:S(2)}) async-start(bf16[32,4,96,128]{3,2,1,0:T(8,128)(2,1)} %bitcast.31), calls=%async_computation | async-start | bytes 6291456 | tf_op jit(solution)/shard_map/all_to_all | solution.py:429
  41.0 2.3 %fusion.8 = (bf16[128,48,128]{2,1,0:T(8,128)(2,1)}, bf16[128,48,128]{2,1,0:T(8,128)(2,1)}) fusion(bf16[128,96,128]{2,1,0:T(8,128)(2,1)S(1)} %copy-done.1), kind=kLoop, calls=%fused_computation.56 | loop fusion | bytes 6291456 | tf_op jit(solution)/shard_map/slice | solution.py:431
  43.3 26.6 %all-to-all-done = bf16[32,4,96,128]{3,2,1,0:T(8,128)(2,1)} async-done(((bf16[32,4,96,128]{3,2,1,0:T(8,128)(2,1)}), bf16[32,4,96,128]{3,2,1,0:T(8,128)(2,1)}, u32[]{:S(2)}, u32[]{:S(2)}) %all-to-all-start) | async-done | bytes 3145760 | tf_op jit(solution)/shard_map/all_to_all | solution.py:429
  71.3 1.9 collective-permute-start.3
  78.9 3.4 %collective-permute-done.3 = bf16[3,4,48,128]{3,2,1,0:T(8,128)(2,1)S(1)} collective-permute-done((bf16[3,4,48,128]{3,2,1,0:T(8,128)(2,1)S(1)}, bf16[3,4,48,128]{3,2,1,0:T(8,128)(2,1)S(1)}, u32[]{:S(2)}, u32[]{:S(2)}) %collective-permute-start.3) | collective-permute-done | bytes 147488 | tf_op jit(solution)/shard_map/ppermute | solution.py:377
  82.4 2.7 %collective-permute-start.10 = (bf16[3,4,96,128]{3,2,1,0:T(8,128)(2,1)S(1)}, bf16[3,4,96,128]{3,2,1,0:T(8,128)(2,1)S(1)}, u32[]{:S(2)}, u32[]{:S(2)}) collective-permute-start(bf16[3,4,96,128]{3,2,1,0:T(8,128)(2,1)S(1)} %get-tuple-element.32), channel_id=1, source_target_pairs={{0,24},{4,28},{8,0},{12,4},{16,8},{20,12},{24,16},{28,20},{32,56},... | collective-permute-start | bytes 884744 | tf_op jit(solution)/shard_map/ppermute | solution.py:356
  86.3 5.3 %collective-permute-done.9 = bf16[3,4,96,128]{3,2,1,0:T(8,128)(2,1)S(1)} collective-permute-done((bf16[3,4,96,128]{3,2,1,0:T(8,128)(2,1)S(1)}, bf16[3,4,96,128]{3,2,1,0:T(8,128)(2,1)S(1)}, u32[]{:S(2)}, u32[]{:S(2)}) %collective-permute-start.9) | collective-permute-done | bytes 294944 | tf_op jit(solution)/shard_map/ppermute | solution.py:356
  94.9 3.6 %collective-permute-done.11 = bf16[3,4,96,128]{3,2,1,0:T(8,128)(2,1)S(1)} collective-permute-done((bf16[3,4,96,128]{3,2,1,0:T(8,128)(2,1)S(1)}, bf16[3,4,96,128]{3,2,1,0:T(8,128)(2,1)S(1)}, u32[]{:S(2)}, u32[]{:S(2)}) %collective-permute-start.11) | collective-permute-done | bytes 294944 | tf_op jit(solution)/shard_map/ppermute | solution.py:356
  98.8 2.7 %collective-permute-start.14 = (bf16[2,3,8,96,128]{4,3,2,1,0:T(8,128)(2,1)S(1)}, bf16[2,3,8,96,128]{4,3,2,1,0:T(8,128)(2,1)S(1)}, u32[]{:S(2)}, u32[]{:S(2)}) collective-permute-start(bf16[2,3,8,96,128]{4,3,2,1,0:T(8,128)(2,1)S(1)} %pad_maximum_fusion.1.refs_0_), channel_id=1, source_target_pairs={{0,96},{4,100},{8,104},{12,108},{16,112},{20,116},{24,120},{28,124... | collective-permute-start | bytes 3538952 | tf_op jit(solution)/shard_map/ppermute | solution.py:356
  101.8 10.9 %collective-permute-done.7.upper_ref.upper_hbm = bf16[128,48,128]{2,1,0:T(8,128)(2,1)S(1)} collective-permute-done((bf16[128,48,128]{2,1,0:T(8,128)(2,1)S(1)}, bf16[128,48,128]{2,1,0:T(8,128)(2,1)S(1)}, u32[]{:S(2)}, u32[]{:S(2)}) %collective-permute-start.7) | collective-permute-done | bytes 1572896 | tf_op jit(solution)/shard_map/ppermute | solution.py:401
  112.7 2.7 %collective-permute-start.18 = (bf16[2,3,8,96,128]{4,3,2,1,0:T(8,128)(2,1)S(1)}, bf16[2,3,8,96,128]{4,3,2,1,0:T(8,128)(2,1)S(1)}, u32[]{:S(2)}, u32[]{:S(2)}) collective-permute-start(bf16[2,3,8,96,128]{4,3,2,1,0:T(8,128)(2,1)S(1)} %pad_maximum_fusion.refs_1_), channel_id=1, source_target_pairs={{0,24},{4,28},{8,0},{12,4},{16,8},{20,12},{24,16},{28,20},{32,56},... | collective-permute-start | bytes 3538952 | tf_op jit(solution)/shard_map/ppermute | solution.py:356
  115.4 2.6 %collective-permute-start.8 = (bf16[128,48,128]{2,1,0:T(8,128)(2,1)S(1)}, bf16[128,48,128]{2,1,0:T(8,128)(2,1)S(1)}, u32[]{:S(2)}, u32[]{:S(2)}) collective-permute-start(bf16[128,48,128]{2,1,0:T(8,128)(2,1)S(1)} %copy-done.10), channel_id=1, source_target_pairs={{0,2},{2,0},{1,3},{3,1},{4,6},{6,4},{5,7},{7,5},{8,10},{10,8},{9,1... | collective-permute-start | bytes 4718600 | tf_op jit(solution)/shard_map/ppermute | solution.py:401
  117.9 10.4 %collective-permute-done.12.refs_2_ = bf16[2,3,8,96,128]{4,3,2,1,0:T(8,128)(2,1)S(1)} collective-permute-done((bf16[2,3,8,96,128]{4,3,2,1,0:T(8,128)(2,1)S(1)}, bf16[2,3,8,96,128]{4,3,2,1,0:T(8,128)(2,1)S(1)}, u32[]{:S(2)}, u32[]{:S(2)}) %collective-permute-start.12) | collective-permute-done | bytes 1179680 | tf_op jit(solution)/shard_map/ppermute | solution.py:356
  130.2 2.7 %collective-permute-start.15 = (bf16[3,8,96,128]{3,2,1,0:T(8,128)(2,1)}, bf16[3,8,96,128]{3,2,1,0:T(8,128)(2,1)}, u32[]{:S(2)}, u32[]{:S(2)}) collective-permute-start(bf16[3,8,96,128]{3,2,1,0:T(8,128)(2,1)} %slice_bitcast_fusion.2), channel_id=1, source_target_pairs={{0,96},{4,100},{8,104},{12,108},{16,112},{20,116},{24,120},{28,124... | collective-permute-start | bytes 1769480 | tf_op jit(solution)/shard_map/ppermute | solution.py:356
  132.9 6.3 %collective-permute-done.16.refs_3_ = bf16[2,3,8,96,128]{4,3,2,1,0:T(8,128)(2,1)S(1)} collective-permute-done((bf16[2,3,8,96,128]{4,3,2,1,0:T(8,128)(2,1)S(1)}, bf16[2,3,8,96,128]{4,3,2,1,0:T(8,128)(2,1)S(1)}, u32[]{:S(2)}, u32[]{:S(2)}) %collective-permute-start.16) | collective-permute-done | bytes 1179680 | tf_op jit(solution)/shard_map/ppermute | solution.py:356
  143.7 6.3 %collective-permute-done.8.lower_ref.lower_hbm = bf16[128,48,128]{2,1,0:T(8,128)(2,1)S(1)} collective-permute-done((bf16[128,48,128]{2,1,0:T(8,128)(2,1)S(1)}, bf16[128,48,128]{2,1,0:T(8,128)(2,1)S(1)}, u32[]{:S(2)}, u32[]{:S(2)}) %collective-permute-start.8) | collective-permute-done | bytes 1572896 | tf_op jit(solution)/shard_map/ppermute | solution.py:401
  151.2 15.2 %near.1.near_ref = f32[3,64,48,128]{3,2,1,0:T(8,128)} custom-call(s32[96]{0:T(128)} %concatenate.47.slots_ref, bf16[96,192]{1,0:T(8,128)(2,1)} %pad_maximum_fusion.8.v_ref, bf16[128,96,128]{2,1,0:T(8,128)(2,1)} %spectra.1.own_ref.own_hbm, bf16[128,48,128]{2,1,0:T(8,128)(2,1)} %copy-done.2, bf16[128,48,128]{2,1,0:T(8,128)(2,1)} %copy-done.3, ...), custom_call_target="tpu_custom_call" | custom-call | tf_op jit(solution)/shard_map/near/pallas_call | solution.py:285
  168.3 10.4 %far.1 = (f32[3,32,48,128]{3,2,1,0:T(8,128)}, bf16[3,32,48,128]{3,2,1,0:T(8,128)(2,1)}) custom-call(s32[33]{0:T(128)} %pad_add_fusion.slots_ref, bf16[96,64]{1,0:T(8,128)(2,1)} %pad_maximum_fusion.9.v_ref, bf16[128,96,128]{2,1,0:T(8,128)(2,1)} %spectra.1.own_ref.own_hbm, bf16[128,48,128]{2,1,0:T(8,128)(2,1)} %copy-done.2, bf16[128,48,128]{2,1,0:T(8,128)(2,1)} %copy-done.3, ...), custom_call_target="tpu_custom_call" | custom-call | tf_op jit(solution)/shard_map/far/pallas_call | solution.py:303
  178.8 3.7 %collective-permute-start.20 = (bf16[3,32,48,128]{3,2,1,0:T(8,128)(2,1)}, bf16[3,32,48,128]{3,2,1,0:T(8,128)(2,1)S(1)}, u32[]{:S(2)}, u32[]{:S(2)}) collective-permute-start(bf16[3,32,48,128]{3,2,1,0:T(8,128)(2,1)} %get-tuple-element.42), channel_id=1, source_target_pairs={{0,1},{1,0},{2,3},{3,2},{4,5},{5,4},{6,7},{7,6},{8,9},{9,8},{10,11... | collective-permute-start | bytes 3538952 | tf_op jit(solution)/shard_map/ppermute | solution.py:397
  182.5 2.7 %collective-permute-done.20.got_ref = bf16[3,32,48,128]{3,2,1,0:T(8,128)(2,1)S(1)} collective-permute-done((bf16[3,32,48,128]{3,2,1,0:T(8,128)(2,1)}, bf16[3,32,48,128]{3,2,1,0:T(8,128)(2,1)S(1)}, u32[]{:S(2)}, u32[]{:S(2)}) %collective-permute-start.20) | collective-permute-done | bytes 1179680 | tf_op jit(solution)/shard_map/ppermute | solution.py:397
  186.2 6.9 %expand.1 = f32[3,3232,128]{2,1,0:T(8,128)} custom-call(bf16[104,144]{1,0:T(8,128)(2,1)} %constant.229.clone.u_ref, f32[3,32,48,128]{3,2,1,0:T(8,128)} %get-tuple-element.41.keep_ref, bf16[3,32,48,128]{3,2,1,0:T(8,128)(2,1)} %copy-done.12), custom_call_target="tpu_custom_call" | custom-call | tf_op jit(solution)/shard_map/expand/pallas_call | solution.py:339
  (110 shorter events, 28.6 us)
Async XLA Ops:
  0.0 30.8 %copy-start = (s32[32]{0:T(128)S(1)}, s32[32]{0:T(128)}, u32[]{:S(2)}) copy-start(s32[32]{0:T(128)} %param.23) | copy-start | bytes 388
  0.9 8.9 %collective-permute-start = (bf16[128,512]{1,0:T(8,128)(2,1)S(1)}, bf16[128,512]{1,0:T(8,128)(2,1)S(1)}, u32[]{:S(2)}, u32[]{:S(2)}) collective-permute-start(bf16[128,512]{1,0:T(8,128)(2,1)S(1)} %slice.76), channel_id=1, source_target_pairs={{1,0},{2,1},{3,2},{5,4},{6,5},{7,6},{9,8},{10,9},{11,10},{13,12},{... | collective-permute-start | bytes 393224 | tf_op jit(solution)/shard_map/ppermute | solution.py:418
  21.6 48.3 %all-to-all-start = ((bf16[32,4,96,128]{3,2,1,0:T(8,128)(2,1)}), bf16[32,4,96,128]{3,2,1,0:T(8,128)(2,1)}, u32[]{:S(2)}, u32[]{:S(2)}) async-start(bf16[32,4,96,128]{3,2,1,0:T(8,128)(2,1)} %bitcast.31), calls=%async_computation | async-start | bytes 6291456 | tf_op jit(solution)/shard_map/all_to_all | solution.py:429
  71.3 6.1 %collective-permute-start.1 = (bf16[3,4,48,128]{3,2,1,0:T(8,128)(2,1)S(1)}, bf16[3,4,48,128]{3,2,1,0:T(8,128)(2,1)S(1)}, u32[]{:S(2)}, u32[]{:S(2)}) collective-permute-start(bf16[3,4,48,128]{3,2,1,0:T(8,128)(2,1)S(1)} %pad_maximum_fusion.7), channel_id=1, source_target_pairs={{0,2},{2,0},{1,3},{3,1},{4,6},{6,4},{5,7},{7,5},{8,10},{10,8},{9,1... | collective-permute-start | bytes 442376 | tf_op jit(solution)/shard_map/ppermute | solution.py:401
  71.3 10.9 %collective-permute-start.3 = (bf16[3,4,48,128]{3,2,1,0:T(8,128)(2,1)S(1)}, bf16[3,4,48,128]{3,2,1,0:T(8,128)(2,1)S(1)}, u32[]{:S(2)}, u32[]{:S(2)}) collective-permute-start(bf16[3,4,48,128]{3,2,1,0:T(8,128)(2,1)S(1)} %pad_maximum_fusion.7), channel_id=1, source_target_pairs={{0,6},{1,7},{2,4},{3,5},{4,2},{5,3},{6,0},{7,1},{8,14},{9,15},{10,... | collective-permute-start | bytes 442376 | tf_op jit(solution)/shard_map/ppermute | solution.py:377
  73.3 5.5 %collective-permute-start.2 = (bf16[3,4,48,128]{3,2,1,0:T(8,128)(2,1)S(1)}, bf16[3,4,48,128]{3,2,1,0:T(8,128)(2,1)S(1)}, u32[]{:S(2)}, u32[]{:S(2)}) collective-permute-start(bf16[3,4,48,128]{3,2,1,0:T(8,128)(2,1)S(1)} %pad_maximum_fusion.6), channel_id=1, source_target_pairs={{0,4},{4,0},{8,12},{12,8},{16,20},{20,16},{24,28},{28,24},{32,36},... | collective-permute-start | bytes 442376 | tf_op jit(solution)/shard_map/ppermute | solution.py:356
  74.2 38.5 %collective-permute-start.7 = (bf16[128,48,128]{2,1,0:T(8,128)(2,1)S(1)}, bf16[128,48,128]{2,1,0:T(8,128)(2,1)S(1)}, u32[]{:S(2)}, u32[]{:S(2)}) collective-permute-start(bf16[128,48,128]{2,1,0:T(8,128)(2,1)S(1)} %copy-done.11), channel_id=1, source_target_pairs={{0,2},{2,0},{1,3},{3,1},{4,6},{6,4},{5,7},{7,5},{8,10},{10,8},{9,1... | collective-permute-start | bytes 4718600 | tf_op jit(solution)/shard_map/ppermute | solution.py:401
  82.4 9.2 %collective-permute-start.9 = (bf16[3,4,96,128]{3,2,1,0:T(8,128)(2,1)S(1)}, bf16[3,4,96,128]{3,2,1,0:T(8,128)(2,1)S(1)}, u32[]{:S(2)}, u32[]{:S(2)}) collective-permute-start(bf16[3,4,96,128]{3,2,1,0:T(8,128)(2,1)S(1)} %get-tuple-element.32), channel_id=1, source_target_pairs={{0,8},{4,12},{8,16},{12,20},{16,24},{20,28},{24,0},{28,4},{32,40},... | collective-permute-start | bytes 884744 | tf_op jit(solution)/shard_map/ppermute | solution.py:356
  82.4 10.8 %collective-permute-start.10 = (bf16[3,4,96,128]{3,2,1,0:T(8,128)(2,1)S(1)}, bf16[3,4,96,128]{3,2,1,0:T(8,128)(2,1)S(1)}, u32[]{:S(2)}, u32[]{:S(2)}) collective-permute-start(bf16[3,4,96,128]{3,2,1,0:T(8,128)(2,1)S(1)} %get-tuple-element.32), channel_id=1, source_target_pairs={{0,24},{4,28},{8,0},{12,4},{16,8},{20,12},{24,16},{28,20},{32,56},... | collective-permute-start | bytes 884744 | tf_op jit(solution)/shard_map/ppermute | solution.py:356
  85.1 13.4 %collective-permute-start.11 = (bf16[3,4,96,128]{3,2,1,0:T(8,128)(2,1)S(1)}, bf16[3,4,96,128]{3,2,1,0:T(8,128)(2,1)S(1)}, u32[]{:S(2)}, u32[]{:S(2)}) collective-permute-start(bf16[3,4,96,128]{3,2,1,0:T(8,128)(2,1)S(1)} %get-tuple-element.32), channel_id=1, source_target_pairs={{0,16},{4,20},{8,24},{12,28},{16,0},{20,4},{24,8},{28,12},{32,48},... | collective-permute-start | bytes 884744 | tf_op jit(solution)/shard_map/ppermute | solution.py:356
  85.7 13.1 %collective-permute-start.4 = (bf16[3,4,96,128]{3,2,1,0:T(8,128)(2,1)S(1)}, bf16[3,4,96,128]{3,2,1,0:T(8,128)(2,1)S(1)}, u32[]{:S(2)}, u32[]{:S(2)}) collective-permute-start(bf16[3,4,96,128]{3,2,1,0:T(8,128)(2,1)S(1)} %get-tuple-element.27), channel_id=1, source_target_pairs={{0,32},{4,36},{8,40},{12,44},{16,48},{20,52},{24,56},{28,60},{32,6... | collective-permute-start | bytes 884744 | tf_op jit(solution)/shard_map/ppermute | solution.py:356
  91.6 9.9 %collective-permute-start.5 = (bf16[3,4,96,128]{3,2,1,0:T(8,128)(2,1)S(1)}, bf16[3,4,96,128]{3,2,1,0:T(8,128)(2,1)S(1)}, u32[]{:S(2)}, u32[]{:S(2)}) collective-permute-start(bf16[3,4,96,128]{3,2,1,0:T(8,128)(2,1)S(1)} %get-tuple-element.27), channel_id=1, source_target_pairs={{0,96},{4,100},{8,104},{12,108},{16,112},{20,116},{24,120},{28,124... | collective-permute-start | bytes 884744 | tf_op jit(solution)/shard_map/ppermute | solution.py:356
  93.3 8.3 %collective-permute-start.6 = (bf16[3,4,96,128]{3,2,1,0:T(8,128)(2,1)S(1)}, bf16[3,4,96,128]{3,2,1,0:T(8,128)(2,1)S(1)}, u32[]{:S(2)}, u32[]{:S(2)}) collective-permute-start(bf16[3,4,96,128]{3,2,1,0:T(8,128)(2,1)S(1)} %get-tuple-element.27), channel_id=1, source_target_pairs={{0,64},{4,68},{8,72},{12,76},{16,80},{20,84},{24,88},{28,92},{32,9... | collective-permute-start | bytes 884744 | tf_op jit(solution)/shard_map/ppermute | solution.py:356
  98.7 29.6 %collective-permute-start.12 = (bf16[2,3,8,96,128]{4,3,2,1,0:T(8,128)(2,1)S(1)}, bf16[2,3,8,96,128]{4,3,2,1,0:T(8,128)(2,1)S(1)}, u32[]{:S(2)}, u32[]{:S(2)}) collective-permute-start(bf16[2,3,8,96,128]{4,3,2,1,0:T(8,128)(2,1)S(1)} %pad_maximum_fusion.1.refs_0_), channel_id=1, source_target_pairs={{0,32},{4,36},{8,40},{12,44},{16,48},{20,52},{24,56},{28,60},{32,6... | collective-permute-start | bytes 3538952 | tf_op jit(solution)/shard_map/ppermute | solution.py:356
  98.8 30.4 %collective-permute-start.14 = (bf16[2,3,8,96,128]{4,3,2,1,0:T(8,128)(2,1)S(1)}, bf16[2,3,8,96,128]{4,3,2,1,0:T(8,128)(2,1)S(1)}, u32[]{:S(2)}, u32[]{:S(2)}) collective-permute-start(bf16[2,3,8,96,128]{4,3,2,1,0:T(8,128)(2,1)S(1)} %pad_maximum_fusion.1.refs_0_), channel_id=1, source_target_pairs={{0,96},{4,100},{8,104},{12,108},{16,112},{20,116},{24,120},{28,124... | collective-permute-start | bytes 3538952 | tf_op jit(solution)/shard_map/ppermute | solution.py:356
  101.8 40.7 %copy-start.5 = (bf16[2,3,8,96,128]{4,3,2,1,0:T(8,128)(2,1)}, bf16[2,3,8,96,128]{4,3,2,1,0:T(8,128)(2,1)S(1)}, u32[]{:S(2)}) copy-start(bf16[2,3,8,96,128]{4,3,2,1,0:T(8,128)(2,1)S(1)} %pad_maximum_fusion.refs_1_) | copy-start | bytes 3538948
  112.7 26.5 %collective-permute-start.16 = (bf16[2,3,8,96,128]{4,3,2,1,0:T(8,128)(2,1)S(1)}, bf16[2,3,8,96,128]{4,3,2,1,0:T(8,128)(2,1)S(1)}, u32[]{:S(2)}, u32[]{:S(2)}) collective-permute-start(bf16[2,3,8,96,128]{4,3,2,1,0:T(8,128)(2,1)S(1)} %pad_maximum_fusion.refs_1_), channel_id=1, source_target_pairs={{0,8},{4,12},{8,16},{12,20},{16,24},{20,28},{24,0},{28,4},{32,40},... | collective-permute-start | bytes 3538952 | tf_op jit(solution)/shard_map/ppermute | solution.py:356
  112.7 28.8 %collective-permute-start.18 = (bf16[2,3,8,96,128]{4,3,2,1,0:T(8,128)(2,1)S(1)}, bf16[2,3,8,96,128]{4,3,2,1,0:T(8,128)(2,1)S(1)}, u32[]{:S(2)}, u32[]{:S(2)}) collective-permute-start(bf16[2,3,8,96,128]{4,3,2,1,0:T(8,128)(2,1)S(1)} %pad_maximum_fusion.refs_1_), channel_id=1, source_target_pairs={{0,24},{4,28},{8,0},{12,4},{16,8},{20,12},{24,16},{28,20},{32,56},... | collective-permute-start | bytes 3538952 | tf_op jit(solution)/shard_map/ppermute | solution.py:356
  115.4 34.7 %collective-permute-start.8 = (bf16[128,48,128]{2,1,0:T(8,128)(2,1)S(1)}, bf16[128,48,128]{2,1,0:T(8,128)(2,1)S(1)}, u32[]{:S(2)}, u32[]{:S(2)}) collective-permute-start(bf16[128,48,128]{2,1,0:T(8,128)(2,1)S(1)} %copy-done.10), channel_id=1, source_target_pairs={{0,2},{2,0},{1,3},{3,1},{4,6},{6,4},{5,7},{7,5},{8,10},{10,8},{9,1... | collective-permute-start | bytes 4718600 | tf_op jit(solution)/shard_map/ppermute | solution.py:401
  129.2 37.2 %collective-permute-start.13 = (bf16[3,8,96,128]{3,2,1,0:T(8,128)(2,1)}, bf16[3,8,96,128]{3,2,1,0:T(8,128)(2,1)S(1)}, u32[]{:S(2)}, u32[]{:S(2)}) collective-permute-start(bf16[3,8,96,128]{3,2,1,0:T(8,128)(2,1)} %slice_bitcast_fusion.3), channel_id=1, source_target_pairs={{0,32},{4,36},{8,40},{12,44},{16,48},{20,52},{24,56},{28,60},{32,6... | collective-permute-start | bytes 1769480 | tf_op jit(solution)/shard_map/ppermute | solution.py:356
  130.2 36.3 %collective-permute-start.15 = (bf16[3,8,96,128]{3,2,1,0:T(8,128)(2,1)}, bf16[3,8,96,128]{3,2,1,0:T(8,128)(2,1)}, u32[]{:S(2)}, u32[]{:S(2)}) collective-permute-start(bf16[3,8,96,128]{3,2,1,0:T(8,128)(2,1)} %slice_bitcast_fusion.2), channel_id=1, source_target_pairs={{0,96},{4,100},{8,104},{12,108},{16,112},{20,116},{24,120},{28,124... | collective-permute-start | bytes 1769480 | tf_op jit(solution)/shard_map/ppermute | solution.py:356
  140.1 26.4 %collective-permute-start.17 = (bf16[3,8,96,128]{3,2,1,0:T(8,128)(2,1)}, bf16[3,8,96,128]{3,2,1,0:T(8,128)(2,1)S(1)}, u32[]{:S(2)}, u32[]{:S(2)}) collective-permute-start(bf16[3,8,96,128]{3,2,1,0:T(8,128)(2,1)} %slice_bitcast_fusion.1), channel_id=1, source_target_pairs={{0,8},{4,12},{8,16},{12,20},{16,24},{20,28},{24,0},{28,4},{32,40},... | collective-permute-start | bytes 1769480 | tf_op jit(solution)/shard_map/ppermute | solution.py:356
  142.5 24.0 %collective-permute-start.19 = (bf16[3,8,96,128]{3,2,1,0:T(8,128)(2,1)}, bf16[3,8,96,128]{3,2,1,0:T(8,128)(2,1)S(1)}, u32[]{:S(2)}, u32[]{:S(2)}) collective-permute-start(bf16[3,8,96,128]{3,2,1,0:T(8,128)(2,1)} %slice_bitcast_fusion), channel_id=1, source_target_pairs={{0,24},{4,28},{8,0},{12,4},{16,8},{20,12},{24,16},{28,20},{32,56},... | collective-permute-start | bytes 1769480 | tf_op jit(solution)/shard_map/ppermute | solution.py:356
  178.8 6.4 %collective-permute-start.20 = (bf16[3,32,48,128]{3,2,1,0:T(8,128)(2,1)}, bf16[3,32,48,128]{3,2,1,0:T(8,128)(2,1)S(1)}, u32[]{:S(2)}, u32[]{:S(2)}) collective-permute-start(bf16[3,32,48,128]{3,2,1,0:T(8,128)(2,1)} %get-tuple-element.42), channel_id=1, source_target_pairs={{0,1},{1,0},{2,3},{3,2},{4,5},{5,4},{6,7},{7,6},{8,9},{9,8},{10,11... | collective-permute-start | bytes 3538952 | tf_op jit(solution)/shard_map/ppermute | solution.py:397
  (21 other events, 182.3 us)

commit v6 on v5

--- a/solution.py
+++ b/solution.py
@@ -239,7 +239,7 @@
         channels = [n * 32 + j for j in range(32)]
         totals = coefficients(v_ref, real_rows, imag_rows, row, bins, channels)
         for b, total in zip(channels, totals):
-            out_ref[0, b] = total
+            out_ref[0, b] = total.astype(out_ref.dtype)
         return carry
 
     lax.fori_loop(0, 2, some, 0)
@@ -272,7 +272,7 @@
         channels = [which * 32 + j for j in range(32)]
         totals = coefficients(v_ref, real_rows, imag_rows, row, bins, channels)
         for j, total in enumerate(totals):
-            out_ref[0, j] = (near_ref[0, channels[j]] + total).astype(out_ref.dtype)
+            out_ref[0, j] = (near_ref[0, channels[j]].astype(jnp.float32) + total).astype(out_ref.dtype)
 
 
 def step_block(shape):
@@ -285,7 +285,7 @@
     return pl.pallas_call(
         functools.partial(near_kernel, len(pieces)),
         grid=(STEPS,),
-        out_shape=jax.ShapeDtypeStruct((STEPS, 64, RANK, 128), jnp.float32),
+        out_shape=jax.ShapeDtypeStruct((STEPS, 64, RANK, 128), jnp.bfloat16),
         in_specs=[pl.BlockSpec(memory_space=pltpu.SMEM), whole(v), whole(own)]
         + [whole(a) for a in across]
         + [pl.BlockSpec((2, 1) + p.shape[2:], lambda s: (0, s, 0, 0, 0)) for p in pieces],
@@ -304,7 +304,7 @@
         functools.partial(far_kernel, len(pieces)),
         grid=(STEPS,),
         out_shape=[
-            jax.ShapeDtypeStruct((STEPS,) + rows, jnp.float32),
+            jax.ShapeDtypeStruct((STEPS,) + rows, jnp.bfloat16),
             jax.ShapeDtypeStruct((STEPS,) + rows, jnp.bfloat16),
         ],
         in_specs=[pl.BlockSpec(memory_space=pltpu.SMEM), pl.BlockSpec(v.shape, lambda s: (0, 0))]
@@ -323,7 +323,7 @@
     count = keep_ref.shape[1]
     results = []
     for n in range(0, count, 2):
-        value = jnp.concatenate([keep_ref[0, b] + got_ref[0, b].astype(jnp.float32) for b in (n, n + 1)], axis=1)
+        value = jnp.concatenate([keep_ref[0, b].astype(jnp.float32) + got_ref[0, b].astype(jnp.float32) for b in (n, n + 1)], axis=1)
         high = value.astype(jnp.bfloat16)
         low = (value - high.astype(jnp.float32)).astype(jnp.bfloat16)
         results.append(

time: 194 us -> 193 us (level)
  no operation moved by 1% of the time
where the time goes in v6:
time: 193 us; the launch traced here: 192 us
  waiting for transfers between devices  84.4 us (44%)
  Pallas kernels  42.5 us (22%)
  starting transfers between devices  40.6 us (21%)
  local copies, waits for them, and re-layouts  15 us (8%)
  between operations  6.33 us (3%)
  other arithmetic  3.08 us (2%)
    ppermute x15, waiting for transfers between devices, shift(): return lax.ppermute(value, 'chan', pairs)  27 us
    all_to_all x1, waiting for transfers between devices, shards(): lax.all_to_all(own.reshape((32, 4) + own.shape[1:]), 'chan', 0, 0)  26.7 us
    ppermute x3, waiting for transfers between devices, from_other_chip(): return lax.ppermute(value, 'tm', [(0, 2), (2, 0), (1, 3), (3, 1)])  19.1 us
    ppermute x15, starting transfers between devices, shift(): return lax.ppermute(value, 'chan', pairs)  18.7 us
    pallas_call x1, Pallas kernels, near_coefficients(): pl.pallas_call(functools.partial(near_kernel, len(pieces)), grid=(STEPS,)...  15 us
    pallas_call x1, Pallas kernels, whitened_spectra(): pl.pallas_call(functools.partial(spectra_kernel, GROUP), grid=(windows //...  11 us
    pallas_call x1, Pallas kernels, all_coefficients(): pl.pallas_call(functools.partial(far_kernel, len(pieces)), grid=(STEPS,),...  10 us
    all_to_all x1, starting transfers between devices, shards(): lax.all_to_all(own.reshape((32, 4) + own.shape[1:]), 'chan', 0, 0)  9.05 us
  transfers between devices with their start and end apart: 22, of which 12 were waited for; matrix products, arithmetic and copies ran while one was open for 6% of the time, Pallas kernels for 8%

profile of v6, /device:TPU:1, one launch (start us, length us, event | category | flops | bytes accessed | tf_op | source)
XLA Modules:
  0.0 192.0 jit_solution(15427601846947733816)
XLA Ops:
  0.9 3.3 %collective-permute-start = (bf16[128,512]{1,0:T(8,128)(2,1)S(1)}, bf16[128,512]{1,0:T(8,128)(2,1)S(1)}, u32[]{:S(2)}, u32[]{:S(2)}) collective-permute-start(bf16[128,512]{1,0:T(8,128)(2,1)S(1)} %slice.76), channel_id=1, source_target_pairs={{1,0},{2,1},{3,2},{5,4},{6,5},{7,6},{9,8},{10,9},{11,10},{13,12},{... | collective-permute-start | bytes 393224 | tf_op jit(solution)/shard_map/ppermute | solution.py:418
  4.3 5.5 %collective-permute-done.edge_ref = bf16[128,512]{1,0:T(8,128)(2,1)S(1)} collective-permute-done((bf16[128,512]{1,0:T(8,128)(2,1)S(1)}, bf16[128,512]{1,0:T(8,128)(2,1)S(1)}, u32[]{:S(2)}, u32[]{:S(2)}) %collective-permute-start) | collective-permute-done | bytes 131104 | tf_op jit(solution)/shard_map/ppermute | solution.py:418
  10.4 11.0 %spectra.1.own_ref.own_hbm = bf16[128,96,128]{2,1,0:T(8,128)(2,1)} custom-call(bf16[128,24576]{1,0:T(8,128)(2,1)} %next_ref.1, bf16[128,24576]{1,0:T(8,128)(2,1)} %next_ref.1, bf16[128,512]{1,0:T(8,128)(2,1)} %copy-done.16, bf16[256,1024]{1,0:T(8,128)(2,1)} %constant.221.clone.table_ref, bf16[128,256]{1,0:T(8,128)(2,1)} %constant.222.clone.band_ref, ...), custom_call_target="tpu_custom_call" | custom-call | tf_op jit(solution)/shard_map/spectra/pallas_call | solution.py:152
  21.5 9.1 %all-to-all-start = ((bf16[32,4,96,128]{3,2,1,0:T(8,128)(2,1)}), bf16[32,4,96,128]{3,2,1,0:T(8,128)(2,1)}, u32[]{:S(2)}, u32[]{:S(2)}) async-start(bf16[32,4,96,128]{3,2,1,0:T(8,128)(2,1)} %bitcast.31), calls=%async_computation | async-start | bytes 6291456 | tf_op jit(solution)/shard_map/all_to_all | solution.py:429
  40.9 2.2 %fusion.8 = (bf16[128,48,128]{2,1,0:T(8,128)(2,1)}, bf16[128,48,128]{2,1,0:T(8,128)(2,1)}) fusion(bf16[128,96,128]{2,1,0:T(8,128)(2,1)S(1)} %copy-done.1), kind=kLoop, calls=%fused_computation.56 | loop fusion | bytes 6291456 | tf_op jit(solution)/shard_map/slice | solution.py:431
  43.1 26.7 %all-to-all-done = bf16[32,4,96,128]{3,2,1,0:T(8,128)(2,1)} async-done(((bf16[32,4,96,128]{3,2,1,0:T(8,128)(2,1)}), bf16[32,4,96,128]{3,2,1,0:T(8,128)(2,1)}, u32[]{:S(2)}, u32[]{:S(2)}) %all-to-all-start) | async-done | bytes 3145760 | tf_op jit(solution)/shard_map/all_to_all | solution.py:429
  75.5 1.9 collective-permute-done.1
  78.8 3.4 %collective-permute-done.3 = bf16[3,4,48,128]{3,2,1,0:T(8,128)(2,1)S(1)} collective-permute-done((bf16[3,4,48,128]{3,2,1,0:T(8,128)(2,1)S(1)}, bf16[3,4,48,128]{3,2,1,0:T(8,128)(2,1)S(1)}, u32[]{:S(2)}, u32[]{:S(2)}) %collective-permute-start.3) | collective-permute-done | bytes 147488 | tf_op jit(solution)/shard_map/ppermute | solution.py:377
  82.4 2.7 %collective-permute-start.10 = (bf16[3,4,96,128]{3,2,1,0:T(8,128)(2,1)S(1)}, bf16[3,4,96,128]{3,2,1,0:T(8,128)(2,1)S(1)}, u32[]{:S(2)}, u32[]{:S(2)}) collective-permute-start(bf16[3,4,96,128]{3,2,1,0:T(8,128)(2,1)S(1)} %get-tuple-element.32), channel_id=1, source_target_pairs={{0,24},{4,28},{8,0},{12,4},{16,8},{20,12},{24,16},{28,20},{32,56},... | collective-permute-start | bytes 884744 | tf_op jit(solution)/shard_map/ppermute | solution.py:356
  86.2 5.3 %collective-permute-done.9 = bf16[3,4,96,128]{3,2,1,0:T(8,128)(2,1)S(1)} collective-permute-done((bf16[3,4,96,128]{3,2,1,0:T(8,128)(2,1)S(1)}, bf16[3,4,96,128]{3,2,1,0:T(8,128)(2,1)S(1)}, u32[]{:S(2)}, u32[]{:S(2)}) %collective-permute-start.9) | collective-permute-done | bytes 294944 | tf_op jit(solution)/shard_map/ppermute | solution.py:356
  94.9 3.6 %collective-permute-done.11 = bf16[3,4,96,128]{3,2,1,0:T(8,128)(2,1)S(1)} collective-permute-done((bf16[3,4,96,128]{3,2,1,0:T(8,128)(2,1)S(1)}, bf16[3,4,96,128]{3,2,1,0:T(8,128)(2,1)S(1)}, u32[]{:S(2)}, u32[]{:S(2)}) %collective-permute-start.11) | collective-permute-done | bytes 294944 | tf_op jit(solution)/shard_map/ppermute | solution.py:356
  98.8 2.7 %collective-permute-start.14 = (bf16[2,3,8,96,128]{4,3,2,1,0:T(8,128)(2,1)S(1)}, bf16[2,3,8,96,128]{4,3,2,1,0:T(8,128)(2,1)S(1)}, u32[]{:S(2)}, u32[]{:S(2)}) collective-permute-start(bf16[2,3,8,96,128]{4,3,2,1,0:T(8,128)(2,1)S(1)} %pad_maximum_fusion.1.refs_0_), channel_id=1, source_target_pairs={{0,96},{4,100},{8,104},{12,108},{16,112},{20,116},{24,120},{28,124... | collective-permute-start | bytes 3538952 | tf_op jit(solution)/shard_map/ppermute | solution.py:356
  101.7 10.9 %collective-permute-done.7.upper_ref.upper_hbm = bf16[128,48,128]{2,1,0:T(8,128)(2,1)S(1)} collective-permute-done((bf16[128,48,128]{2,1,0:T(8,128)(2,1)S(1)}, bf16[128,48,128]{2,1,0:T(8,128)(2,1)S(1)}, u32[]{:S(2)}, u32[]{:S(2)}) %collective-permute-start.7) | collective-permute-done | bytes 1572896 | tf_op jit(solution)/shard_map/ppermute | solution.py:401
  112.6 2.7 %collective-permute-start.18 = (bf16[2,3,8,96,128]{4,3,2,1,0:T(8,128)(2,1)S(1)}, bf16[2,3,8,96,128]{4,3,2,1,0:T(8,128)(2,1)S(1)}, u32[]{:S(2)}, u32[]{:S(2)}) collective-permute-start(bf16[2,3,8,96,128]{4,3,2,1,0:T(8,128)(2,1)S(1)} %pad_maximum_fusion.refs_1_), channel_id=1, source_target_pairs={{0,24},{4,28},{8,0},{12,4},{16,8},{20,12},{24,16},{28,20},{32,56},... | collective-permute-start | bytes 3538952 | tf_op jit(solution)/shard_map/ppermute | solution.py:356
  115.3 2.6 %collective-permute-start.8 = (bf16[128,48,128]{2,1,0:T(8,128)(2,1)S(1)}, bf16[128,48,128]{2,1,0:T(8,128)(2,1)S(1)}, u32[]{:S(2)}, u32[]{:S(2)}) collective-permute-start(bf16[128,48,128]{2,1,0:T(8,128)(2,1)S(1)} %copy-done.10), channel_id=1, source_target_pairs={{0,2},{2,0},{1,3},{3,1},{4,6},{6,4},{5,7},{7,5},{8,10},{10,8},{9,1... | collective-permute-start | bytes 4718600 | tf_op jit(solution)/shard_map/ppermute | solution.py:401
  117.9 10.4 %collective-permute-done.12.refs_2_ = bf16[2,3,8,96,128]{4,3,2,1,0:T(8,128)(2,1)S(1)} collective-permute-done((bf16[2,3,8,96,128]{4,3,2,1,0:T(8,128)(2,1)S(1)}, bf16[2,3,8,96,128]{4,3,2,1,0:T(8,128)(2,1)S(1)}, u32[]{:S(2)}, u32[]{:S(2)}) %collective-permute-start.12) | collective-permute-done | bytes 1179680 | tf_op jit(solution)/shard_map/ppermute | solution.py:356
  130.2 2.7 %collective-permute-start.15 = (bf16[3,8,96,128]{3,2,1,0:T(8,128)(2,1)}, bf16[3,8,96,128]{3,2,1,0:T(8,128)(2,1)}, u32[]{:S(2)}, u32[]{:S(2)}) collective-permute-start(bf16[3,8,96,128]{3,2,1,0:T(8,128)(2,1)} %slice_bitcast_fusion.2), channel_id=1, source_target_pairs={{0,96},{4,100},{8,104},{12,108},{16,112},{20,116},{24,120},{28,124... | collective-permute-start | bytes 1769480 | tf_op jit(solution)/shard_map/ppermute | solution.py:356
  132.9 6.3 %collective-permute-done.16.refs_3_ = bf16[2,3,8,96,128]{4,3,2,1,0:T(8,128)(2,1)S(1)} collective-permute-done((bf16[2,3,8,96,128]{4,3,2,1,0:T(8,128)(2,1)S(1)}, bf16[2,3,8,96,128]{4,3,2,1,0:T(8,128)(2,1)S(1)}, u32[]{:S(2)}, u32[]{:S(2)}) %collective-permute-start.16) | collective-permute-done | bytes 1179680 | tf_op jit(solution)/shard_map/ppermute | solution.py:356
  143.7 6.3 %collective-permute-done.8.lower_ref.lower_hbm = bf16[128,48,128]{2,1,0:T(8,128)(2,1)S(1)} collective-permute-done((bf16[128,48,128]{2,1,0:T(8,128)(2,1)S(1)}, bf16[128,48,128]{2,1,0:T(8,128)(2,1)S(1)}, u32[]{:S(2)}, u32[]{:S(2)}) %collective-permute-start.8) | collective-permute-done | bytes 1572896 | tf_op jit(solution)/shard_map/ppermute | solution.py:401
  151.1 15.0 %near.1.near_ref = bf16[3,64,48,128]{3,2,1,0:T(8,128)(2,1)} custom-call(s32[96]{0:T(128)} %concatenate.47.slots_ref, bf16[96,192]{1,0:T(8,128)(2,1)} %pad_maximum_fusion.8.v_ref, bf16[128,96,128]{2,1,0:T(8,128)(2,1)} %spectra.1.own_ref.own_hbm, bf16[128,48,128]{2,1,0:T(8,128)(2,1)} %copy-done.2, bf16[128,48,128]{2,1,0:T(8,128)(2,1)} %copy-done.3, ...), custom_call_target="tpu_custom_call" | custom-call | tf_op jit(solution)/shard_map/near/pallas_call | solution.py:285
  168.1 10.0 %far.1 = (bf16[3,32,48,128]{3,2,1,0:T(8,128)(2,1)}, bf16[3,32,48,128]{3,2,1,0:T(8,128)(2,1)}) custom-call(s32[33]{0:T(128)} %pad_add_fusion.slots_ref, bf16[96,64]{1,0:T(8,128)(2,1)} %pad_maximum_fusion.9.v_ref, bf16[128,96,128]{2,1,0:T(8,128)(2,1)} %spectra.1.own_ref.own_hbm, bf16[128,48,128]{2,1,0:T(8,128)(2,1)} %copy-done.2, ...), custom_call_target="tpu_custom_call" | custom-call | tf_op jit(solution)/shard_map/far/pallas_call | solution.py:303
  178.1 3.7 %collective-permute-start.20 = (bf16[3,32,48,128]{3,2,1,0:T(8,128)(2,1)}, bf16[3,32,48,128]{3,2,1,0:T(8,128)(2,1)S(1)}, u32[]{:S(2)}, u32[]{:S(2)}) collective-permute-start(bf16[3,32,48,128]{3,2,1,0:T(8,128)(2,1)} %get-tuple-element.42), channel_id=1, source_target_pairs={{0,1},{1,0},{2,3},{3,2},{4,5},{5,4},{6,7},{7,6},{8,9},{9,8},{10,11... | collective-permute-start | bytes 3538952 | tf_op jit(solution)/shard_map/ppermute | solution.py:397
  181.8 2.7 %collective-permute-done.20.got_ref = bf16[3,32,48,128]{3,2,1,0:T(8,128)(2,1)S(1)} collective-permute-done((bf16[3,32,48,128]{3,2,1,0:T(8,128)(2,1)}, bf16[3,32,48,128]{3,2,1,0:T(8,128)(2,1)S(1)}, u32[]{:S(2)}, u32[]{:S(2)}) %collective-permute-start.20) | collective-permute-done | bytes 1179680 | tf_op jit(solution)/shard_map/ppermute | solution.py:397
  185.6 6.4 %expand.1 = f32[3,3232,128]{2,1,0:T(8,128)} custom-call(bf16[104,144]{1,0:T(8,128)(2,1)} %constant.229.clone.u_ref, bf16[3,32,48,128]{3,2,1,0:T(8,128)(2,1)} %get-tuple-element.41.keep_ref, bf16[3,32,48,128]{3,2,1,0:T(8,128)(2,1)} %copy-done.12), custom_call_target="tpu_custom_call" | custom-call | tf_op jit(solution)/shard_map/expand/pallas_call | solution.py:339
  (110 shorter events, 28.6 us)
Async XLA Ops:
  0.0 30.7 %copy-start = (s32[32]{0:T(128)S(1)}, s32[32]{0:T(128)}, u32[]{:S(2)}) copy-start(s32[32]{0:T(128)} %param.23) | copy-start | bytes 388
  0.9 8.9 %collective-permute-start = (bf16[128,512]{1,0:T(8,128)(2,1)S(1)}, bf16[128,512]{1,0:T(8,128)(2,1)S(1)}, u32[]{:S(2)}, u32[]{:S(2)}) collective-permute-start(bf16[128,512]{1,0:T(8,128)(2,1)S(1)} %slice.76), channel_id=1, source_target_pairs={{1,0},{2,1},{3,2},{5,4},{6,5},{7,6},{9,8},{10,9},{11,10},{13,12},{... | collective-permute-start | bytes 393224 | tf_op jit(solution)/shard_map/ppermute | solution.py:418
  21.5 48.3 %all-to-all-start = ((bf16[32,4,96,128]{3,2,1,0:T(8,128)(2,1)}), bf16[32,4,96,128]{3,2,1,0:T(8,128)(2,1)}, u32[]{:S(2)}, u32[]{:S(2)}) async-start(bf16[32,4,96,128]{3,2,1,0:T(8,128)(2,1)} %bitcast.31), calls=%async_computation | async-start | bytes 6291456 | tf_op jit(solution)/shard_map/all_to_all | solution.py:429
  71.2 6.1 %collective-permute-start.1 = (bf16[3,4,48,128]{3,2,1,0:T(8,128)(2,1)S(1)}, bf16[3,4,48,128]{3,2,1,0:T(8,128)(2,1)S(1)}, u32[]{:S(2)}, u32[]{:S(2)}) collective-permute-start(bf16[3,4,48,128]{3,2,1,0:T(8,128)(2,1)S(1)} %pad_maximum_fusion.7), channel_id=1, source_target_pairs={{0,2},{2,0},{1,3},{3,1},{4,6},{6,4},{5,7},{7,5},{8,10},{10,8},{9,1... | collective-permute-start | bytes 442376 | tf_op jit(solution)/shard_map/ppermute | solution.py:401
  71.3 10.9 %collective-permute-start.3 = (bf16[3,4,48,128]{3,2,1,0:T(8,128)(2,1)S(1)}, bf16[3,4,48,128]{3,2,1,0:T(8,128)(2,1)S(1)}, u32[]{:S(2)}, u32[]{:S(2)}) collective-permute-start(bf16[3,4,48,128]{3,2,1,0:T(8,128)(2,1)S(1)} %pad_maximum_fusion.7), channel_id=1, source_target_pairs={{0,6},{1,7},{2,4},{3,5},{4,2},{5,3},{6,0},{7,1},{8,14},{9,15},{10,... | collective-permute-start | bytes 442376 | tf_op jit(solution)/shard_map/ppermute | solution.py:377
  73.3 5.5 %collective-permute-start.2 = (bf16[3,4,48,128]{3,2,1,0:T(8,128)(2,1)S(1)}, bf16[3,4,48,128]{3,2,1,0:T(8,128)(2,1)S(1)}, u32[]{:S(2)}, u32[]{:S(2)}) collective-permute-start(bf16[3,4,48,128]{3,2,1,0:T(8,128)(2,1)S(1)} %pad_maximum_fusion.6), channel_id=1, source_target_pairs={{0,4},{4,0},{8,12},{12,8},{16,20},{20,16},{24,28},{28,24},{32,36},... | collective-permute-start | bytes 442376 | tf_op jit(solution)/shard_map/ppermute | solution.py:356
  74.2 38.5 %collective-permute-start.7 = (bf16[128,48,128]{2,1,0:T(8,128)(2,1)S(1)}, bf16[128,48,128]{2,1,0:T(8,128)(2,1)S(1)}, u32[]{:S(2)}, u32[]{:S(2)}) collective-permute-start(bf16[128,48,128]{2,1,0:T(8,128)(2,1)S(1)} %copy-done.11), channel_id=1, source_target_pairs={{0,2},{2,0},{1,3},{3,1},{4,6},{6,4},{5,7},{7,5},{8,10},{10,8},{9,1... | collective-permute-start | bytes 4718600 | tf_op jit(solution)/shard_map/ppermute | solution.py:401
  82.3 9.2 %collective-permute-start.9 = (bf16[3,4,96,128]{3,2,1,0:T(8,128)(2,1)S(1)}, bf16[3,4,96,128]{3,2,1,0:T(8,128)(2,1)S(1)}, u32[]{:S(2)}, u32[]{:S(2)}) collective-permute-start(bf16[3,4,96,128]{3,2,1,0:T(8,128)(2,1)S(1)} %get-tuple-element.32), channel_id=1, source_target_pairs={{0,8},{4,12},{8,16},{12,20},{16,24},{20,28},{24,0},{28,4},{32,40},... | collective-permute-start | bytes 884744 | tf_op jit(solution)/shard_map/ppermute | solution.py:356
  82.4 10.8 %collective-permute-start.10 = (bf16[3,4,96,128]{3,2,1,0:T(8,128)(2,1)S(1)}, bf16[3,4,96,128]{3,2,1,0:T(8,128)(2,1)S(1)}, u32[]{:S(2)}, u32[]{:S(2)}) collective-permute-start(bf16[3,4,96,128]{3,2,1,0:T(8,128)(2,1)S(1)} %get-tuple-element.32), channel_id=1, source_target_pairs={{0,24},{4,28},{8,0},{12,4},{16,8},{20,12},{24,16},{28,20},{32,56},... | collective-permute-start | bytes 884744 | tf_op jit(solution)/shard_map/ppermute | solution.py:356
  85.1 13.4 %collective-permute-start.11 = (bf16[3,4,96,128]{3,2,1,0:T(8,128)(2,1)S(1)}, bf16[3,4,96,128]{3,2,1,0:T(8,128)(2,1)S(1)}, u32[]{:S(2)}, u32[]{:S(2)}) collective-permute-start(bf16[3,4,96,128]{3,2,1,0:T(8,128)(2,1)S(1)} %get-tuple-element.32), channel_id=1, source_target_pairs={{0,16},{4,20},{8,24},{12,28},{16,0},{20,4},{24,8},{28,12},{32,48},... | collective-permute-start | bytes 884744 | tf_op jit(solution)/shard_map/ppermute | solution.py:356
  85.7 13.1 %collective-permute-start.4 = (bf16[3,4,96,128]{3,2,1,0:T(8,128)(2,1)S(1)}, bf16[3,4,96,128]{3,2,1,0:T(8,128)(2,1)S(1)}, u32[]{:S(2)}, u32[]{:S(2)}) collective-permute-start(bf16[3,4,96,128]{3,2,1,0:T(8,128)(2,1)S(1)} %get-tuple-element.27), channel_id=1, source_target_pairs={{0,32},{4,36},{8,40},{12,44},{16,48},{20,52},{24,56},{28,60},{32,6... | collective-permute-start | bytes 884744 | tf_op jit(solution)/shard_map/ppermute | solution.py:356
  91.6 9.9 %collective-permute-start.5 = (bf16[3,4,96,128]{3,2,1,0:T(8,128)(2,1)S(1)}, bf16[3,4,96,128]{3,2,1,0:T(8,128)(2,1)S(1)}, u32[]{:S(2)}, u32[]{:S(2)}) collective-permute-start(bf16[3,4,96,128]{3,2,1,0:T(8,128)(2,1)S(1)} %get-tuple-element.27), channel_id=1, source_target_pairs={{0,96},{4,100},{8,104},{12,108},{16,112},{20,116},{24,120},{28,124... | collective-permute-start | bytes 884744 | tf_op jit(solution)/shard_map/ppermute | solution.py:356
  93.2 8.3 %collective-permute-start.6 = (bf16[3,4,96,128]{3,2,1,0:T(8,128)(2,1)S(1)}, bf16[3,4,96,128]{3,2,1,0:T(8,128)(2,1)S(1)}, u32[]{:S(2)}, u32[]{:S(2)}) collective-permute-start(bf16[3,4,96,128]{3,2,1,0:T(8,128)(2,1)S(1)} %get-tuple-element.27), channel_id=1, source_target_pairs={{0,64},{4,68},{8,72},{12,76},{16,80},{20,84},{24,88},{28,92},{32,9... | collective-permute-start | bytes 884744 | tf_op jit(solution)/shard_map/ppermute | solution.py:356
  98.7 29.6 %collective-permute-start.12 = (bf16[2,3,8,96,128]{4,3,2,1,0:T(8,128)(2,1)S(1)}, bf16[2,3,8,96,128]{4,3,2,1,0:T(8,128)(2,1)S(1)}, u32[]{:S(2)}, u32[]{:S(2)}) collective-permute-start(bf16[2,3,8,96,128]{4,3,2,1,0:T(8,128)(2,1)S(1)} %pad_maximum_fusion.1.refs_0_), channel_id=1, source_target_pairs={{0,32},{4,36},{8,40},{12,44},{16,48},{20,52},{24,56},{28,60},{32,6... | collective-permute-start | bytes 3538952 | tf_op jit(solution)/shard_map/ppermute | solution.py:356
  98.8 30.5 %collective-permute-start.14 = (bf16[2,3,8,96,128]{4,3,2,1,0:T(8,128)(2,1)S(1)}, bf16[2,3,8,96,128]{4,3,2,1,0:T(8,128)(2,1)S(1)}, u32[]{:S(2)}, u32[]{:S(2)}) collective-permute-start(bf16[2,3,8,96,128]{4,3,2,1,0:T(8,128)(2,1)S(1)} %pad_maximum_fusion.1.refs_0_), channel_id=1, source_target_pairs={{0,96},{4,100},{8,104},{12,108},{16,112},{20,116},{24,120},{28,124... | collective-permute-start | bytes 3538952 | tf_op jit(solution)/shard_map/ppermute | solution.py:356
  101.7 40.7 %copy-start.5 = (bf16[2,3,8,96,128]{4,3,2,1,0:T(8,128)(2,1)}, bf16[2,3,8,96,128]{4,3,2,1,0:T(8,128)(2,1)S(1)}, u32[]{:S(2)}) copy-start(bf16[2,3,8,96,128]{4,3,2,1,0:T(8,128)(2,1)S(1)} %pad_maximum_fusion.refs_1_) | copy-start | bytes 3538948
  112.6 26.5 %collective-permute-start.16 = (bf16[2,3,8,96,128]{4,3,2,1,0:T(8,128)(2,1)S(1)}, bf16[2,3,8,96,128]{4,3,2,1,0:T(8,128)(2,1)S(1)}, u32[]{:S(2)}, u32[]{:S(2)}) collective-permute-start(bf16[2,3,8,96,128]{4,3,2,1,0:T(8,128)(2,1)S(1)} %pad_maximum_fusion.refs_1_), channel_id=1, source_target_pairs={{0,8},{4,12},{8,16},{12,20},{16,24},{20,28},{24,0},{28,4},{32,40},... | collective-permute-start | bytes 3538952 | tf_op jit(solution)/shard_map/ppermute | solution.py:356
  112.6 28.8 %collective-permute-start.18 = (bf16[2,3,8,96,128]{4,3,2,1,0:T(8,128)(2,1)S(1)}, bf16[2,3,8,96,128]{4,3,2,1,0:T(8,128)(2,1)S(1)}, u32[]{:S(2)}, u32[]{:S(2)}) collective-permute-start(bf16[2,3,8,96,128]{4,3,2,1,0:T(8,128)(2,1)S(1)} %pad_maximum_fusion.refs_1_), channel_id=1, source_target_pairs={{0,24},{4,28},{8,0},{12,4},{16,8},{20,12},{24,16},{28,20},{32,56},... | collective-permute-start | bytes 3538952 | tf_op jit(solution)/shard_map/ppermute | solution.py:356
  115.3 34.7 %collective-permute-start.8 = (bf16[128,48,128]{2,1,0:T(8,128)(2,1)S(1)}, bf16[128,48,128]{2,1,0:T(8,128)(2,1)S(1)}, u32[]{:S(2)}, u32[]{:S(2)}) collective-permute-start(bf16[128,48,128]{2,1,0:T(8,128)(2,1)S(1)} %copy-done.10), channel_id=1, source_target_pairs={{0,2},{2,0},{1,3},{3,1},{4,6},{6,4},{5,7},{7,5},{8,10},{10,8},{9,1... | collective-permute-start | bytes 4718600 | tf_op jit(solution)/shard_map/ppermute | solution.py:401
  129.2 37.0 %collective-permute-start.13 = (bf16[3,8,96,128]{3,2,1,0:T(8,128)(2,1)}, bf16[3,8,96,128]{3,2,1,0:T(8,128)(2,1)S(1)}, u32[]{:S(2)}, u32[]{:S(2)}) collective-permute-start(bf16[3,8,96,128]{3,2,1,0:T(8,128)(2,1)} %slice_bitcast_fusion.3), channel_id=1, source_target_pairs={{0,32},{4,36},{8,40},{12,44},{16,48},{20,52},{24,56},{28,60},{32,6... | collective-permute-start | bytes 1769480 | tf_op jit(solution)/shard_map/ppermute | solution.py:356
  130.2 36.0 %collective-permute-start.15 = (bf16[3,8,96,128]{3,2,1,0:T(8,128)(2,1)}, bf16[3,8,96,128]{3,2,1,0:T(8,128)(2,1)}, u32[]{:S(2)}, u32[]{:S(2)}) collective-permute-start(bf16[3,8,96,128]{3,2,1,0:T(8,128)(2,1)} %slice_bitcast_fusion.2), channel_id=1, source_target_pairs={{0,96},{4,100},{8,104},{12,108},{16,112},{20,116},{24,120},{28,124... | collective-permute-start | bytes 1769480 | tf_op jit(solution)/shard_map/ppermute | solution.py:356
  140.1 26.1 %collective-permute-start.17 = (bf16[3,8,96,128]{3,2,1,0:T(8,128)(2,1)}, bf16[3,8,96,128]{3,2,1,0:T(8,128)(2,1)S(1)}, u32[]{:S(2)}, u32[]{:S(2)}) collective-permute-start(bf16[3,8,96,128]{3,2,1,0:T(8,128)(2,1)} %slice_bitcast_fusion.1), channel_id=1, source_target_pairs={{0,8},{4,12},{8,16},{12,20},{16,24},{20,28},{24,0},{28,4},{32,40},... | collective-permute-start | bytes 1769480 | tf_op jit(solution)/shard_map/ppermute | solution.py:356
  142.4 23.8 %collective-permute-start.19 = (bf16[3,8,96,128]{3,2,1,0:T(8,128)(2,1)}, bf16[3,8,96,128]{3,2,1,0:T(8,128)(2,1)S(1)}, u32[]{:S(2)}, u32[]{:S(2)}) collective-permute-start(bf16[3,8,96,128]{3,2,1,0:T(8,128)(2,1)} %slice_bitcast_fusion), channel_id=1, source_target_pairs={{0,24},{4,28},{8,0},{12,4},{16,8},{20,12},{24,16},{28,20},{32,56},... | collective-permute-start | bytes 1769480 | tf_op jit(solution)/shard_map/ppermute | solution.py:356
  178.1 6.4 %collective-permute-start.20 = (bf16[3,32,48,128]{3,2,1,0:T(8,128)(2,1)}, bf16[3,32,48,128]{3,2,1,0:T(8,128)(2,1)S(1)}, u32[]{:S(2)}, u32[]{:S(2)}) collective-permute-start(bf16[3,32,48,128]{3,2,1,0:T(8,128)(2,1)} %get-tuple-element.42), channel_id=1, source_target_pairs={{0,1},{1,0},{2,3},{3,2},{4,5},{5,4},{6,7},{7,6},{8,9},{9,8},{10,11... | collective-permute-start | bytes 3538952 | tf_op jit(solution)/shard_map/ppermute | solution.py:397
  (21 other events, 182.0 us)
